TPU v7x, 32 devices: a whole 2x2x4 slice. The times are simulated.
32 devices in a mesh: ctx: 8 (over y, x, core), hx: 4 (over z).
Axes of the slice: x: 2, y: 2, z: 4, core: 2. Of those that a mesh axis runs over, the one named last changes fastest.
Arguments:
- tokens: bfloat16 [4096, 5120], P('ctx'), may hold values from -6 to 6
- attn_gain: bfloat16 [5120], replicated, may hold values from 0.5 to 1.5
- ffn_gain: bfloat16 [5120], replicated, may hold values from 0.5 to 1.5
- w_query: bfloat16 [5120, 3072], P('ctx', 'hx'), may hold values from -3 to 3
- w_key: bfloat16 [5120, 1024], P('ctx', 'hx'), may hold values from -1 to 1
- w_value: bfloat16 [5120, 1024], P('ctx', 'hx'), may hold values from -0.078125 to 0.078125
- w_out: bfloat16 [3072, 5120], P('hx'), may hold values from -0.109375 to 0.109375
- w_router: bfloat16 [5120, 8], replicated, may hold values from -0.078125 to 0.078125
- routes: int32 [4096, 1], P('ctx'), may hold values from 0 to 7; in each aligned block of 512 rows (0 to 511, 512 to 1023, ...) at most 64 rows name the same one
- w_gate: bfloat16 [8, 5120, 4096], P('ctx', None, 'hx'), may hold values from -0.078125 to 0.078125
- w_up: bfloat16 [8, 5120, 4096], P('ctx', None, 'hx'), may hold values from -0.078125 to 0.078125
- w_down: bfloat16 [8, 4096, 5120], P('ctx', 'hx'), may hold values from -0.09375 to 0.09375
Outputs:
- layer_out: bfloat16 [4096, 5120], P('ctx', 'hx')
Inputs may be any that keep to these rules, and one draw needn't show every extreme that they name: `routes`: within the 512 rows of one device, no expert is named by more than 64 rows, a bound that some block reaches.
All inputs are finite; a program needn't handle non-finite values.
Results may differ from a plain program's by a relative error of at most 0.0095.
Values may be sent and summed in bfloat16 or wider, within the bound.
No kernel may reach another device: no remote copies, remote signals or barrier semaphores. Data moves between devices by JAX's collectives and lax.ppermute only.
A program may use at most 128 MiB of HBM per device.

v0:
```python
import jax
import jax.numpy as jnp
from jax import lax
from jax.sharding import PartitionSpec as P

HD = 128


epsilon = 1e-05
block_rows = 1024


def root_norm(values, gains):
    floats = values.astype(jnp.float32)
    inverse = lax.rsqrt(jnp.mean(floats * floats, axis=-1, keepdims=True) + epsilon)
    return (floats * inverse * gains.astype(jnp.float32)).astype(jnp.bfloat16)


def body(
    tokens,
    attn_gain,
    ffn_gain,
    w_query,
    w_key,
    w_value,
    w_out,
    w_router,
    routes,
    w_gate,
    w_up,
    w_down,
):
    ctx_count = lax.axis_size("ctx")
    hx_count = lax.axis_size("hx")
    hx_index = lax.axis_index("hx")
    tok_rows = tokens.shape[0]
    full_width = tokens.shape[1]
    local_width = full_width // hx_count
    normed = root_norm(tokens, attn_gain)
    pieces = (
        lax.all_gather(w_query, "ctx", axis=0, tiled=True),
        lax.all_gather(w_key, "ctx", axis=0, tiled=True),
        lax.all_gather(w_value, "ctx", axis=0, tiled=True),
    )
    queries, key_proj, value_proj = tuple(
        (jnp.dot(normed, matrix, preferred_element_type=jnp.float32) for matrix in pieces)
    )
    kv_heads = key_proj.shape[1] // HD
    group_size = queries.shape[1] // HD // kv_heads
    queries_all = queries.astype(jnp.bfloat16).reshape(tok_rows, kv_heads, group_size, HD)
    key_local = key_proj.astype(jnp.bfloat16)
    value_local = value_proj.astype(jnp.bfloat16)
    query_first = lax.axis_index("ctx") * tok_rows
    query_last = query_first + tok_rows - 1
    query_pos = query_first + jnp.arange(tok_rows, dtype=jnp.int32)

    def attend(running, key_block, value_block, key_start):
        running_max, running_sum, running_out = running
        count_here = key_block.shape[0]
        key_heads = key_block.reshape(count_here, kv_heads, HD)
        value_heads = value_block.reshape(count_here, kv_heads, HD)
        scores = jnp.einsum(
            "tkgd,skd->tkgs", queries_all, key_heads, preferred_element_type=jnp.float32
        ) * HD ** (-0.5)
        key_pos = key_start + jnp.arange(count_here, dtype=jnp.int32)
        visible = (key_pos[None, :] <= query_pos[:, None])[:, None, None, :]
        masked = jnp.where(visible, scores, -jnp.inf)
        new_max = jnp.maximum(running_max, jnp.max(masked, axis=-1))
        weights = jnp.where(visible, jnp.exp(scores - new_max[..., None]), 0.0)
        factor = jnp.exp(running_max - new_max)
        new_sum = running_sum * factor + jnp.sum(weights, axis=-1)
        contrib = jnp.einsum(
            "tkgs,skd->tkgd",
            weights.astype(jnp.bfloat16),
            value_heads,
            preferred_element_type=jnp.float32,
        )
        return (new_max, new_sum, running_out * factor[..., None] + contrib)

    def visit(running, key_block, value_block, key_start):
        return lax.cond(
            key_start <= query_last,
            lambda held: attend(held, key_block, value_block, key_start),
            lambda held: held,
            running,
        )

    start_max = jnp.full((tok_rows, kv_heads, group_size), -1e30, jnp.float32)
    start_sum = jnp.zeros((tok_rows, kv_heads, group_size), jnp.float32)
    start_out = jnp.zeros((tok_rows, kv_heads, group_size, HD), jnp.float32)
    key_rows = lax.all_gather(key_local, "ctx", axis=0, tiled=True)
    value_rows = lax.all_gather(value_local, "ctx", axis=0, tiled=True)
    count_all = key_rows.shape[0]

    def block_step(block_index, held):
        inner = block_index * block_rows
        key_block = lax.dynamic_slice_in_dim(key_rows, inner, block_rows, 0)
        value_block = lax.dynamic_slice_in_dim(value_rows, inner, block_rows, 0)
        return visit(held, key_block, value_block, inner)

    final_max, final_sum, final_out = lax.fori_loop(
        0, count_all // block_rows, block_step, (start_max, start_sum, start_out)
    )
    attended = (final_out / final_sum[..., None]).astype(jnp.bfloat16).reshape(tok_rows, -1)
    partial_attn = jnp.dot(attended, w_out, preferred_element_type=jnp.float32)
    attn_sum = lax.psum(partial_attn.astype(jnp.bfloat16), "hx").astype(jnp.float32)
    stream = (tokens.astype(jnp.float32) + attn_sum).astype(jnp.bfloat16)
    own_stream = lax.dynamic_slice_in_dim(stream, hx_index * local_width, local_width, 1)
    normed2 = root_norm(stream, ffn_gain)
    logits = jnp.dot(normed2, w_router, preferred_element_type=jnp.float32)
    expert_count = w_router.shape[1]
    chosen = routes[:, 0]
    onehot = chosen[:, None] == jnp.arange(expert_count, dtype=jnp.int32)[None, :]
    router_score = jax.nn.sigmoid(jnp.sum(jnp.where(onehot, logits, 0.0), axis=-1))
    routed = (normed2.astype(jnp.float32) * router_score[:, None]).astype(jnp.bfloat16)
    counts = jnp.cumsum(onehot.astype(jnp.int32), axis=0)
    position = jnp.sum(jnp.where(onehot, counts, 0), axis=-1) - 1
    capacity = tok_rows // 8
    slot_index = chosen * capacity + position
    exp_local = w_gate.shape[0]
    buffer = (
        jnp.zeros((expert_count * capacity, full_width), jnp.bfloat16).at[slot_index].set(routed)
    )
    buffer = buffer.reshape(ctx_count, exp_local, capacity, full_width)
    expert_rows = lax.all_to_all(buffer, "ctx", split_axis=0, concat_axis=0, tiled=True)
    gate_out = jnp.einsum("secd,edf->secf", expert_rows, w_gate, preferred_element_type=jnp.float32)
    up_out = jnp.einsum("secd,edf->secf", expert_rows, w_up, preferred_element_type=jnp.float32)
    hidden = (jax.nn.silu(gate_out) * up_out).astype(jnp.bfloat16)
    partial_expert = jnp.einsum(
        "secf,efd->secd", hidden, w_down, preferred_element_type=jnp.float32
    )
    reduced = lax.psum_scatter(
        partial_expert.astype(jnp.bfloat16), "hx", scatter_dimension=3, tiled=True
    )
    returned = lax.all_to_all(reduced, "ctx", split_axis=0, concat_axis=0, tiled=True)
    flat_rows = returned.reshape(expert_count * capacity, local_width)
    expert_out = flat_rows[slot_index]
    return (own_stream.astype(jnp.float32) + expert_out.astype(jnp.float32)).astype(jnp.bfloat16)


def solution(mesh):
    return jax.shard_map(
        body,
        mesh=mesh,
        in_specs=(
            P("ctx", None),
            P(),
            P(),
            P("ctx", "hx"),
            P("ctx", "hx"),
            P("ctx", "hx"),
            P("hx", None),
            P(),
            P("ctx", None),
            P("ctx", None, "hx"),
            P("ctx", None, "hx"),
            P("ctx", "hx", None),
        ),
        out_specs=P("ctx", "hx"),
        check_vma=False,
    )
```

profile of v0, /device:TPU:16, one launch (start us, length us, event | category | flops | bytes accessed | tf_op | source)
XLA Modules:
  0.0 700.6 jit_solution(15272873829122865083)
XLA Ops:
  6.5 0.7 all-gather.6.cloned.1.call-update
  7.3 0.7 all-gather.12.cloned.1.call-update
  8.1 0.7 convert_element_type.89
  8.8 3.6 fusion.17
  12.4 28.1 %all-gather.6.cloned.1.call-done = bf16[5120,256]{1,0:T(8,128)(2,1)} async-done(((bf16[640,256]{1,0:T(8,128)(2,1)}), bf16[5120,256]{1,0:T(8,128)(2,1)}) %all-gather.6.cloned.1.call-update) | async-done | bytes 2621456 | tf_op jit(solution)/shard_map/all_gather | solution.py:42
  40.5 5.6 convolution_convert_fusion.3
  46.1 26.4 %all-gather.12.cloned.1.call-done = bf16[5120,256]{1,0:T(8,128)(2,1)} async-done(((bf16[640,256]{1,0:T(8,128)(2,1)}), bf16[5120,256]{1,0:T(8,128)(2,1)}) %all-gather.12.cloned.1.call-update) | async-done | bytes 2621456 | tf_op jit(solution)/shard_map/all_gather | solution.py:43
  72.5 5.6 convolution_convert_fusion.2
  78.2 0.5 all-gather.10.cloned.1.call-update
  78.7 0.6 all-reduce.2.cloned.1.call-start
  79.3 23.0 %all-gather.8.cloned.1.call-done = bf16[4096,256]{1,0:T(8,128)(2,1)} async-done(((bf16[512,256]{1,0:T(8,128)(2,1)}), bf16[4096,256]{1,0:T(8,128)(2,1)}) %all-gather.8.cloned.1.call-update) | async-done | bytes 2097168 | tf_op jit(solution)/shard_map/all_gather | solution.py:91
  102.3 4.1 copy.27
  106.5 25.5 %all-gather.14.cloned.1.call-done = bf16[4096,256]{1,0:T(8,128)(2,1)} async-done(((bf16[512,256]{1,0:T(8,128)(2,1)}), bf16[4096,256]{1,0:T(8,128)(2,1)}) %all-gather.14.cloned.1.call-update) | async-done | bytes 2097168 | tf_op jit(solution)/shard_map/all_gather | solution.py:92
  132.0 4.1 copy.29
  136.1 49.9 %all-gather.10.cloned.1.call-done = bf16[5120,768]{1,0:T(8,128)(2,1)} async-done(((bf16[640,768]{1,0:T(8,128)(2,1)}), bf16[5120,768]{1,0:T(8,128)(2,1)}) %all-gather.10.cloned.1.call-update) | async-done | bytes 7864336 | tf_op jit(solution)/shard_map/all_gather | solution.py:41
  185.9 9.1 %convolution_convert_fusion.1 = bf16[512,768]{1,0:T(8,128)(2,1)S(1)} fusion(bf16[5120,768]{1,0:T(8,128)(2,1)} %all-gather.10.cloned.1.call-done, bf16[512,5120]{1,0:T(8,128)(2,1)} %param.16, f32[5120]{0:T(1024)S(1)} %convert_element_type.89, f32[512]{0:T(512)S(1)} %add_rsqrt_fusion.1), kind=kOutput, calls=%fused_computation.58 | convolution fusion | flops 4037410816 | bytes 13916160 | tf_op jit(solution)/shard_map/dot_general | solution.py:46
  195.0 0.3 copy.26
  195.3 0.4 copy.28
  195.7 0.1 broadcast_in_dim.64
  195.9 16.2 %while.18 = (s32[]{:T(128)}, f32[512,2,3]{0,2,1:T(4,128)S(1)}, f32[512,2,3]{0,2,1:T(4,128)S(1)}, f32[512,2,3,128]{3,0,2,1:T(8,128)S(1)}, s32[]{:T(128)}, /*index...) while((s32[]{:T(128)}, f32[512,2,3]{0,2,1:T(4,128)S(1)}, ...), condition=%wide.region_6.7_spmd.clone, body=%wide.region_1.6_spmd.clone.sunk | while | flops 1646534144 | bytes 97468752 | solution.py:101
  195.9 16.0 %conditional.3 = ((f32[512,2,3]{0,2,1:T(4,128)S(1)}, f32[512,2,3]{0,2,1:T(4,128)S(1)}, f32[512,2,3,128]{3,0,2,1:T(8,128)S(1)})) conditional(s32[]{:T(128)} %convert_element_type.169, (f32[512,2,3]{0,2,1:T(4,128)S(1)}, f32[512,2,3]{0,2,1:T(4,128)S(1)}, f32[512,2,3,128]{3,0,2,1:T(8,128)S(1)}) %tuple.58, (s32[]{:T(128)}, s32[]{:T(128)}, ...), branch_computations={%region_2.0_spmd, %region_3.5_spmd} | conditional | flops 1646534144 | bytes 97466472 | solution.py:81
  195.9 1.3 constant_dynamic-slice_fusion
  197.2 0.4 broadcast_compare_fusion
  197.6 2.9 fusion.2
  200.6 2.6 fusion.6
  203.2 1.9 copy-done.1
  205.1 6.8 bitcast_add_fusion
  212.1 0.5 copy.30
  212.6 0.2 divide_convert_fusion
  212.8 9.5 %convolution_convert_fusion = bf16[512,5120]{1,0:T(8,128)(2,1)} fusion(bf16[512,768]{0,1:T(8,128)(2,1)S(1)} %bitcast.126, bf16[768,5120]{1,0:T(8,128)(2,1)} %param.22), kind=kOutput, calls=%fused_computation.42 | convolution fusion | flops 4029153280 | bytes 13893632 | tf_op jit(solution)/shard_map/dot_general | solution.py:105
  222.3 0.6 copy-done.4
  223.0 1.1 reduce-window.6
  224.1 0.2 slice_reduce_fusion
  224.5 233.8 %all-reduce.2.cloned.1.call-done = bf16[512,5120]{1,0:T(8,128)(2,1)} async-done(((bf16[512,5120]{1,0:T(8,128)(2,1)}), bf16[512,5120]{1,0:T(8,128)(2,1)}) %all-reduce.2.cloned.1.call-update) | async-done | bytes 5242896 | tf_op jit(solution)/shard_map/psum | solution.py:106
  458.3 6.5 fusion.14
  464.8 2.3 copy-done.2
  467.1 4.3 fusion.16
  471.4 4.0 fusion.51
  475.3 12.7 %scatter_custom_fusion = bf16[512,5120]{1,0:T(8,128)(2,1)} fusion(s32[512]{0:T(512)S(1)} %bitcast.130, bf16[512,5120]{1,0:T(8,128)(2,1)} %fusion.16, f32[512]{0:T(512)S(1)} %add_divide_fusion, bf16[]{:T(256)} %constant.99.clone.1), kind=kCustom, calls=%fused_computation.44 | custom fusion | flops 7864320 | bytes 10487810 | tf_op jit(solution)/shard_map/scatter | solution.py:122
  488.0 64.5 %all_to_all.10 = bf16[8,1,64,5120]{3,2,1,0:T(8,128)(2,1)S(1)} all-to-all(bf16[8,1,64,5120]{3,2,1,0:T(8,128)(2,1)} %bitcast.122), channel_id=1, replica_groups=mesh['ctx'=8,'hx'=4] {'ctx'}, dimensions={0} | all-to-all | bytes 10485760 | tf_op jit(solution)/shard_map/all_to_all | solution.py:125
  552.5 8.4 %fusion.25 = f32[8,64,1024]{2,1,0:T(8,128)S(1)} fusion(bf16[1,5120,1024]{2,1,0:T(8,128)(2,1)} %param.25, bf16[8,1,64,5120]{3,2,1,0:T(8,128)(2,1)S(1)} %all_to_all.10), kind=kOutput, calls=%fused_computation.38 | convolution fusion | flops 5368709120 | bytes 17825792 | tf_op jit(solution)/shard_map/secd,edf->secf/dot_general | solution.py:126
  561.0 5.8 fusion.46
  566.8 7.4 %fusion.30 = bf16[8,1,64,5120]{3,2,0,1:T(8,128)(2,1)} fusion(bf16[8,64,1024]{2,1,0:T(8,128)(2,1)S(1)} %fusion.46, bf16[1,1024,5120]{2,1,0:T(8,128)(2,1)S(1)} %bitcast.136), kind=kOutput, calls=%fused_computation.43 | convolution fusion | flops 5371330560 | bytes 16777216 | tf_op jit(solution)/shard_map/secf,efd->secd/dot_general | solution.py:129
  574.2 92.6 %reduce-scatter.2.cloned.1.call-done = bf16[8,1,64,1280]{3,2,0,1:T(8,128)(2,1)} async-done(((bf16[8,1,64,5120]{3,2,0,1:T(8,128)(2,1)}), bf16[8,1,64,1280]{3,2,0,1:T(8,128)(2,1)}) %reduce-scatter.2.cloned.1.call-update) | async-done | bytes 1310736 | tf_op jit(solution)/shard_map/reduce_scatter | solution.py:132
  666.8 3.7 all-to-all-start.1
  670.5 18.2 %all-to-all-done.1 = bf16[8,1,64,1280]{3,2,1,0:T(8,128)(2,1)S(1)} async-done(((bf16[8,1,64,1280]{3,2,1,0:T(8,128)(2,1)}), bf16[8,1,64,1280]{3,2,1,0:T(8,128)(2,1)S(1)}, u32[]{:S(2)}, u32[]{:S(2)}) %all-to-all-start.1) | async-done | bytes 1310752 | tf_op jit(solution)/shard_map/all_to_all | solution.py:135
  688.7 2.1 gather_fusion
  690.8 2.7 add_convert_fusion
  (56 shorter events, 0.6 us)
Async XLA Ops:
  6.5 464.8 %copy-start = (bf16[5120,8]{0,1:T(8,128)(2,1)S(1)}, bf16[5120,8]{0,1:T(8,128)(2,1)}, u32[]{:S(2)}) copy-start(bf16[5120,8]{0,1:T(8,128)(2,1)} %param.23) | copy-start | bytes 245764
  6.5 33.9 %all-gather.6.cloned.1.call-start = ((), (), s32[]{:S(2)}) async-start(), calls=%async_computation.3 | async-start | bytes 2949120 | tf_op jit(solution)/shard_map/all_gather | solution.py:42
  7.3 65.2 %all-gather.12.cloned.1.call-start = ((), (), s32[]{:S(2)}) async-start(), calls=%async_computation.6 | async-start | bytes 2949120 | tf_op jit(solution)/shard_map/all_gather | solution.py:43
  8.0 94.3 %all-gather.8.cloned.1.call-start = ((), (), s32[]{:S(2)}) async-start(), calls=%async_computation.4 | async-start | bytes 2359296 | tf_op jit(solution)/shard_map/all_gather | solution.py:91
  46.1 85.9 %all-gather.14.cloned.1.call-start = ((), (), s32[]{:S(2)}) async-start(), calls=%async_computation.7 | async-start | bytes 2359296 | tf_op jit(solution)/shard_map/all_gather | solution.py:92
  78.1 107.8 %all-gather.10.cloned.1.call-start = ((), (), s32[]{:S(2)}) async-start(), calls=%async_computation.5 | async-start | bytes 8847360 | tf_op jit(solution)/shard_map/all_gather | solution.py:41
  78.7 379.6 %all-reduce.2.cloned.1.call-start = ((), (), s32[]{:S(2)}) async-start(), calls=%async_computation.8 | async-start | bytes 10485760 | tf_op jit(solution)/shard_map/psum | solution.py:106
  200.6 4.5 copy-start.1
  222.3 0.7 copy-start.4
  222.3 0.7 copy-start.3
  222.3 444.5 %reduce-scatter.2.cloned.1.call-start = ((), (), s32[]{:S(2)}) async-start(), calls=%async_computation.9 | async-start | bytes 6553600 | tf_op jit(solution)/shard_map/reduce_scatter | solution.py:132
  464.8 2.3 copy-start.2
  488.0 72.9 %slice-start = ((s8[10485760]{0:T(1024)(128)(4,1)}), s8[4194304]{0:T(1024)(128)(4,1)S(1)}, s32[]{:S(2)}) async-start(s8[10485760]{0:T(1024)(128)(4,1)} %bitcast.133), calls=%async_computation.10 | async-start | bytes 8388608
  552.5 8.4 %slice-start.1 = ((s8[10485760]{0:T(1024)(128)(4,1)}), s8[4194304]{0:T(1024)(128)(4,1)S(1)}, s32[]{:S(2)}) async-start(s8[10485760]{0:T(1024)(128)(4,1)} %bitcast.133), calls=%async_computation.11 | async-start | bytes 8388608
  552.5 8.4 %slice-start.2 = ((s8[10485760]{0:T(1024)(128)(4,1)}), s8[2097152]{0:T(1024)(128)(4,1)S(1)}, s32[]{:S(2)}) async-start(s8[10485760]{0:T(1024)(128)(4,1)} %bitcast.133), calls=%async_computation.12 | async-start | bytes 4194304
  552.5 14.3 %slice-start.3 = ((s8[10485760]{0:T(1024)(128)(4,1)}), s8[4194304]{0:T(1024)(128)(4,1)S(1)}, s32[]{:S(2)}) async-start(s8[10485760]{0:T(1024)(128)(4,1)} %bitcast.135), calls=%async_computation.13 | async-start | bytes 8388608
  552.5 14.3 %slice-start.4 = ((s8[10485760]{0:T(1024)(128)(4,1)}), s8[4194304]{0:T(1024)(128)(4,1)S(1)}, s32[]{:S(2)}) async-start(s8[10485760]{0:T(1024)(128)(4,1)} %bitcast.135), calls=%async_computation.14 | async-start | bytes 8388608
  560.9 5.9 slice-start.5
  666.8 21.9 %all-to-all-start.1 = ((bf16[8,1,64,1280]{3,2,1,0:T(8,128)(2,1)}), bf16[8,1,64,1280]{3,2,1,0:T(8,128)(2,1)S(1)}, u32[]{:S(2)}, u32[]{:S(2)}) async-start(bf16[8,1,64,1280]{3,2,1,0:T(8,128)(2,1)} %bitcast.125), calls=%async_computation.2 | async-start | bytes 2621440 | tf_op jit(solution)/shard_map/all_to_all | solution.py:135
Sparse Core Ops, SparseCore 0:
  9.2 31.1 all-gather.5
  42.3 30.1 all-gather.11
  74.4 27.8 all-gather.7
  104.1 27.8 all-gather.13
  133.7 52.1 all-gather.9
  222.4 235.8 all-reduce.1
  574.3 92.4 reduce-scatter.1
where the time goes:
time: 706 us; the launch traced here: 701 us
  waiting for transfers between devices  499 us (71%)
  matrix products  65 us (9%)
  blocking collectives  64.5 us (9%)
  other arithmetic  35 us (5%)
  local copies, waits for them, and re-layouts  18 us (3%)
  between operations  14 us (2%)
    psum x1, waiting for transfers between devices, body(): lax.psum(partial_attn.astype(jnp.bfloat16), 'hx').astype(jnp.float32)  234 us
    reduce_scatter x1, waiting for transfers between devices, body(): lax.psum_scatter(partial_expert.astype(jnp.bfloat16), 'hx', scatter_dimen...  92.6 us
    all_to_all x1, blocking collectives, body(): lax.all_to_all(buffer, 'ctx', split_axis=0, concat_axis=0, tiled=True)  64.5 us
    all_gather x1, waiting for transfers between devices, body(): lax.all_gather(w_query, 'ctx', axis=0, tiled=True)  49.9 us
    all_gather x1, waiting for transfers between devices, body(): lax.all_gather(w_key, 'ctx', axis=0, tiled=True)  28.1 us
    all_gather x1, waiting for transfers between devices, body(): lax.all_gather(w_value, 'ctx', axis=0, tiled=True)  26.4 us
    all_gather x1, waiting for transfers between devices, body(): value_rows = lax.all_gather(value_local, 'ctx', axis=0, tiled=True)  25.5 us
    all_gather x1, waiting for transfers between devices, body(): key_rows = lax.all_gather(key_local, 'ctx', axis=0, tiled=True)  23 us
  transfers between devices with their start and end apart: 8, of which 8 were waited for; matrix products, arithmetic and copies ran while one was open for 4% of the time, Pallas kernels for 0%

commit v1 on v0

v1 whole, which is shorter than its diff:
```python
import functools

import jax
import jax.numpy as jnp
from jax import lax
from jax.experimental import pallas as pl
from jax.experimental.pallas import tpu as pltpu
from jax.sharding import PartitionSpec as P

HD = 128
epsilon = 1e-05
LOG2E = 1.4426950408889634
CHUNKS = 2
F32 = jnp.float32
BF16 = jnp.bfloat16


def dot32(left, right):
    return jnp.dot(left, right, preferred_element_type=F32)


def root_norm(values, gains):
    floats = values.astype(F32)
    inverse = lax.rsqrt(jnp.mean(floats * floats, axis=-1, keepdims=True) + epsilon)
    return (floats * inverse * gains.astype(F32)).astype(BF16)


def swap(value, axis, offset):
    count = lax.axis_size(axis)
    return lax.ppermute(value, axis, [(i, i ^ offset) for i in range(count)])


def xor_gather(block):
    count = lax.axis_size("ctx")
    half = block.shape[0] // 2
    held = {0: block}
    for offset in sorted(range(2, count, 2), key=lambda o: (o.bit_count(), o)):
        low = offset & -offset
        high = 1 << (offset.bit_length() - 1)
        if low == high:
            held[offset] = swap(block, "ctx", offset)
        else:
            top = swap(held[offset ^ low][:half], "ctx", low)
            bottom = swap(held[offset ^ high][half:], "ctx", high)
            held[offset] = jnp.concatenate([top, bottom], axis=0)
    if count > 1:
        for offset in range(0, count, 2):
            held[offset ^ 1] = swap(held[offset], "ctx", 1)
    return held


def line_gather(block):
    count = lax.axis_size("hx")
    own = lax.axis_index("hx")
    right = left = block
    rights, lefts = [], []
    for step in range(1, count):
        right = lax.ppermute(right, "hx", [(i, i + 1) for i in range(step - 1, count - 1)])
        left = lax.ppermute(left, "hx", [(i + 1, i) for i in range(0, count - step)])
        rights.append(right)
        lefts.append(left)
    return [block] + [
        jnp.where(own >= k, rights[k - 1], lefts[count - k - 1]) for k in range(1, count)
    ]


def line_scatter(values):
    count = lax.axis_size("hx")
    own = lax.axis_index("hx")
    width = values.shape[1] // count

    def share(index):
        index = jnp.clip(index, 0, count - 1)
        return lax.dynamic_slice_in_dim(values, index * width, width, 1)

    right = left = None
    for step in range(1, count):
        to_right = share(count - step + own)
        to_left = share(own + step - count)
        if right is not None:
            to_right = (to_right.astype(F32) + right.astype(F32)).astype(BF16)
            to_left = (to_left.astype(F32) + left.astype(F32)).astype(BF16)
        right = lax.ppermute(to_right, "hx", [(i, i + 1) for i in range(step)])
        left = lax.ppermute(to_left, "hx", [(i, i - 1) for i in range(count - step, count)])
    total = share(own).astype(F32)
    if right is not None:
        total = total + right.astype(F32) + left.astype(F32)
    return total.astype(BF16)


def attend_kernel(index_ref, query_ref, key_ref, value_ref, out_ref, *, group_size):
    rows = query_ref.shape[0]
    own = index_ref[0]
    scale = HD ** (-0.5) * LOG2E
    queries = [query_ref[:, g * HD : (g + 1) * HD] for g in range(group_size)]

    def block(start, states, masked):
        keys = key_ref[pl.ds(start, rows), :]
        values = value_ref[pl.ds(start, rows), :]
        states_out = []
        for query, (top, total, acc) in zip(queries, states):
            scores = lax.dot_general(
                keys, query, (((1,), (1,)), ((), ())), preferred_element_type=F32
            )
            if masked:
                key_at = lax.broadcasted_iota(jnp.int32, scores.shape, 0)
                query_at = lax.broadcasted_iota(jnp.int32, scores.shape, 1)
                scores = jnp.where(key_at <= query_at, scores, -1e30)
            new_top = jnp.maximum(top, jnp.max(scores, axis=0, keepdims=True))
            weights = jnp.exp2((scores - new_top) * scale)
            factor = jnp.exp2((top - new_top) * scale)
            total = total * factor + jnp.sum(weights, axis=0, keepdims=True)
            mixed = lax.dot_general(
                values,
                weights.astype(BF16),
                (((0,), (0,)), ((), ())),
                preferred_element_type=F32,
            )
            states_out.append((new_top, total, acc * factor + mixed))
        return tuple(states_out)

    start_state = tuple(
        (
            jnp.full((1, rows), -1e30, F32),
            jnp.zeros((1, rows), F32),
            jnp.zeros((HD, rows), F32),
        )
        for _ in range(group_size)
    )
    states = block(pl.multiple_of(own * rows, rows), start_state, True)
    states = lax.fori_loop(
        0, own, lambda j, held: block(pl.multiple_of(j * rows, rows), held, False), states
    )
    for g, (_, total, acc) in enumerate(states):
        out_ref[:, g * HD : (g + 1) * HD] = (acc / total).T.astype(BF16)


def attend(own, queries, keys, values):
    rows, width = queries.shape
    group_size = width // HD
    return pl.pallas_call(
        functools.partial(attend_kernel, group_size=group_size),
        out_shape=jax.ShapeDtypeStruct((rows, width), BF16),
        grid_spec=pltpu.PrefetchScalarGridSpec(
            num_scalar_prefetch=1,
            grid=(1,),
            in_specs=[
                pl.BlockSpec(queries.shape, lambda g, s: (0, 0)),
                pl.BlockSpec(keys.shape, lambda g, s: (0, 0)),
                pl.BlockSpec(values.shape, lambda g, s: (0, 0)),
            ],
            out_specs=pl.BlockSpec((rows, width), lambda g, s: (0, 0)),
        ),
        compiler_params=pltpu.CompilerParams(vmem_limit_bytes=48 * 1024 * 1024),
        cost_estimate=pl.CostEstimate(
            flops=4 * rows * keys.shape[0] * width,
            bytes_accessed=4 * keys.size,
            transcendentals=rows * keys.shape[0] * group_size,
        ),
        name="attend",
    )(own, queries, keys, values)


def body(
    tokens,
    attn_gain,
    ffn_gain,
    w_query,
    w_key,
    w_value,
    w_out,
    w_router,
    routes,
    w_gate,
    w_up,
    w_down,
):
    ctx_count = lax.axis_size("ctx")
    hx_count = lax.axis_size("hx")
    ctx_index = lax.axis_index("ctx")
    hx_index = lax.axis_index("hx")
    parity = ctx_index % 2
    tok_rows, full_width = tokens.shape
    width = full_width // hx_count
    own_rows = w_query.shape[0]
    kv_heads = w_key.shape[1] // HD
    group_width = w_query.shape[1] // kv_heads
    expert_count = w_router.shape[1]

    half = width // 2
    out_mats = []
    for k in range(hx_count):
        dest = (hx_index + k) % hx_count
        mine = lax.dynamic_slice_in_dim(w_out, dest * width + parity * half, half, 1)
        if k > 0:
            mine = lax.ppermute(
                mine, "hx", [(i, (i + k) % hx_count) for i in range(hx_count)]
            )
            other = swap(mine, "ctx", 1)
        else:
            other = lax.dynamic_slice_in_dim(w_out, dest * width + (1 - parity) * half, half, 1)
        out_mats.append((mine, other))

    normed = root_norm(tokens, attn_gain)
    offsets = range(ctx_count)
    normed_at = [
        lax.dynamic_slice_in_dim(normed, (ctx_index ^ o) * own_rows, own_rows, 1) for o in offsets
    ]

    def project(blocks):
        total = dot32(normed_at[0], blocks[0])
        for o in offsets[1:]:
            total = total + dot32(normed_at[o], blocks[o])
        return total.astype(BF16)

    kv_own = project(xor_gather(jnp.concatenate([w_key, w_value], axis=1)))
    kv_blocks = xor_gather(kv_own)
    kv_all = jnp.zeros((ctx_count * tok_rows, kv_own.shape[1]), BF16)
    for o in offsets:
        kv_all = lax.dynamic_update_slice_in_dim(
            kv_all, kv_blocks[o], (ctx_index ^ o) * tok_rows, 0
        )

    attended = []
    for g in range(kv_heads):
        queries = project(xor_gather(w_query[:, g * group_width : (g + 1) * group_width]))
        mixed = attend(
            ctx_index.reshape(1),
            queries,
            kv_all[:, g * HD : (g + 1) * HD],
            kv_all[:, (kv_heads + g) * HD : (kv_heads + g + 1) * HD],
        )
        attended.append(line_gather(mixed))

    chosen = routes[:, 0]
    onehot = chosen[:, None] == jnp.arange(expert_count, dtype=jnp.int32)[None, :]
    counts = jnp.cumsum(onehot.astype(jnp.int32), axis=0)
    position = jnp.sum(jnp.where(onehot, counts, 0), axis=-1) - 1
    capacity = tok_rows // 8
    part = capacity // CHUNKS
    exp_local = w_gate.shape[0]
    slot_expert = jnp.arange(expert_count * part, dtype=jnp.int32) // part
    slot_place = jnp.arange(expert_count * part, dtype=jnp.int32) % part
    pickers = [
        (
            (slot_expert[:, None] == chosen[None, :])
            & (slot_place[:, None] + c * part == position[None, :])
        ).astype(BF16)
        for c in range(CHUNKS)
    ]

    sums = [jnp.zeros((tok_rows, half), F32) for _ in range(2)]
    for k in range(hx_count):
        rows_k = jnp.concatenate([attended[g][k] for g in range(kv_heads)], axis=1)
        sums = [s + dot32(rows_k, m) for s, m in zip(sums, out_mats[k])]
    first = jnp.where(parity == 0, sums[0], sums[1])
    second = jnp.where(parity == 0, sums[1], sums[0])
    attn_sum = jnp.concatenate([first, second], axis=1)
    own_tokens = lax.dynamic_slice_in_dim(tokens, hx_index * width, width, 1)
    stream = (own_tokens.astype(F32) + attn_sum).astype(BF16)

    expert_out = None
    for c in range(CHUNKS):
        sent = dot32(pickers[c], stream).astype(BF16)
        sent = sent.reshape(ctx_count, exp_local, part, width)
        taken = lax.all_to_all(sent, "ctx", split_axis=0, concat_axis=0, tiled=True)
        shares = line_gather(taken.reshape(ctx_count * exp_local * part, width))
        rows = jnp.zeros((ctx_count * exp_local * part, full_width), BF16)
        for k in range(hx_count):
            source = (hx_index - k + hx_count) % hx_count
            rows = lax.dynamic_update_slice_in_dim(rows, shares[k], source * width, 1)
        normed2 = root_norm(rows, ffn_gain).reshape(ctx_count, exp_local, part, full_width)
        outs = []
        for e in range(exp_local):
            here = normed2[:, e].reshape(ctx_count * part, full_width)
            logits = dot32(here, w_router)
            column = jnp.arange(expert_count, dtype=jnp.int32) == ctx_index * exp_local + e
            score = jax.nn.sigmoid(jnp.sum(jnp.where(column[None, :], logits, 0.0), axis=-1))
            routed = (here.astype(F32) * score[:, None]).astype(BF16)
            gate_out = dot32(routed, w_gate[e])
            up_out = dot32(routed, w_up[e])
            hidden = (jax.nn.silu(gate_out) * up_out).astype(BF16)
            outs.append(dot32(hidden, w_down[e]).astype(BF16))
        reduced = jnp.stack(
            [line_scatter(o).reshape(ctx_count, part, width) for o in outs], axis=1
        )
        returned = lax.all_to_all(reduced, "ctx", split_axis=0, concat_axis=0, tiled=True)
        back = lax.dot_general(
            pickers[c],
            returned.reshape(expert_count * part, width),
            (((0,), (0,)), ((), ())),
            preferred_element_type=F32,
        )
        expert_out = back if expert_out is None else expert_out + back
    return (stream.astype(F32) + expert_out).astype(BF16)


def solution(mesh):
    return jax.shard_map(
        body,
        mesh=mesh,
        in_specs=(
            P("ctx", None),
            P(),
            P(),
            P("ctx", "hx"),
            P("ctx", "hx"),
            P("ctx", "hx"),
            P("hx", None),
            P(),
            P("ctx", None),
            P("ctx", None, "hx"),
            P("ctx", None, "hx"),
            P("ctx", "hx", None),
        ),
        out_specs=P("ctx", "hx"),
        check_vma=False,
    )
```

time: 706 us -> 521 us (0.74)
  waiting for transfers between devices: 499 us -> 251 us
  starting transfers between devices: 4.42 us -> 131 us
  blocking collectives: 64.5 us -> 13.5 us
  between operations: 14 us -> 1.95 us
    psum x1 -> x0, waiting for transfers between devices: 234 us -> none  [body(): lax.psum(partial_attn.astype(jnp.bfloat16), 'hx').astype(jnp.float32)]
    ppermute x0 -> x74, waiting for transfers between devices: none -> 228 us  [the longest x12 99.7 us: line_gather(): lax.ppermute(right, 'hx', [(i, i + 1) for i in range(step - 1, count - 1)])]
    all_gather x5 -> x0, waiting for transfers between devices: 153 us -> none  [the longest x1 49.9 us: body(): lax.all_gather(w_query, 'ctx', axis=0, tiled=True)]
    ppermute x0 -> x74, starting transfers between devices: none -> 110 us  [the longest x12 31.3 us: line_gather(): lax.ppermute(left, 'hx', [(i + 1, i) for i in range(0, count - step)])]
    reduce_scatter x1 -> x0, waiting for transfers between devices: 92.6 us -> none  [body(): lax.psum_scatter(partial_expert.astype(jnp.bfloat16), 'hx', scatter_dimen...]
    all_to_all x1, blocking collectives: 64.5 us -> 13.5 us  [body(): taken = lax.all_to_all(sent, 'ctx', split_axis=0, concat_axis=0, tiled=True)]
    convert_element_type x5 -> x12, other arithmetic: 7.88 us -> 24 us  [the longest x4 9.27 us: line_scatter(): to_right = (to_right.astype(F32) + right.astype(F32)).astype(BF16)]
    all_to_all x0 -> x1, starting transfers between devices: none -> 13.7 us  [body(): taken = lax.all_to_all(sent, 'ctx', split_axis=0, concat_axis=0, tiled=True)]
  transfers between devices with their start and end apart: 8 -> 77, of which waited for: 8 -> 40; matrix products, arithmetic and copies ran while one was open for 4% -> 15% of each run, Pallas kernels for 0% -> 1%
where the time goes in v1:
time: 521 us; the launch traced here: 513 us
  waiting for transfers between devices  251 us (48%)
  starting transfers between devices  131 us (25%)
  matrix products  58.6 us (11%)
  other arithmetic  35.9 us (7%)
  local copies, waits for them, and re-layouts  17.4 us (3%)
  blocking collectives  13.5 us (3%)
    ppermute x12, waiting for transfers between devices, line_gather(): lax.ppermute(right, 'hx', [(i, i + 1) for i in range(step - 1, count - 1)])  99.7 us
    ppermute x35, waiting for transfers between devices, swap(): return lax.ppermute(value, axis, [(i, i ^ offset) for i in range(count)])  54.8 us
    dot_general x42, matrix products, dot32(): return jnp.dot(left, right, preferred_element_type=F32)  53.6 us
    ppermute x6, waiting for transfers between devices, line_scatter(): lax.ppermute(to_left, 'hx', [(i, i - 1) for i in range(count - step, coun...  39.1 us
    ppermute x12, starting transfers between devices, line_gather(): lax.ppermute(left, 'hx', [(i + 1, i) for i in range(0, count - step)])  31.3 us
    ppermute x12, starting transfers between devices, line_gather(): lax.ppermute(right, 'hx', [(i, i + 1) for i in range(step - 1, count - 1)])  29.8 us
    ppermute x12, waiting for transfers between devices, line_gather(): lax.ppermute(left, 'hx', [(i + 1, i) for i in range(0, count - step)])  29.6 us
    ppermute x35, starting transfers between devices, swap(): return lax.ppermute(value, axis, [(i, i ^ offset) for i in range(count)])  19.4 us
  transfers between devices with their start and end apart: 77, of which 40 were waited for; matrix products, arithmetic and copies ran while one was open for 15% of the time, Pallas kernels for 1%

profile of v1, /device:TPU:16, one launch (start us, length us, event | category | flops | bytes accessed | tf_op | source)
XLA Modules:
  0.0 512.8 jit_solution(11117998867646332956)
XLA Ops:
  9.3 3.6 fusion
  12.9 4.5 fusion.2
  26.1 3.5 constant_dynamic-slice_fusion.5
  34.8 9.1 %collective-permute-done.1 = bf16[640,384]{1,0:T(8,128)(2,1)S(1)} collective-permute-done((bf16[640,384]{1,0:T(8,128)(2,1)}, bf16[640,384]{1,0:T(8,128)(2,1)S(1)}, u32[]{:S(2)}, u32[]{:S(2)}) %collective-permute-start.1) | collective-permute-done | bytes 491552 | tf_op jit(solution)/shard_map/ppermute | solution.py:30
  44.9 8.5 %collective-permute-done.25 = bf16[640,384]{1,0:T(8,128)(2,1)S(1)} collective-permute-done((bf16[640,384]{1,0:T(8,128)(2,1)}, bf16[640,384]{1,0:T(8,128)(2,1)S(1)}, u32[]{:S(2)}, u32[]{:S(2)}) %collective-permute-start.25) | collective-permute-done | bytes 491552 | tf_op jit(solution)/shard_map/ppermute | solution.py:30
  57.7 8.2 %collective-permute-done.27 = bf16[640,384]{1,0:T(8,128)(2,1)S(1)} collective-permute-done((bf16[640,384]{1,0:T(8,128)(2,1)}, bf16[640,384]{1,0:T(8,128)(2,1)S(1)}, u32[]{:S(2)}, u32[]{:S(2)}) %collective-permute-start.27) | collective-permute-done | bytes 491552 | tf_op jit(solution)/shard_map/ppermute | solution.py:30
  80.9 6.7 %collective-permute-done.13 = bf16[320,512]{1,0:T(8,128)(2,1)S(1)} collective-permute-done((bf16[320,512]{1,0:T(8,128)(2,1)S(1)}, bf16[320,512]{1,0:T(8,128)(2,1)S(1)}, u32[]{:S(2)}, u32[]{:S(2)}) %collective-permute-start.13) | collective-permute-done | bytes 327712 | tf_op jit(solution)/shard_map/ppermute | solution.py:30
  97.9 11.0 %collective-permute-done.19 = bf16[512,512]{1,0:T(8,128)(2,1)S(1)} collective-permute-done((bf16[512,512]{1,0:T(8,128)(2,1)S(1)}, bf16[512,512]{1,0:T(8,128)(2,1)S(1)}, u32[]{:S(2)}, u32[]{:S(2)}) %collective-permute-start.19) | collective-permute-done | bytes 524320 | tf_op jit(solution)/shard_map/ppermute | solution.py:30
  112.5 4.4 collective-permute-done.21
  124.9 3.5 collective-permute-start.32
  132.6 12.6 %collective-permute-done.33 = bf16[512,384]{1,0:T(8,128)(2,1)S(1)} collective-permute-done((bf16[512,384]{1,0:T(8,128)(2,1)S(1)}, bf16[512,384]{1,0:T(8,128)(2,1)S(1)}, u32[]{:S(2)}, u32[]{:S(2)}) %collective-permute-start.33) | collective-permute-done | bytes 393248 | tf_op jit(solution)/shard_map/ppermute | solution.py:59
  147.1 4.7 collective-permute-start.34
  157.5 39.7 %collective-permute-done.36 = bf16[512,384]{1,0:T(8,128)(2,1)S(1)} collective-permute-done((bf16[512,384]{1,0:T(8,128)(2,1)S(1)}, bf16[512,384]{1,0:T(8,128)(2,1)S(1)}, u32[]{:S(2)}, u32[]{:S(2)}) %collective-permute-start.36) | collective-permute-done | bytes 393248 | tf_op jit(solution)/shard_map/ppermute | solution.py:58
  198.6 3.5 collective-permute-done.34
  210.2 4.4 collective-permute-done.42
  214.6 3.4 collective-permute-start.45
  218.0 4.0 collective-permute-done.44
  222.7 6.3 %collective-permute-done.45 = bf16[512,384]{1,0:T(8,128)(2,1)S(1)} collective-permute-done((bf16[512,384]{1,0:T(8,128)(2,1)S(1)}, bf16[512,384]{1,0:T(8,128)(2,1)S(1)}, u32[]{:S(2)}, u32[]{:S(2)}) %collective-permute-start.45) | collective-permute-done | bytes 393248 | tf_op jit(solution)/shard_map/ppermute | solution.py:58
  239.5 13.7 %all-to-all-start = ((bf16[8,1,32,1280]{3,2,1,0:T(8,128)(2,1)}), bf16[8,1,32,1280]{3,2,1,0:T(8,128)(2,1)S(1)}, u32[]{:S(2)}, u32[]{:S(2)}) async-start(bf16[8,1,32,1280]{3,2,1,0:T(8,128)(2,1)} %bitcast.6), calls=%async_computation | async-start | bytes 1310720 | tf_op jit(solution)/shard_map/all_to_all | solution.py:266
  253.1 11.1 %all-to-all-done = bf16[8,1,32,1280]{3,2,1,0:T(8,128)(2,1)S(1)} async-done(((bf16[8,1,32,1280]{3,2,1,0:T(8,128)(2,1)}), bf16[8,1,32,1280]{3,2,1,0:T(8,128)(2,1)S(1)}, u32[]{:S(2)}, u32[]{:S(2)}) %all-to-all-start) | async-done | bytes 655392 | tf_op jit(solution)/shard_map/all_to_all | solution.py:266
  267.8 13.5 %all_to_all.20 = bf16[8,1,32,1280]{3,2,1,0:T(8,128)(2,1)S(1)} all-to-all(bf16[8,1,32,1280]{3,2,1,0:T(8,128)(2,1)S(1)} %bitcast.98), channel_id=1, replica_groups=mesh['ctx'=8,'hx'=4] {'ctx'}, dimensions={0} | all-to-all | bytes 1310720 | tf_op jit(solution)/shard_map/all_to_all | solution.py:266
  281.4 4.2 collective-permute-start.63
  290.0 4.8 collective-permute-start.52
  294.8 6.0 %collective-permute-done.63 = bf16[256,1280]{1,0:T(8,128)(2,1)} collective-permute-done((bf16[256,1280]{1,0:T(8,128)(2,1)S(1)}, bf16[256,1280]{1,0:T(8,128)(2,1)}, u32[]{:S(2)}, u32[]{:S(2)}) %collective-permute-start.63) | collective-permute-done | bytes 655392 | tf_op jit(solution)/shard_map/ppermute | solution.py:59
  300.7 4.5 collective-permute-start.64
  307.6 11.6 %collective-permute-done.62 = bf16[256,1280]{1,0:T(8,128)(2,1)S(1)} collective-permute-done((bf16[256,1280]{1,0:T(8,128)(2,1)S(1)}, bf16[256,1280]{1,0:T(8,128)(2,1)S(1)}, u32[]{:S(2)}, u32[]{:S(2)}) %collective-permute-start.62) | collective-permute-done | bytes 655392 | tf_op jit(solution)/shard_map/ppermute | solution.py:58
  324.0 3.6 collective-permute-done.64
  328.3 5.1 collective-permute-done.54
  335.8 9.9 %collective-permute-done.66 = bf16[256,1280]{1,0:T(8,128)(2,1)} collective-permute-done((bf16[256,1280]{1,0:T(8,128)(2,1)S(1)}, bf16[256,1280]{1,0:T(8,128)(2,1)}, u32[]{:S(2)}, u32[]{:S(2)}) %collective-permute-start.66) | collective-permute-done | bytes 655392 | tf_op jit(solution)/shard_map/ppermute | solution.py:58
  345.7 4.3 collective-permute-start.67
  353.1 6.4 %collective-permute-done.55 = bf16[256,1280]{1,0:T(8,128)(2,1)S(1)} collective-permute-done((bf16[256,1280]{1,0:T(8,128)(2,1)}, bf16[256,1280]{1,0:T(8,128)(2,1)S(1)}, u32[]{:S(2)}, u32[]{:S(2)}) %collective-permute-start.55) | collective-permute-done | bytes 655392 | tf_op jit(solution)/shard_map/ppermute | solution.py:58
  359.5 12.4 %collective-permute-done.67 = bf16[256,1280]{1,0:T(8,128)(2,1)S(1)} collective-permute-done((bf16[256,1280]{1,0:T(8,128)(2,1)}, bf16[256,1280]{1,0:T(8,128)(2,1)S(1)}, u32[]{:S(2)}, u32[]{:S(2)}) %collective-permute-start.67) | collective-permute-done | bytes 655392 | tf_op jit(solution)/shard_map/ppermute | solution.py:58
  386.2 3.4 fusion.44
  389.6 3.2 fusion.15
  409.4 11.2 %collective-permute-done.59 = bf16[256,1280]{1,0:T(8,128)(2,1)} collective-permute-done((bf16[256,1280]{1,0:T(8,128)(2,1)}, bf16[256,1280]{1,0:T(8,128)(2,1)}, u32[]{:S(2)}, u32[]{:S(2)}) %collective-permute-start.59) | collective-permute-done | bytes 655392 | tf_op jit(solution)/shard_map/ppermute | solution.py:84
  420.6 3.5 collective-permute-done.57
  427.1 4.3 collective-permute-start.60
  431.4 3.2 collective-permute-done.71
  438.3 5.0 collective-permute-start.72
  445.3 3.4 collective-permute-done.60
  452.1 4.7 collective-permute-start.70
  456.8 5.9 %collective-permute-done.72 = bf16[256,1280]{1,0:T(8,128)(2,1)} collective-permute-done((bf16[256,1280]{1,0:T(8,128)(2,1)}, bf16[256,1280]{1,0:T(8,128)(2,1)}, u32[]{:S(2)}, u32[]{:S(2)}) %collective-permute-start.72) | collective-permute-done | bytes 655392 | tf_op jit(solution)/shard_map/ppermute | solution.py:84
  466.8 9.9 %collective-permute-done.61 = bf16[256,1280]{1,0:T(8,128)(2,1)} collective-permute-done((bf16[256,1280]{1,0:T(8,128)(2,1)S(1)}, bf16[256,1280]{1,0:T(8,128)(2,1)}, u32[]{:S(2)}, u32[]{:S(2)}) %collective-permute-start.61) | collective-permute-done | bytes 655392 | tf_op jit(solution)/shard_map/ppermute | solution.py:84
  479.3 3.5 all-to-all-start.1
  482.9 5.3 %collective-permute-done.73 = bf16[256,1280]{1,0:T(8,128)(2,1)} collective-permute-done((bf16[256,1280]{1,0:T(8,128)(2,1)}, bf16[256,1280]{1,0:T(8,128)(2,1)}, u32[]{:S(2)}, u32[]{:S(2)}) %collective-permute-start.73) | collective-permute-done | bytes 655392 | tf_op jit(solution)/shard_map/ppermute | solution.py:84
  490.6 3.3 all-to-all-done.1
  494.8 3.5 all-to-all-start.3
  500.2 9.2 %all-to-all-done.3 = bf16[8,1,32,1280]{3,2,1,0:T(8,128)(2,1)S(1)} async-done(((bf16[8,1,32,1280]{3,2,1,0:T(8,128)(2,1)}), bf16[8,1,32,1280]{3,2,1,0:T(8,128)(2,1)S(1)}, u32[]{:S(2)}, u32[]{:S(2)}) %all-to-all-start.3) | async-done | bytes 655392 | tf_op jit(solution)/shard_map/all_to_all | solution.py:287
  (290 shorter events, 175.5 us)
Async XLA Ops:
  3.5 63.6 %collective-permute-start.8 = (bf16[640,512]{1,0:T(8,128)(2,1)}, bf16[640,512]{1,0:T(8,128)(2,1)}, u32[]{:S(2)}, u32[]{:S(2)}) collective-permute-start(bf16[640,512]{1,0:T(8,128)(2,1)} %constant_dynamic-update-slice_fusion.2), channel_id=1, source_target_pairs={{0,4},{4,0},{8,12},{12,8},{16,20},{20,16},{24,28},{28,24},{1,5},{5... | collective-permute-start | bytes 1966088 | tf_op jit(solution)/shard_map/ppermute | solution.py:30
  3.5 65.8 %collective-permute-start.9 = (bf16[640,512]{1,0:T(8,128)(2,1)}, bf16[640,512]{1,0:T(8,128)(2,1)}, u32[]{:S(2)}, u32[]{:S(2)}) collective-permute-start(bf16[640,512]{1,0:T(8,128)(2,1)} %constant_dynamic-update-slice_fusion.2), channel_id=1, source_target_pairs={{0,8},{4,12},{8,0},{12,4},{16,24},{20,28},{24,16},{28,20},{1,9},{5... | collective-permute-start | bytes 1966088 | tf_op jit(solution)/shard_map/ppermute | solution.py:30
  5.0 67.5 %collective-permute-start.11 = (bf16[640,512]{1,0:T(8,128)(2,1)}, bf16[640,512]{1,0:T(8,128)(2,1)S(1)}, u32[]{:S(2)}, u32[]{:S(2)}) collective-permute-start(bf16[640,512]{1,0:T(8,128)(2,1)} %constant_dynamic-update-slice_fusion.2), channel_id=1, source_target_pairs={{0,16},{4,20},{8,24},{12,28},{16,0},{20,4},{24,8},{28,12},{1,17},{... | collective-permute-start | bytes 1966088 | tf_op jit(solution)/shard_map/ppermute | solution.py:30
  8.8 20.8 %collective-permute-start = (bf16[640,384]{1,0:T(8,128)(2,1)}, bf16[640,384]{1,0:T(8,128)(2,1)}, u32[]{:S(2)}, u32[]{:S(2)}) collective-permute-start(bf16[640,384]{1,0:T(8,128)(2,1)} %get-tuple-element.22), channel_id=1, source_target_pairs={{0,4},{4,0},{8,12},{12,8},{16,20},{20,16},{24,28},{28,24},{1,5},{5... | collective-permute-start | bytes 1474568 | tf_op jit(solution)/shard_map/ppermute | solution.py:30
  8.8 22.9 %collective-permute-start.24 = (bf16[640,384]{1,0:T(8,128)(2,1)}, bf16[640,384]{1,0:T(8,128)(2,1)}, u32[]{:S(2)}, u32[]{:S(2)}) collective-permute-start(bf16[640,384]{1,0:T(8,128)(2,1)} %get-tuple-element.23), channel_id=1, source_target_pairs={{0,4},{4,0},{8,12},{12,8},{16,20},{20,16},{24,28},{28,24},{1,5},{5... | collective-permute-start | bytes 1474568 | tf_op jit(solution)/shard_map/ppermute | solution.py:30
  31.7 21.7 %collective-permute-start.25 = (bf16[640,384]{1,0:T(8,128)(2,1)}, bf16[640,384]{1,0:T(8,128)(2,1)S(1)}, u32[]{:S(2)}, u32[]{:S(2)}) collective-permute-start(bf16[640,384]{1,0:T(8,128)(2,1)} %get-tuple-element.23), channel_id=1, source_target_pairs={{0,8},{4,12},{8,0},{12,4},{16,24},{20,28},{24,16},{28,20},{1,9},{5... | collective-permute-start | bytes 1474568 | tf_op jit(solution)/shard_map/ppermute | solution.py:30
  55.4 77.1 %collective-permute-start.40 = (bf16[768,640]{1,0:T(8,128)(2,1)S(1)}, bf16[768,640]{1,0:T(8,128)(2,1)S(1)}, u32[]{:S(2)}, u32[]{:S(2)}) collective-permute-start(bf16[768,640]{1,0:T(8,128)(2,1)S(1)} %get-tuple-element.6), channel_id=1, source_target_pairs={{0,1},{1,2},{2,3},{3,0},{4,5},{5,6},{6,7},{7,4},{8,9},{9,10},{10,1... | collective-permute-start | bytes 2949128 | tf_op jit(solution)/shard_map/ppermute | solution.py:196
  77.4 18.1 %collective-permute-start.4 = (bf16[640,384]{1,0:T(8,128)(2,1)S(1)}, bf16[640,384]{1,0:T(8,128)(2,1)S(1)}, u32[]{:S(2)}, u32[]{:S(2)}) collective-permute-start(bf16[640,384]{1,0:T(8,128)(2,1)S(1)} %collective-permute-done.3), channel_id=1, source_target_pairs={{0,4},{4,0},{8,12},{12,8},{16,20},{20,16},{24,28},{28,24},{1,5},{5... | collective-permute-start | bytes 1474568 | tf_op jit(solution)/shard_map/ppermute | solution.py:30
  92.0 19.1 %collective-permute-start.28 = (bf16[640,384]{1,0:T(8,128)(2,1)S(1)}, bf16[640,384]{1,0:T(8,128)(2,1)S(1)}, u32[]{:S(2)}, u32[]{:S(2)}) collective-permute-start(bf16[640,384]{1,0:T(8,128)(2,1)S(1)} %collective-permute-done.27), channel_id=1, source_target_pairs={{0,4},{4,0},{8,12},{12,8},{16,20},{20,16},{24,28},{28,24},{1,5},{5... | collective-permute-start | bytes 1474568 | tf_op jit(solution)/shard_map/ppermute | solution.py:30
  95.5 15.1 %collective-permute-start.17 = (bf16[512,512]{1,0:T(8,128)(2,1)S(1)}, bf16[512,512]{1,0:T(8,128)(2,1)S(1)}, u32[]{:S(2)}, u32[]{:S(2)}) collective-permute-start(bf16[512,512]{1,0:T(8,128)(2,1)S(1)} %get-tuple-element.25), channel_id=1, source_target_pairs={{0,8},{4,12},{8,0},{12,4},{16,24},{20,28},{24,16},{28,20},{1,9},{5... | collective-permute-start | bytes 1572872 | tf_op jit(solution)/shard_map/ppermute | solution.py:30
  111.7 95.7 %collective-permute-start.46 = (bf16[768,640]{1,0:T(8,128)(2,1)}, bf16[768,640]{1,0:T(8,128)(2,1)}, u32[]{:S(2)}, u32[]{:S(2)}) collective-permute-start(bf16[768,640]{1,0:T(8,128)(2,1)} %get-tuple-element.7), channel_id=1, source_target_pairs={{0,3},{1,0},{2,1},{3,2},{4,7},{5,4},{6,5},{7,6},{8,11},{9,8},{10,9... | collective-permute-start | bytes 2949128 | tf_op jit(solution)/shard_map/ppermute | solution.py:196
  122.5 22.7 %collective-permute-start.33 = (bf16[512,384]{1,0:T(8,128)(2,1)S(1)}, bf16[512,384]{1,0:T(8,128)(2,1)S(1)}, u32[]{:S(2)}, u32[]{:S(2)}) collective-permute-start(bf16[512,384]{1,0:T(8,128)(2,1)S(1)} %attend.2), channel_id=1, source_target_pairs={{1,0},{2,1},{3,2},{5,4},{6,5},{7,6},{9,8},{10,9},{11,10},{13,12},{... | collective-permute-start | bytes 1179656 | tf_op jit(solution)/shard_map/ppermute | solution.py:59
  124.9 22.2 %collective-permute-start.32 = (bf16[512,384]{1,0:T(8,128)(2,1)S(1)}, bf16[512,384]{1,0:T(8,128)(2,1)S(1)}, u32[]{:S(2)}, u32[]{:S(2)}) collective-permute-start(bf16[512,384]{1,0:T(8,128)(2,1)S(1)} %attend.2), channel_id=1, source_target_pairs={{0,1},{1,2},{2,3},{4,5},{5,6},{6,7},{8,9},{9,10},{10,11},{12,13},{... | collective-permute-start | bytes 1179656 | tf_op jit(solution)/shard_map/ppermute | solution.py:58
  130.0 23.6 %collective-permute-start.37 = (bf16[512,384]{1,0:T(8,128)(2,1)S(1)}, bf16[512,384]{1,0:T(8,128)(2,1)S(1)}, u32[]{:S(2)}, u32[]{:S(2)}) collective-permute-start(bf16[512,384]{1,0:T(8,128)(2,1)S(1)} %attend.3), channel_id=1, source_target_pairs={{1,0},{2,1},{3,2},{5,4},{6,5},{7,6},{9,8},{10,9},{11,10},{13,12},{... | collective-permute-start | bytes 1179656 | tf_op jit(solution)/shard_map/ppermute | solution.py:59
  132.5 75.0 %collective-permute-start.43 = (bf16[768,640]{1,0:T(8,128)(2,1)}, bf16[768,640]{1,0:T(8,128)(2,1)S(1)}, u32[]{:S(2)}, u32[]{:S(2)}) collective-permute-start(bf16[768,640]{1,0:T(8,128)(2,1)} %get-tuple-element.5), channel_id=1, source_target_pairs={{0,2},{1,3},{2,0},{3,1},{4,6},{5,7},{6,4},{7,5},{8,10},{9,11},{10,... | collective-permute-start | bytes 2949128 | tf_op jit(solution)/shard_map/ppermute | solution.py:196
  145.1 52.0 %collective-permute-start.36 = (bf16[512,384]{1,0:T(8,128)(2,1)S(1)}, bf16[512,384]{1,0:T(8,128)(2,1)S(1)}, u32[]{:S(2)}, u32[]{:S(2)}) collective-permute-start(bf16[512,384]{1,0:T(8,128)(2,1)S(1)} %attend.3), channel_id=1, source_target_pairs={{0,1},{1,2},{2,3},{4,5},{5,6},{6,7},{8,9},{9,10},{10,11},{12,13},{... | collective-permute-start | bytes 1179656 | tf_op jit(solution)/shard_map/ppermute | solution.py:58
  147.1 55.0 %collective-permute-start.34 = (bf16[512,384]{1,0:T(8,128)(2,1)S(1)}, bf16[512,384]{1,0:T(8,128)(2,1)}, u32[]{:S(2)}, u32[]{:S(2)}) collective-permute-start(bf16[512,384]{1,0:T(8,128)(2,1)S(1)} %collective-permute-done.33), channel_id=1, source_target_pairs={{1,0},{2,1},{5,4},{6,5},{9,8},{10,9},{13,12},{14,13},{17,16},{18,1... | collective-permute-start | bytes 1179656 | tf_op jit(solution)/shard_map/ppermute | solution.py:59
  153.6 52.4 %collective-permute-start.41 = (bf16[512,384]{1,0:T(8,128)(2,1)S(1)}, bf16[512,384]{1,0:T(8,128)(2,1)S(1)}, u32[]{:S(2)}, u32[]{:S(2)}) collective-permute-start(bf16[512,384]{1,0:T(8,128)(2,1)S(1)} %collective-permute-done.32), channel_id=1, source_target_pairs={{1,2},{2,3},{5,6},{6,7},{9,10},{10,11},{13,14},{14,15},{17,18},{18... | collective-permute-start | bytes 1179656 | tf_op jit(solution)/shard_map/ppermute | solution.py:58
  206.0 16.0 %collective-permute-start.44 = (bf16[512,384]{1,0:T(8,128)(2,1)S(1)}, bf16[512,384]{1,0:T(8,128)(2,1)S(1)}, u32[]{:S(2)}, u32[]{:S(2)}) collective-permute-start(bf16[512,384]{1,0:T(8,128)(2,1)S(1)} %collective-permute-done.41), channel_id=1, source_target_pairs={{2,3},{6,7},{10,11},{14,15},{18,19},{22,23},{26,27},{30,31}} | collective-permute-start | bytes 1179656 | tf_op jit(solution)/shard_map/ppermute | solution.py:58
  207.4 26.5 %collective-permute-start.47 = (bf16[768,640]{1,0:T(8,128)(2,1)S(1)}, bf16[768,640]{1,0:T(8,128)(2,1)S(1)}, u32[]{:S(2)}, u32[]{:S(2)}) collective-permute-start(bf16[768,640]{1,0:T(8,128)(2,1)S(1)} %copy-done.10), channel_id=1, source_target_pairs={{0,4},{4,0},{8,12},{12,8},{16,20},{20,16},{24,28},{28,24},{1,5},{5... | collective-permute-start | bytes 2949128 | tf_op jit(solution)/shard_map/ppermute | solution.py:30
  207.5 24.7 %collective-permute-start.49 = (bf16[768,640]{1,0:T(8,128)(2,1)}, bf16[768,640]{1,0:T(8,128)(2,1)S(1)}, u32[]{:S(2)}, u32[]{:S(2)}) collective-permute-start(bf16[768,640]{1,0:T(8,128)(2,1)} %collective-permute-done.46), channel_id=1, source_target_pairs={{0,4},{4,0},{8,12},{12,8},{16,20},{20,16},{24,28},{28,24},{1,5},{5... | collective-permute-start | bytes 2949128 | tf_op jit(solution)/shard_map/ppermute | solution.py:30
  210.2 25.4 %collective-permute-start.48 = (bf16[768,640]{1,0:T(8,128)(2,1)S(1)}, bf16[768,640]{1,0:T(8,128)(2,1)S(1)}, u32[]{:S(2)}, u32[]{:S(2)}) collective-permute-start(bf16[768,640]{1,0:T(8,128)(2,1)S(1)} %collective-permute-done.43), channel_id=1, source_target_pairs={{0,4},{4,0},{8,12},{12,8},{16,20},{20,16},{24,28},{28,24},{1,5},{5... | collective-permute-start | bytes 2949128 | tf_op jit(solution)/shard_map/ppermute | solution.py:30
  214.6 14.4 %collective-permute-start.45 = (bf16[512,384]{1,0:T(8,128)(2,1)S(1)}, bf16[512,384]{1,0:T(8,128)(2,1)S(1)}, u32[]{:S(2)}, u32[]{:S(2)}) collective-permute-start(bf16[512,384]{1,0:T(8,128)(2,1)S(1)} %collective-permute-done.42), channel_id=1, source_target_pairs={{2,3},{6,7},{10,11},{14,15},{18,19},{22,23},{26,27},{30,31}} | collective-permute-start | bytes 1179656 | tf_op jit(solution)/shard_map/ppermute | solution.py:58
  239.5 24.8 %all-to-all-start = ((bf16[8,1,32,1280]{3,2,1,0:T(8,128)(2,1)}), bf16[8,1,32,1280]{3,2,1,0:T(8,128)(2,1)S(1)}, u32[]{:S(2)}, u32[]{:S(2)}) async-start(bf16[8,1,32,1280]{3,2,1,0:T(8,128)(2,1)} %bitcast.6), calls=%async_computation | async-start | bytes 1310720 | tf_op jit(solution)/shard_map/all_to_all | solution.py:266
  264.3 25.7 %collective-permute-start.51 = (bf16[256,1280]{1,0:T(8,128)(2,1)S(1)}, bf16[256,1280]{1,0:T(8,128)(2,1)S(1)}, u32[]{:S(2)}, u32[]{:S(2)}) collective-permute-start(bf16[256,1280]{1,0:T(8,128)(2,1)S(1)} %bitcast.89), channel_id=1, source_target_pairs={{1,0},{2,1},{3,2},{5,4},{6,5},{7,6},{9,8},{10,9},{11,10},{13,12},{... | collective-permute-start | bytes 1966088 | tf_op jit(solution)/shard_map/ppermute | solution.py:59
  281.4 19.4 %collective-permute-start.63 = (bf16[256,1280]{1,0:T(8,128)(2,1)S(1)}, bf16[256,1280]{1,0:T(8,128)(2,1)}, u32[]{:S(2)}, u32[]{:S(2)}) collective-permute-start(bf16[256,1280]{1,0:T(8,128)(2,1)S(1)} %bitcast.92), channel_id=1, source_target_pairs={{1,0},{2,1},{3,2},{5,4},{6,5},{7,6},{9,8},{10,9},{11,10},{13,12},{... | collective-permute-start | bytes 1966088 | tf_op jit(solution)/shard_map/ppermute | solution.py:59
  285.6 19.7 %collective-permute-start.50 = (bf16[256,1280]{1,0:T(8,128)(2,1)S(1)}, bf16[256,1280]{1,0:T(8,128)(2,1)S(1)}, u32[]{:S(2)}, u32[]{:S(2)}) collective-permute-start(bf16[256,1280]{1,0:T(8,128)(2,1)S(1)} %bitcast.90), channel_id=1, source_target_pairs={{0,1},{1,2},{2,3},{4,5},{5,6},{6,7},{8,9},{9,10},{10,11},{12,13},{... | collective-permute-start | bytes 1966088 | tf_op jit(solution)/shard_map/ppermute | solution.py:58
  288.0 31.2 %collective-permute-start.62 = (bf16[256,1280]{1,0:T(8,128)(2,1)S(1)}, bf16[256,1280]{1,0:T(8,128)(2,1)S(1)}, u32[]{:S(2)}, u32[]{:S(2)}) collective-permute-start(bf16[256,1280]{1,0:T(8,128)(2,1)S(1)} %bitcast.93), channel_id=1, source_target_pairs={{0,1},{1,2},{2,3},{4,5},{5,6},{6,7},{8,9},{9,10},{10,11},{12,13},{... | collective-permute-start | bytes 1966088 | tf_op jit(solution)/shard_map/ppermute | solution.py:58
  290.0 31.7 %collective-permute-start.52 = (bf16[256,1280]{1,0:T(8,128)(2,1)S(1)}, bf16[256,1280]{1,0:T(8,128)(2,1)}, u32[]{:S(2)}, u32[]{:S(2)}) collective-permute-start(bf16[256,1280]{1,0:T(8,128)(2,1)S(1)} %collective-permute-done.51), channel_id=1, source_target_pairs={{1,0},{2,1},{5,4},{6,5},{9,8},{10,9},{13,12},{14,13},{17,16},{18,1... | collective-permute-start | bytes 1966088 | tf_op jit(solution)/shard_map/ppermute | solution.py:59
  300.7 26.8 %collective-permute-start.64 = (bf16[256,1280]{1,0:T(8,128)(2,1)}, bf16[256,1280]{1,0:T(8,128)(2,1)S(1)}, u32[]{:S(2)}, u32[]{:S(2)}) collective-permute-start(bf16[256,1280]{1,0:T(8,128)(2,1)} %collective-permute-done.63), channel_id=1, source_target_pairs={{1,0},{2,1},{5,4},{6,5},{9,8},{10,9},{13,12},{14,13},{17,16},{18,1... | collective-permute-start | bytes 1966088 | tf_op jit(solution)/shard_map/ppermute | solution.py:59
  305.3 28.1 %collective-permute-start.54 = (bf16[256,1280]{1,0:T(8,128)(2,1)S(1)}, bf16[256,1280]{1,0:T(8,128)(2,1)}, u32[]{:S(2)}, u32[]{:S(2)}) collective-permute-start(bf16[256,1280]{1,0:T(8,128)(2,1)S(1)} %collective-permute-done.50), channel_id=1, source_target_pairs={{1,2},{2,3},{5,6},{6,7},{9,10},{10,11},{13,14},{14,15},{17,18},{18... | collective-permute-start | bytes 1966088 | tf_op jit(solution)/shard_map/ppermute | solution.py:58
  319.2 26.5 %collective-permute-start.66 = (bf16[256,1280]{1,0:T(8,128)(2,1)S(1)}, bf16[256,1280]{1,0:T(8,128)(2,1)}, u32[]{:S(2)}, u32[]{:S(2)}) collective-permute-start(bf16[256,1280]{1,0:T(8,128)(2,1)S(1)} %collective-permute-done.62), channel_id=1, source_target_pairs={{1,2},{2,3},{5,6},{6,7},{9,10},{10,11},{13,14},{14,15},{17,18},{18... | collective-permute-start | bytes 1966088 | tf_op jit(solution)/shard_map/ppermute | solution.py:58
  321.7 28.4 %collective-permute-start.53 = (bf16[256,1280]{1,0:T(8,128)(2,1)}, bf16[256,1280]{1,0:T(8,128)(2,1)}, u32[]{:S(2)}, u32[]{:S(2)}) collective-permute-start(bf16[256,1280]{1,0:T(8,128)(2,1)} %collective-permute-done.52), channel_id=1, source_target_pairs={{1,0},{5,4},{9,8},{13,12},{17,16},{21,20},{25,24},{29,28}} | collective-permute-start | bytes 1966088 | tf_op jit(solution)/shard_map/ppermute | solution.py:59
  327.6 24.0 %collective-permute-start.65 = (bf16[256,1280]{1,0:T(8,128)(2,1)S(1)}, bf16[256,1280]{1,0:T(8,128)(2,1)S(1)}, u32[]{:S(2)}, u32[]{:S(2)}) collective-permute-start(bf16[256,1280]{1,0:T(8,128)(2,1)S(1)} %collective-permute-done.64), channel_id=1, source_target_pairs={{1,0},{5,4},{9,8},{13,12},{17,16},{21,20},{25,24},{29,28}} | collective-permute-start | bytes 1966088 | tf_op jit(solution)/shard_map/ppermute | solution.py:59
  333.3 26.1 %collective-permute-start.55 = (bf16[256,1280]{1,0:T(8,128)(2,1)}, bf16[256,1280]{1,0:T(8,128)(2,1)S(1)}, u32[]{:S(2)}, u32[]{:S(2)}) collective-permute-start(bf16[256,1280]{1,0:T(8,128)(2,1)} %collective-permute-done.54), channel_id=1, source_target_pairs={{2,3},{6,7},{10,11},{14,15},{18,19},{22,23},{26,27},{30,31}} | collective-permute-start | bytes 1966088 | tf_op jit(solution)/shard_map/ppermute | solution.py:58
  345.7 26.1 %collective-permute-start.67 = (bf16[256,1280]{1,0:T(8,128)(2,1)}, bf16[256,1280]{1,0:T(8,128)(2,1)S(1)}, u32[]{:S(2)}, u32[]{:S(2)}) collective-permute-start(bf16[256,1280]{1,0:T(8,128)(2,1)} %collective-permute-done.66), channel_id=1, source_target_pairs={{2,3},{6,7},{10,11},{14,15},{18,19},{22,23},{26,27},{30,31}} | collective-permute-start | bytes 1966088 | tf_op jit(solution)/shard_map/ppermute | solution.py:58
  400.7 19.9 %collective-permute-start.59 = (bf16[256,1280]{1,0:T(8,128)(2,1)}, bf16[256,1280]{1,0:T(8,128)(2,1)}, u32[]{:S(2)}, u32[]{:S(2)}) collective-permute-start(bf16[256,1280]{1,0:T(8,128)(2,1)} %get-tuple-element.19), channel_id=1, source_target_pairs={{3,2},{7,6},{11,10},{15,14},{19,18},{23,22},{27,26},{31,30}} | collective-permute-start | bytes 1966088 | tf_op jit(solution)/shard_map/ppermute | solution.py:84
  404.2 19.9 %collective-permute-start.57 = (bf16[256,1280]{1,0:T(8,128)(2,1)}, bf16[256,1280]{1,0:T(8,128)(2,1)}, u32[]{:S(2)}, u32[]{:S(2)}) collective-permute-start(bf16[256,1280]{1,0:T(8,128)(2,1)} %add_convert_fusion.9), channel_id=1, source_target_pairs={{0,1},{1,2},{4,5},{5,6},{8,9},{9,10},{12,13},{13,14},{16,17},{17,1... | collective-permute-start | bytes 1966088 | tf_op jit(solution)/shard_map/ppermute | solution.py:83
  405.5 29.2 %collective-permute-start.71 = (bf16[256,1280]{1,0:T(8,128)(2,1)}, bf16[256,1280]{1,0:T(8,128)(2,1)}, u32[]{:S(2)}, u32[]{:S(2)}) collective-permute-start(bf16[256,1280]{1,0:T(8,128)(2,1)} %get-tuple-element.15), channel_id=1, source_target_pairs={{3,2},{7,6},{11,10},{15,14},{19,18},{23,22},{27,26},{31,30}} | collective-permute-start | bytes 1966088 | tf_op jit(solution)/shard_map/ppermute | solution.py:84
  408.1 27.4 %collective-permute-start.69 = (bf16[256,1280]{1,0:T(8,128)(2,1)S(1)}, bf16[256,1280]{1,0:T(8,128)(2,1)}, u32[]{:S(2)}, u32[]{:S(2)}) collective-permute-start(bf16[256,1280]{1,0:T(8,128)(2,1)S(1)} %add_convert_fusion.4), channel_id=1, source_target_pairs={{0,1},{1,2},{4,5},{5,6},{8,9},{9,10},{12,13},{13,14},{16,17},{17,1... | collective-permute-start | bytes 1966088 | tf_op jit(solution)/shard_map/ppermute | solution.py:83
  427.1 21.6 %collective-permute-start.60 = (bf16[256,1280]{1,0:T(8,128)(2,1)}, bf16[256,1280]{1,0:T(8,128)(2,1)}, u32[]{:S(2)}, u32[]{:S(2)}) collective-permute-start(bf16[256,1280]{1,0:T(8,128)(2,1)} %get-tuple-element.17), channel_id=1, source_target_pairs={{2,1},{3,2},{6,5},{7,6},{10,9},{11,10},{14,13},{15,14},{18,17},{19... | collective-permute-start | bytes 1966088 | tf_op jit(solution)/shard_map/ppermute | solution.py:84
  438.3 24.4 %collective-permute-start.72 = (bf16[256,1280]{1,0:T(8,128)(2,1)}, bf16[256,1280]{1,0:T(8,128)(2,1)}, u32[]{:S(2)}, u32[]{:S(2)}) collective-permute-start(bf16[256,1280]{1,0:T(8,128)(2,1)} %get-tuple-element.13), channel_id=1, source_target_pairs={{2,1},{3,2},{6,5},{7,6},{10,9},{11,10},{14,13},{15,14},{18,17},{19... | collective-permute-start | bytes 1966088 | tf_op jit(solution)/shard_map/ppermute | solution.py:84
  443.3 23.5 %collective-permute-start.58 = (bf16[256,1280]{1,0:T(8,128)(2,1)}, bf16[256,1280]{1,0:T(8,128)(2,1)}, u32[]{:S(2)}, u32[]{:S(2)}) collective-permute-start(bf16[256,1280]{1,0:T(8,128)(2,1)} %get-tuple-element.16), channel_id=1, source_target_pairs={{0,1},{1,2},{2,3},{4,5},{5,6},{6,7},{8,9},{9,10},{10,11},{12,13},{... | collective-permute-start | bytes 1966088 | tf_op jit(solution)/shard_map/ppermute | solution.py:83
  450.1 26.6 %collective-permute-start.61 = (bf16[256,1280]{1,0:T(8,128)(2,1)S(1)}, bf16[256,1280]{1,0:T(8,128)(2,1)}, u32[]{:S(2)}, u32[]{:S(2)}) collective-permute-start(bf16[256,1280]{1,0:T(8,128)(2,1)S(1)} %add_convert_fusion.6), channel_id=1, source_target_pairs={{1,0},{2,1},{3,2},{5,4},{6,5},{7,6},{9,8},{10,9},{11,10},{13,12},{... | collective-permute-start | bytes 1966088 | tf_op jit(solution)/shard_map/ppermute | solution.py:84
  452.1 30.8 %collective-permute-start.70 = (bf16[256,1280]{1,0:T(8,128)(2,1)}, bf16[256,1280]{1,0:T(8,128)(2,1)}, u32[]{:S(2)}, u32[]{:S(2)}) collective-permute-start(bf16[256,1280]{1,0:T(8,128)(2,1)} %get-tuple-element.12), channel_id=1, source_target_pairs={{0,1},{1,2},{2,3},{4,5},{5,6},{6,7},{8,9},{9,10},{10,11},{12,13},{... | collective-permute-start | bytes 1966088 | tf_op jit(solution)/shard_map/ppermute | solution.py:83
  464.9 23.3 %collective-permute-start.73 = (bf16[256,1280]{1,0:T(8,128)(2,1)}, bf16[256,1280]{1,0:T(8,128)(2,1)}, u32[]{:S(2)}, u32[]{:S(2)}) collective-permute-start(bf16[256,1280]{1,0:T(8,128)(2,1)} %add_convert_fusion.1), channel_id=1, source_target_pairs={{1,0},{2,1},{3,2},{5,4},{6,5},{7,6},{9,8},{10,9},{11,10},{13,12},{... | collective-permute-start | bytes 1966088 | tf_op jit(solution)/shard_map/ppermute | solution.py:84
  479.3 14.6 %all-to-all-start.1 = ((bf16[8,1,32,1280]{3,2,1,0:T(8,128)(2,1)}), bf16[8,1,32,1280]{3,2,1,0:T(8,128)(2,1)S(1)}, u32[]{:S(2)}, u32[]{:S(2)}) async-start(bf16[8,1,32,1280]{3,2,1,0:T(8,128)(2,1)} %bitcast.96), calls=%async_computation.1 | async-start | bytes 1310720 | tf_op jit(solution)/shard_map/all_to_all | solution.py:287
  494.8 14.6 %all-to-all-start.3 = ((bf16[8,1,32,1280]{3,2,1,0:T(8,128)(2,1)}), bf16[8,1,32,1280]{3,2,1,0:T(8,128)(2,1)S(1)}, u32[]{:S(2)}, u32[]{:S(2)}) async-start(bf16[8,1,32,1280]{3,2,1,0:T(8,128)(2,1)} %bitcast.97), calls=%async_computation.3 | async-start | bytes 1310720 | tf_op jit(solution)/shard_map/all_to_all | solution.py:287
  (58 other events, 933.7 us)

commit v2 on v1

v2 whole, which is shorter than its diff:
```python
import functools

import jax
import jax.numpy as jnp
import numpy as np
from jax import lax
from jax.experimental import pallas as pl
from jax.experimental.pallas import tpu as pltpu
from jax.sharding import PartitionSpec as P

HD = 128
epsilon = 1e-05
LOG2E = 1.4426950408889634
CHUNKS = 2
F32 = jnp.float32
BF16 = jnp.bfloat16


def dot32(left, right):
    return jnp.dot(left, right, preferred_element_type=F32)


def root_norm(values, gains):
    floats = values.astype(F32)
    inverse = lax.rsqrt(jnp.mean(floats * floats, axis=-1, keepdims=True) + epsilon)
    return (floats * inverse * gains.astype(F32)).astype(BF16)


def swap(value, axis, offset):
    count = lax.axis_size(axis)
    return lax.ppermute(value, axis, [(i, i ^ offset) for i in range(count)])


def near_blocks(block):
    return {offset: swap(block, "ctx", offset) for offset in (2, 4)}


def far_block(near):
    half = near[2].shape[0] // 2
    return swap(near[4][:half], "ctx", 2), swap(near[2][half:], "ctx", 4)


def after(value, *earlier):
    return lax.optimization_barrier((value,) + earlier)[0]


def ring_shift(values, k):
    count = lax.axis_size("hx")
    return lax.ppermute(values, "hx", [(j, (j + k) % count) for j in range(count)])


def line_pairs(step, spread):
    count = lax.axis_size("hx")
    pairs = [[], []]
    for j in range(count - 1):
        if (j >= step - 1) if spread else (j < step):
            pairs[j % 2].append((j, j + 1))
        if (j + 1 <= count - step) if spread else (j + 1 >= count - step):
            pairs[j % 2].append((j + 1, j))
    return pairs


def pass_on(values, pairs):
    return lax.ppermute(values, "hx", pairs) if pairs else jnp.zeros_like(values)


def line_gather(block):
    count = lax.axis_size("hx")
    even_in = odd_in = block
    earlier = ()
    for step in range(1, count):
        pairs = line_pairs(step, True)
        if earlier:
            even_in, odd_in = lax.optimization_barrier((even_in, odd_in) + tuple(earlier))[:2]
        even_in, odd_in = (
            pass_on(odd_in, pairs[0]) if pairs[0] else None,
            pass_on(even_in, pairs[1]) if pairs[1] else None,
        )
        even_in = odd_in if even_in is None else even_in
        odd_in = even_in if odd_in is None else odd_in
        even_in, odd_in = lax.optimization_barrier((even_in, odd_in))
        earlier = yield (even_in, odd_in)


def arrival_order(count):
    table = []
    for own in range(count):
        entries = []
        for step in range(1, count):
            for source, swap_is_odd in (
                (own - step, own % 2 == 0),
                (own + step, own % 2 == 1),
            ):
                if 0 <= source < count:
                    entries.append((source, 2 * (step - 1) + swap_is_odd))
        table.append(entries)
    return table


def line_scatter(values):
    count = lax.axis_size("hx")
    odd = lax.axis_index("hx") % 2 == 1
    even_in = odd_in = None
    for step in range(1, count):
        pairs = line_pairs(step, False)
        right, left = values[(count - step) % count], values[step % count]
        even_out, odd_out = jnp.where(odd, left, right), jnp.where(odd, right, left)
        if step > 1:
            even_out = (even_out.astype(F32) + odd_in.astype(F32)).astype(BF16)
            odd_out = (odd_out.astype(F32) + even_in.astype(F32)).astype(BF16)
            earlier = tuple(earlier or ())
            even_out, odd_out = lax.optimization_barrier((even_out, odd_out) + earlier)[:2]
        even_in, odd_in = pass_on(even_out, pairs[0]), pass_on(odd_out, pairs[1])
        if step < count - 1:
            earlier = yield (even_in, odd_in)
    total = values[0].astype(F32)
    if count > 1:
        total = total + even_in.astype(F32) + odd_in.astype(F32)
    yield total.astype(BF16)


SMALL = pl.CostEstimate(flops=0, bytes_accessed=4096, transcendentals=0)
VMEM_LIMIT = 48 * 1024 * 1024


def norm_kernel(values_ref, gains_ref, out_ref):
    floats = values_ref[...].astype(F32)
    inverse = lax.rsqrt(jnp.mean(floats * floats, axis=-1, keepdims=True) + epsilon)
    out_ref[...] = (floats * inverse * gains_ref[...].astype(F32)).astype(BF16)


def norm_rows(values, gains):
    rows, columns = values.shape
    tile = min(rows, 128)
    return pl.pallas_call(
        norm_kernel,
        out_shape=jax.ShapeDtypeStruct((rows, columns), BF16),
        grid=(rows // tile,),
        in_specs=[
            pl.BlockSpec((tile, columns), lambda r: (r, 0)),
            pl.BlockSpec((1, columns), lambda r: (0, 0)),
        ],
        out_specs=pl.BlockSpec((tile, columns), lambda r: (r, 0)),
        compiler_params=pltpu.CompilerParams(vmem_limit_bytes=VMEM_LIMIT),
        cost_estimate=SMALL,
        name="norm_rows",
    )(values, gains.reshape(1, columns))


def choose(code, refs):
    value = refs[0][...]
    for number in range(1, len(refs)):
        value = jnp.where(code == number, refs[number][...], value)
    return value


def sum_dots_kernel(codes_ref, *refs, lefts, splits, added):
    left, right, chosen = refs[:lefts], refs[lefts : lefts + sum(splits)], refs[-1]
    out_ref = refs[-2]

    @pl.when(pl.program_id(0) == 0)
    def _():
        for k in range(len(splits)):
            chosen[k] = choose(codes_ref[k], left)

    total = None
    for more in refs[lefts + sum(splits) : lefts + sum(splits) + added]:
        part = more[...].astype(F32)
        total = part if total is None else total + part
    number = 0
    for k, split in enumerate(splits):
        at = 0
        for _ in range(split):
            rows = right[number].shape[0]
            part = dot32(chosen[k, :, at : at + rows], right[number][...])
            total = part if total is None else total + part
            at += rows
            number += 1
    out_ref[...] = total.astype(out_ref.dtype)


def sum_dots(codes, lefts, rights, added):
    rows, columns = lefts[0].shape[0], rights[0][0].shape[1]
    tile = 256 if columns % 256 == 0 else 128
    flat = [m for mats in rights for m in mats]
    out = pl.BlockSpec((rows, tile), lambda c, s: (0, c))
    return pl.pallas_call(
        functools.partial(
            sum_dots_kernel,
            lefts=len(lefts),
            splits=tuple(len(mats) for mats in rights),
            added=len(added),
        ),
        out_shape=jax.ShapeDtypeStruct((rows, columns), BF16),
        grid_spec=pltpu.PrefetchScalarGridSpec(
            num_scalar_prefetch=1,
            grid=(columns // tile,),
            in_specs=[pl.BlockSpec(m.shape, lambda c, s: (0, 0)) for m in lefts]
            + [pl.BlockSpec((m.shape[0], tile), lambda c, s: (0, c)) for m in flat]
            + [out] * len(added),
            out_specs=out,
            scratch_shapes=[pltpu.VMEM((len(rights),) + lefts[0].shape, BF16)],
        ),
        compiler_params=pltpu.CompilerParams(vmem_limit_bytes=VMEM_LIMIT),
        cost_estimate=SMALL,
        name="sum_dots",
    )(codes, *lefts, *flat, *added)


def project_kernel(places_ref, *refs, count, mats, added):
    del places_ref
    outs = refs[len(refs) - count :]
    for j in range(count):
        total = refs[(count + 1) * mats + j][...] if added else None
        for k in range(mats):
            part = dot32(refs[j * mats + k][...], refs[count * mats + k][...])
            total = part if total is None else total + part
        outs[j][...] = total.astype(outs[j].dtype)


def project(values, mats, places, totals, dtype):
    rows = values[0].shape[0]
    columns = mats[0].shape[1]
    whole = pl.BlockSpec((rows, columns), lambda g, s: (0, 0))

    def columns_at(k):
        return pl.BlockSpec((rows, mats[k].shape[0]), lambda g, s: (0, s[k]))

    return pl.pallas_call(
        functools.partial(
            project_kernel, count=len(values), mats=len(mats), added=totals is not None
        ),
        out_shape=[jax.ShapeDtypeStruct((rows, columns), dtype) for _ in values],
        grid_spec=pltpu.PrefetchScalarGridSpec(
            num_scalar_prefetch=1,
            grid=(1,),
            in_specs=[columns_at(k) for _ in values for k in range(len(mats))]
            + [pl.BlockSpec(m.shape, lambda g, s: (0, 0)) for m in mats]
            + [whole] * len(totals or ()),
            out_specs=[whole] * len(values),
        ),
        compiler_params=pltpu.CompilerParams(vmem_limit_bytes=VMEM_LIMIT),
        cost_estimate=SMALL,
        name="project",
    )(
        jnp.stack(places).astype(jnp.int32),
        *[v for v in values for _ in mats],
        *mats,
        *(totals or ()),
    )


def attend_kernel(places_ref, query_ref, *refs, group_size):
    *pieces, out_ref, held = refs
    rows = query_ref.shape[0]
    own = places_ref[0]
    scale = HD ** (-0.5) * LOG2E
    queries = [query_ref[:, g * HD : (g + 1) * HD] for g in range(group_size)]

    number = 1
    for piece in pieces:
        for start in range(0, piece.shape[0], rows):
            to = pl.multiple_of(places_ref[number] * rows, rows)
            held[pl.ds(to, rows), :] = piece[start : start + rows, :]
            number += 1

    def block(start, states, masked):
        keys = held[pl.ds(start, rows), :HD]
        values = held[pl.ds(start, rows), HD:]
        states_out = []
        for query, (top, total, acc) in zip(queries, states):
            scores = lax.dot_general(
                keys, query, (((1,), (1,)), ((), ())), preferred_element_type=F32
            )
            if masked:
                key_at = lax.broadcasted_iota(jnp.int32, scores.shape, 0)
                query_at = lax.broadcasted_iota(jnp.int32, scores.shape, 1)
                scores = jnp.where(key_at <= query_at, scores, -1e30)
            new_top = jnp.maximum(top, jnp.max(scores, axis=0, keepdims=True))
            weights = jnp.exp2((scores - new_top) * scale)
            factor = jnp.exp2((top - new_top) * scale)
            total = total * factor + jnp.sum(weights, axis=0, keepdims=True)
            mixed = lax.dot_general(
                values,
                weights.astype(BF16),
                (((0,), (0,)), ((), ())),
                preferred_element_type=F32,
            )
            states_out.append((new_top, total, acc * factor + mixed))
        return tuple(states_out)

    start_state = tuple(
        (
            jnp.full((1, rows), -1e30, F32),
            jnp.zeros((1, rows), F32),
            jnp.zeros((HD, rows), F32),
        )
        for _ in range(group_size)
    )
    states = block(pl.multiple_of(own * rows, rows), start_state, True)
    states = lax.fori_loop(
        0, own, lambda j, held: block(pl.multiple_of(j * rows, rows), held, False), states
    )
    for g, (_, total, acc) in enumerate(states):
        out_ref[:, g * HD : (g + 1) * HD] = (acc / total).T.astype(BF16)


def attend(own, queries, pieces, places):
    rows, width = queries.shape
    count = sum(p.shape[0] for p in pieces)
    whole = pl.BlockSpec((rows, width), lambda g, s: (0, 0))
    return pl.pallas_call(
        functools.partial(attend_kernel, group_size=width // HD),
        out_shape=jax.ShapeDtypeStruct((rows, width), BF16),
        grid_spec=pltpu.PrefetchScalarGridSpec(
            num_scalar_prefetch=1,
            grid=(1,),
            in_specs=[whole] + [pl.BlockSpec(p.shape, lambda g, s: (0, 0)) for p in pieces],
            out_specs=whole,
            scratch_shapes=[pltpu.VMEM((count, 2 * HD), BF16)],
        ),
        compiler_params=pltpu.CompilerParams(vmem_limit_bytes=VMEM_LIMIT),
        cost_estimate=pl.CostEstimate(
            flops=4 * rows * count * width,
            bytes_accessed=4 * count * HD,
            transcendentals=rows * count * width // HD,
        ),
        name="attend",
    )(jnp.stack([own] + places).astype(jnp.int32), queries, *pieces)


def hidden_tile(hidden):
    return 256 if hidden % 256 == 0 else 128


def scale_share(code_ref, shares, gain_ref, router_ref, scaled_ref):
    value = choose(code_ref[1], shares).astype(F32)
    scaled = (value * gain_ref[...].astype(F32)).astype(BF16)
    scaled_ref[...] = scaled

    def lanes(wide):
        return sum(wide[:, at : at + 128] for at in range(0, wide.shape[1], 128))

    return lanes(value * value), lanes(scaled.astype(F32) * router_ref[...].astype(F32))


def share_kernel(code_ref, *refs, shares, added):
    gain_ref, router_ref, gate_ref, up_ref = refs[shares : shares + 4]
    totals, outs, scaled = refs[shares + 4 : -5], refs[-5:-1], refs[-1]

    @pl.when(pl.program_id(0) == 0)
    def _():
        parts = scale_share(code_ref, refs[:shares], gain_ref, router_ref, scaled)
        for number, part in enumerate(parts):
            outs[2 + number][...] = part + totals[2 + number][...] if added else part

    for number, mat in enumerate((gate_ref, up_ref)):
        part = dot32(scaled[...], mat[0])
        outs[number][...] = part + totals[number][...] if added else part


def expert_share(code, shares, gains, router_row, w_gate, w_up, totals, which):
    rows, width = shares[0].shape
    hidden = w_gate.shape[2]
    tile = hidden_tile(hidden)
    sums = [pl.BlockSpec((rows, tile), lambda t, s: (0, t))] * 2 + [
        pl.BlockSpec((rows, 128), lambda t, s: (0, 0))
    ] * 2
    return pl.pallas_call(
        functools.partial(share_kernel, shares=len(shares), added=totals is not None),
        out_shape=[jax.ShapeDtypeStruct((rows, n), F32) for n in (hidden, hidden, 128, 128)],
        grid_spec=pltpu.PrefetchScalarGridSpec(
            num_scalar_prefetch=1,
            grid=(hidden // tile,),
            in_specs=[pl.BlockSpec((rows, width), lambda t, s: (0, 0))] * len(shares)
            + [pl.BlockSpec((1, width), lambda t, s: (0, s[0]))] * 2
            + [pl.BlockSpec((1, width, tile), lambda t, s: (which, s[0], t))] * 2
            + (sums if totals is not None else []),
            out_specs=sums,
            scratch_shapes=[pltpu.VMEM((rows, width), BF16)],
        ),
        compiler_params=pltpu.CompilerParams(vmem_limit_bytes=VMEM_LIMIT),
        cost_estimate=SMALL,
        name="expert_share",
    )(code, *shares, gains, router_row, w_gate, w_up, *(totals or ()))


def finish_kernel(code_ref, *refs, shares, tiles, full_width):
    gain_ref, router_ref, gate_ref, up_ref = refs[shares : shares + 4]
    gate_sum, up_sum, squares_sum, logits_sum, down_ref, out_ref = refs[shares + 4 : shares + 10]
    scaled, factor, hidden = refs[-3:]
    step = pl.program_id(0)

    @pl.when(step == 0)
    def _():
        squares, logits = scale_share(code_ref, refs[:shares], gain_ref, router_ref, scaled)
        squares = jnp.sum(squares + squares_sum[...], axis=-1, keepdims=True)
        logit = jnp.sum(logits + logits_sum[...], axis=-1, keepdims=True)
        inverse = lax.rsqrt(squares / full_width + epsilon)
        score = 1.0 / (1.0 + jnp.exp(-logit * inverse))
        factor[...] = jnp.broadcast_to(inverse * score, factor.shape)

    @pl.when(step < tiles)
    def _():
        scale = factor[:, :1]
        gate = (dot32(scaled[...], gate_ref[0]) + gate_sum[...]) * scale
        up = (dot32(scaled[...], up_ref[0]) + up_sum[...]) * scale
        hidden[step] = (gate / (1.0 + jnp.exp(-gate)) * up).astype(BF16)

    @pl.when(step >= tiles)
    def _():
        tile = hidden.shape[2]
        total = None
        for t in range(tiles):
            part = dot32(hidden[t], down_ref[0, t * tile : (t + 1) * tile, :])
            total = part if total is None else total + part
        out_ref[0] = total.astype(BF16)


def expert_finish(code, shares, gains, router_row, w_gate, w_up, totals, w_down, which):
    rows, width = shares[0].shape
    hidden = w_gate.shape[2]
    count = w_down.shape[2] // width
    tile = hidden_tile(hidden)
    tiles = hidden // tile

    def at(t):
        return jnp.minimum(t, tiles - 1)

    def after_tiles(t):
        return jnp.maximum(t - tiles, 0)

    return pl.pallas_call(
        functools.partial(
            finish_kernel, shares=len(shares), tiles=tiles, full_width=w_down.shape[2]
        ),
        out_shape=jax.ShapeDtypeStruct((count, rows, width), BF16),
        grid_spec=pltpu.PrefetchScalarGridSpec(
            num_scalar_prefetch=1,
            grid=(tiles + count,),
            in_specs=[pl.BlockSpec((rows, width), lambda t, s: (0, 0))] * len(shares)
            + [pl.BlockSpec((1, width), lambda t, s: (0, s[0]))] * 2
            + [pl.BlockSpec((1, width, tile), lambda t, s: (which, s[0], at(t)))] * 2
            + [pl.BlockSpec((rows, tile), lambda t, s: (0, at(t)))] * 2
            + [pl.BlockSpec((rows, 128), lambda t, s: (0, 0))] * 2
            + [
                pl.BlockSpec(
                    (1, hidden, width),
                    lambda t, s: (which, 0, lax.rem(s[2] + after_tiles(t), count)),
                )
            ],
            out_specs=pl.BlockSpec((1, rows, width), lambda t, s: (after_tiles(t), 0, 0)),
            scratch_shapes=[
                pltpu.VMEM((rows, width), BF16),
                pltpu.VMEM((rows, 128), F32),
                pltpu.VMEM((tiles, rows, tile), BF16),
            ],
        ),
        compiler_params=pltpu.CompilerParams(vmem_limit_bytes=VMEM_LIMIT),
        cost_estimate=SMALL,
        name="expert_finish",
    )(code, *shares, gains, router_row, w_gate, w_up, *totals, w_down)


def attention_share(tokens, own_tokens, attn_gain, w_query, w_key, w_value, w_out):
    ctx_index = lax.axis_index("ctx")
    kv_heads = w_key.shape[1] // HD
    group_width = w_query.shape[1] // kv_heads
    normed = root_norm(tokens, attn_gain)
    queries, keys, values = (
        dot32(normed, lax.all_gather(w, "ctx", axis=0, tiled=True)).astype(BF16)
        for w in (w_query, w_key, w_value)
    )
    keys = lax.all_gather(keys, "ctx", axis=0, tiled=True)
    values = lax.all_gather(values, "ctx", axis=0, tiled=True)
    places = [jnp.int32(b) for b in range(lax.axis_size("ctx"))]
    attended = []
    for g in range(kv_heads):
        head = slice(g * HD, (g + 1) * HD)
        piece = jnp.concatenate([keys[:, head], values[:, head]], axis=1)
        query = queries[:, g * group_width : (g + 1) * group_width]
        attended.append(attend(ctx_index, query, [piece], places))
    partial = dot32(jnp.concatenate(attended, axis=1), w_out).astype(BF16)
    attn_sum = lax.psum_scatter(partial, "hx", scatter_dimension=1, tiled=True)
    return (own_tokens.astype(F32) + attn_sum.astype(F32)).astype(BF16)


def paired_attention_share(tokens, own_tokens, attn_gain, w_query, w_key, w_value, w_out):
    ctx_count = lax.axis_size("ctx")
    hx_count = lax.axis_size("hx")
    ctx_index = lax.axis_index("ctx")
    hx_index = lax.axis_index("hx")
    parity = ctx_index % 2
    tok_rows, full_width = tokens.shape
    width = full_width // hx_count
    kv_heads = w_key.shape[1] // HD // 2
    kv_width = kv_heads * HD
    query_width = w_query.shape[1] // 2
    group_width = query_width // kv_heads

    def side(matrix, which, size, axis=1):
        return lax.dynamic_slice_in_dim(matrix, which * size, size, axis)

    own_kv = jnp.concatenate([side(m, parity, kv_width) for m in (w_key, w_value)], axis=1)
    own_query = side(w_query, parity, query_width)
    other_kv = jnp.concatenate([side(m, 1 - parity, kv_width) for m in (w_key, w_value)], axis=1)
    take = swap(other_kv, "ctx", 1)
    take_query = swap(side(w_query, after(1 - parity, take), query_width), "ctx", 1)
    other_tokens = swap(after(tokens, take_query), "ctx", 1)
    middle = hx_count // 2 if hx_count > 2 else 0
    half_rows = query_width // 2
    moves = []
    for k in [k for k in range(1, hx_count) if k != middle] + [middle] * (middle > 0):
        pieces = ((0, half_rows), (half_rows, half_rows)) if k == middle else ((0, query_width),)
        moves += [(k, *piece) for piece in pieces]

    def out_block(k, first_row, size, row_at):
        place = (row_at + first_row, (hx_index + k) % hx_count * width)
        return lax.dynamic_slice(w_out, place, (size, width))

    out_parts = {}

    def next_block(*earlier):
        if not moves:
            return None
        k, first_row, size = moves.pop(0)
        return k, out_block(k, first_row, size, after(parity * query_width, *earlier))

    def move(sent, *earlier):
        if sent is None:
            return ()
        k, block = sent
        block = after(block, *earlier) if earlier else block
        out_parts.setdefault(k, []).append(ring_shift(block, k))
        return (out_parts[k][-1],)

    def ready(sent):
        return () if sent is None else (sent[1],)

    def in_order(own, other):
        pair = (jnp.where(parity == 0, own, other), jnp.where(parity == 0, other, own))
        return jnp.concatenate(pair, axis=0)

    kv_mats = in_order(own_kv, take)
    query_mats = in_order(own_query, take_query)

    def together(arrived, *others):
        flat, tree = jax.tree.flatten(arrived)
        flat = lax.optimization_barrier(tuple(flat) + others)
        return jax.tree.unflatten(tree, flat[: len(flat) - len(others)])

    def pair_at(offset):
        return (ctx_index ^ offset) // 2

    def project_near(mats, near):
        places = [pair_at(0), pair_at(2), pair_at(4)]
        return project(normed, [mats, near[2], near[4]], places, None, F32)

    def project_far(far, total):
        places = [2 * pair_at(6), 2 * pair_at(6) + 1]
        return project(normed, list(far), places, total, BF16)

    normed = [norm_rows(t, attn_gain) for t in (tokens, other_tokens)]
    sent = next_block(take)
    following = next_block(take_query)
    kv_near = together(
        near_blocks(kv_mats), *move(sent), *ready(following), other_tokens, normed[0]
    )
    first = kv_near[2]
    sent, following = following, next_block(first)
    kv_total = project_near(kv_mats, kv_near)
    kv_far, query_near, kv_total = together(
        (far_block(kv_near), near_blocks(after(query_mats, first)), kv_total),
        *move(sent, first),
        *ready(following),
    )
    before, first = first, query_near[2]
    sent, following = following, next_block(before)
    kv_pair = jnp.concatenate(project_far(kv_far, kv_total), axis=0)
    query_total = project_near(query_mats, query_near)
    block_near, query_far, query_total = together(
        (near_blocks(kv_pair), far_block(query_near), query_total),
        *move(sent, first),
        *ready(following),
    )
    first = block_near[2]
    last_move = move(following, first)
    out_parts[0] = [out_block(0, 0, query_width, after(parity * query_width, first))]
    block_far = far_block(block_near)
    queries = project_far(query_far, query_total)
    pieces = [kv_pair, block_near[2], block_near[4], *block_far]
    places = [ctx_index ^ o ^ j for o in (0, 2, 4, 6) for j in (0, 1)]

    def head(piece, g):
        if kv_heads == 1:
            return piece
        columns = [piece[:, h * HD : (h + 1) * HD] for h in (g, kv_heads + g)]
        return jnp.concatenate(columns, axis=1)

    lefts = {}
    for j in (1, 0):
        attended = [
            attend(
                ctx_index ^ j,
                queries[j][:, g * group_width : (g + 1) * group_width],
                [head(piece, g) for piece in pieces],
                places,
            )
            for g in range(kv_heads)
        ]
        attended = jnp.concatenate(attended, axis=1)
        if j == 1:
            attended = after(attended, *last_move) if last_move else attended
        lefts[j] = [attended] + [x for pair in line_gather(attended) for x in pair]
    flat = lax.optimization_barrier(tuple(lefts[1]) + tuple(lefts[0]))
    lefts = {1: flat[: len(lefts[1])], 0: flat[len(lefts[1]) :]}
    table = np.zeros((hx_count, hx_count), np.int32)
    for own, entries in enumerate(arrival_order(hx_count)):
        for source, number in entries:
            table[own, (own - source) % hx_count] = 1 + number
    codes = jnp.asarray(table)[hx_index]
    rights = [out_parts[k] for k in range(hx_count)]
    given = swap(sum_dots(codes, lefts[1], rights, ()), "ctx", 1)
    return sum_dots(codes, lefts[0], rights, (given, own_tokens))


def body(
    tokens,
    attn_gain,
    ffn_gain,
    w_query,
    w_key,
    w_value,
    w_out,
    w_router,
    routes,
    w_gate,
    w_up,
    w_down,
):
    ctx_count = lax.axis_size("ctx")
    hx_count = lax.axis_size("hx")
    ctx_index = lax.axis_index("ctx")
    hx_index = lax.axis_index("hx")
    tok_rows, full_width = tokens.shape
    width = full_width // hx_count
    expert_count = w_router.shape[1]

    chosen = routes[:, 0]
    onehot = chosen[:, None] == jnp.arange(expert_count, dtype=jnp.int32)[None, :]
    counts = jnp.cumsum(onehot.astype(jnp.int32), axis=0)
    position = jnp.sum(jnp.where(onehot, counts, 0), axis=-1) - 1
    capacity = tok_rows // 8
    part = capacity // CHUNKS
    exp_local = w_gate.shape[0]
    slot_expert = jnp.arange(expert_count * part, dtype=jnp.int32) // part
    slot_place = jnp.arange(expert_count * part, dtype=jnp.int32) % part
    pickers = [
        (
            (slot_expert[:, None] == chosen[None, :])
            & (slot_place[:, None] + c * part == position[None, :])
        ).astype(BF16)
        for c in range(CHUNKS)
    ]

    paired = ctx_count // 2 == 4 and (w_key.shape[1] // HD) % 2 == 0
    share_of = paired_attention_share if paired else attention_share
    own_tokens = lax.dynamic_slice_in_dim(tokens, hx_index * width, width, 1)
    stream = share_of(tokens, own_tokens, attn_gain, w_query, w_key, w_value, w_out)

    gains = ffn_gain.reshape(1, full_width)
    router_rows = w_router.T
    order = arrival_order(hx_count)
    codes = [jnp.stack([hx_index, jnp.int32(0), hx_index]).astype(jnp.int32)]
    for t in range(hx_count - 1):
        found = jnp.asarray(np.array([entries[t] for entries in order], np.int32))[hx_index]
        codes.append(jnp.concatenate([found, codes[0][2:]]))

    def give_back(c, reduced):
        reduced = jnp.stack([r.reshape(ctx_count, part, width) for r in reduced], axis=1)
        returned = lax.all_to_all(reduced, "ctx", split_axis=0, concat_axis=0, tiled=True)
        return returned.reshape(expert_count * part, width)

    returned = []
    scatter, arrived, reached = None, (), ()
    for c in range(CHUNKS):
        sent = dot32(pickers[c], stream).astype(BF16)
        sent = sent.reshape(ctx_count, exp_local, part, width)
        taken = lax.all_to_all(sent, "ctx", split_axis=0, concat_axis=0, tiled=True)
        if reached:
            taken = after(taken, *reached)
        taken = taken.reshape(ctx_count, exp_local, part, width)
        taken = taken.swapaxes(0, 1).reshape(exp_local * ctx_count * part, width)
        gather = line_gather(taken)
        rows = [slice(e * ctx_count * part, (e + 1) * ctx_count * part) for e in range(exp_local)]
        router = [
            lax.dynamic_slice_in_dim(router_rows, ctx_index * exp_local + e, 1, 0)
            for e in range(exp_local)
        ]
        shares = [taken]
        totals = [None] * exp_local
        for t in range(hx_count - 1):
            earlier = [x for sums in totals if sums for x in sums[2:]] + shares[-1:] * (t == 0)
            if t == hx_count - 2:
                earlier += arrived
            pair = next(gather) if t == 0 else gather.send(earlier)
            totals = [
                expert_share(
                    codes[t], [x[rows[e]] for x in shares[t > 0 :]], gains, router[e], w_gate, w_up, totals[e], e
                )
                for e in range(exp_local)
            ]
            reached = pair
            if scatter and t == hx_count - 2:
                arrived = [x for sums in scatter for x in next(sums)]
                pair = lax.optimization_barrier(tuple(pair) + tuple(arrived))[:2]
            shares = shares + list(pair)
        outs = [
            expert_finish(
                codes[-1], [x[rows[e]] for x in shares[1:]], gains, router[e], w_gate, w_up, totals[e], w_down, e
            )
            for e in range(exp_local)
        ]
        reduced = None
        if scatter:
            for _ in range(hx_count - 4):
                [next(sums) for sums in scatter]
            reduced = [next(sums) for sums in scatter]
            outs = [after(o, *reduced) for o in outs]
        scatter = [line_scatter(o) for o in outs]
        arrived = [x for sums in scatter for x in next(sums)]
        if reduced:
            returned.append(give_back(c - 1, [after(r, *arrived) for r in reduced]))
    for step in range(hx_count - 3):
        [next(sums) for sums in scatter]
    reduced = [sums.send(returned) if hx_count > 2 else next(sums) for sums in scatter]
    returned.append(give_back(CHUNKS - 1, reduced))
    expert_out = sum(
        lax.dot_general(p, r, (((0,), (0,)), ((), ())), preferred_element_type=F32)
        for p, r in zip(pickers, returned)
    )
    return (stream.astype(F32) + expert_out).astype(BF16)


def solution(mesh):
    return jax.shard_map(
        body,
        mesh=mesh,
        in_specs=(
            P("ctx", None),
            P(),
            P(),
            P("ctx", "hx"),
            P("ctx", "hx"),
            P("ctx", "hx"),
            P("hx", None),
            P(),
            P("ctx", None),
            P("ctx", None, "hx"),
            P("ctx", None, "hx"),
            P("ctx", "hx", None),
        ),
        out_specs=P("ctx", "hx"),
        check_vma=False,
    )
```

time: 521 us -> 452 us (0.87)
  waiting for transfers between devices: 251 us -> 129 us
  Pallas kernels: 3.21 us -> 117 us
  matrix products: 58.6 us -> 9.14 us
  local copies, waits for them, and re-layouts: 17.4 us -> 50 us
  other arithmetic: 35.9 us -> 13.8 us
  blocking collectives: 13.5 us -> 0 us
  starting transfers between devices: 131 us -> 124 us
    pallas_call x2 -> x18, Pallas kernels: 3.21 us -> 117 us  [the longest x6 32.8 us: expert_share(): pl.pallas_call(functools.partial(share_kernel, shares=len(shares), added=...]
    ppermute x39 -> x34, waiting for transfers between devices: 173 us -> 88.2 us  [the longest x30 78.4 us: pass_on(): lax.ppermute(values, 'hx', pairs)]
    dot_general x42 -> x2, matrix products: 53.6 us -> 4.17 us  [dot32(): return jnp.dot(left, right, preferred_element_type=F32)]
    ppermute x35 -> x16, waiting for transfers between devices: 54.8 us -> 20 us  [swap(): return lax.ppermute(value, axis, [(i, i ^ offset) for i in range(count)])]
    unnamed x61 -> x125, local copies, waits for them, and re-layouts: 3.24 us -> 28.4 us
    convert_element_type x12 -> x8, other arithmetic: 24 us -> 8.03 us  [the longest x4 3.41 us: line_scatter(): odd_out = (odd_out.astype(F32) + even_in.astype(F32)).astype(BF16)]
    all_to_all x1 -> x0, blocking collectives: 13.5 us -> none  [body(): taken = lax.all_to_all(sent, 'ctx', split_axis=0, concat_axis=0, tiled=True)]
    ppermute x39 -> x34, starting transfers between devices: 90.7 us -> 79.7 us  [the longest x30 71.8 us: pass_on(): lax.ppermute(values, 'hx', pairs)]
  transfers between devices with their start and end apart: 77 -> 54, of which waited for: 40 -> 32; matrix products, arithmetic and copies ran while one was open for 15% -> 7% of each run, Pallas kernels for 1% -> 22%
where the time goes in v2:
time: 452 us; the launch traced here: 444 us
  waiting for transfers between devices  129 us (29%)
  starting transfers between devices  124 us (27%)
  Pallas kernels  117 us (26%)
  local copies, waits for them, and re-layouts  50 us (11%)
  other arithmetic  13.8 us (3%)
  matrix products  9.14 us (2%)
    ppermute x30, waiting for transfers between devices, pass_on(): lax.ppermute(values, 'hx', pairs)  78.4 us
    ppermute x30, starting transfers between devices, pass_on(): lax.ppermute(values, 'hx', pairs)  71.8 us
    pallas_call x6, Pallas kernels, expert_share(): pl.pallas_call(functools.partial(share_kernel, shares=len(shares), added=...  32.8 us
    unnamed x125, local copies, waits for them, and re-layouts  28.4 us
    pallas_call x2, Pallas kernels, expert_finish(): pl.pallas_call(functools.partial(finish_kernel, shares=len(shares), tiles...  26.9 us
    pallas_call x4, Pallas kernels, project(): pl.pallas_call(functools.partial(project_kernel, count=len(values), mats=...  22.2 us
    all_to_all x2, starting transfers between devices, body(): taken = lax.all_to_all(sent, 'ctx', split_axis=0, concat_axis=0, tiled=True)  21.7 us
    ppermute x16, waiting for transfers between devices, swap(): return lax.ppermute(value, axis, [(i, i ^ offset) for i in range(count)])  20 us
  transfers between devices with their start and end apart: 54, of which 32 were waited for; matrix products, arithmetic and copies ran while one was open for 7% of the time, Pallas kernels for 22%

profile of v2, /device:TPU:16, one launch (start us, length us, event | category | flops | bytes accessed | tf_op | source)
XLA Modules:
  0.0 443.9 jit_solution(10743672341831398341)
XLA Ops:
  5.2 3.9 fusion.32
  13.9 5.1 %norm_rows.2.refs_0_.refs_1_.refs_2_ = bf16[512,5120]{1,0:T(8,128)(2,1)S(1)} custom-call(bf16[512,5120]{1,0:T(8,128)(2,1)} %values_ref.1, bf16[1,5120]{1,0:T(2,128)(2,1)S(1)} %reshape.82.gains_ref), custom_call_target="tpu_custom_call" | custom-call | bytes 4096 | tf_op jit(solution)/shard_map/norm_rows/pallas_call | solution.py:135
  22.7 4.8 %collective-permute-done.3.refs_7_ = bf16[1280,256]{1,0:T(8,128)(2,1)S(1)} collective-permute-done((bf16[1280,256]{1,0:T(8,128)(2,1)S(1)}, bf16[1280,256]{1,0:T(8,128)(2,1)S(1)}, u32[]{:S(2)}, u32[]{:S(2)}) %collective-permute-start.3) | collective-permute-done | bytes 655392 | tf_op jit(solution)/shard_map/ppermute | solution.py:31
  28.9 4.4 collective-permute-done.5.refs_8_
  40.5 5.0 %norm_rows.3.refs_3_.refs_4_.refs_5_.refs_2_ = bf16[512,5120]{1,0:T(8,128)(2,1)S(1)} custom-call(bf16[512,5120]{1,0:T(8,128)(2,1)} %collective-permute-done.2.values_ref, bf16[1,5120]{1,0:T(2,128)(2,1)S(1)} %reshape.82.gains_ref), custom_call_target="tpu_custom_call" | custom-call | bytes 4096 | tf_op jit(solution)/shard_map/norm_rows/pallas_call | solution.py:135
  47.8 6.3 %project.4 = (f32[512,256]{1,0:T(8,128)S(1)}, f32[512,256]{1,0:T(8,128)S(1)}) custom-call(s32[3]{0:T(128)S(1)} %pad_add_fusion.1.places_ref, bf16[512,5120]{1,0:T(8,128)(2,1)} %copy-done.2, bf16[512,5120]{1,0:T(8,128)(2,1)} %copy-done.2, bf16[512,5120]{1,0:T(8,128)(2,1)} %copy-done.2, bf16[512,5120]{1,0:T(8,128)(2,1)} %copy-done.3, ...), custom_call_target="tpu_custom_call" | custom-call | bytes 4096 | tf_op jit(solution)/shard_map/project/pallas_call | solution.py:229
  58.3 5.2 %collective-permute-done.6.refs_4_ = bf16[640,256]{1,0:T(8,128)(2,1)} collective-permute-done((bf16[640,256]{1,0:T(8,128)(2,1)}, bf16[640,256]{1,0:T(8,128)(2,1)}, u32[]{:S(2)}, u32[]{:S(2)}) %collective-permute-start.6) | collective-permute-done | bytes 327712 | tf_op jit(solution)/shard_map/ppermute | solution.py:31
  64.8 3.4 project.5
  76.8 8.6 %project.6 = (f32[512,384]{1,0:T(8,128)S(1)}, f32[512,384]{1,0:T(8,128)S(1)}) custom-call(s32[3]{0:T(128)S(1)} %pad_add_fusion.1.places_ref, bf16[512,5120]{1,0:T(8,128)(2,1)} %copy-done.2, bf16[512,5120]{1,0:T(8,128)(2,1)} %copy-done.2, bf16[512,5120]{1,0:T(8,128)(2,1)} %copy-done.2, bf16[512,5120]{1,0:T(8,128)(2,1)} %copy-done.3, ...), custom_call_target="tpu_custom_call" | custom-call | bytes 4096 | tf_op jit(solution)/shard_map/project/pallas_call | solution.py:229
  87.2 3.8 collective-permute-done.13.refs_4_
  98.9 3.4 collective-permute-start.18
  104.4 3.9 project.7
  108.4 3.3 attend.3.refs_0_
  115.3 5.4 %attend.2.refs_0_ = bf16[512,384]{1,0:T(8,128)(2,1)S(1)} custom-call(s32[9]{0:T(128)S(1)} %stack.83.places_ref, bf16[512,384]{1,0:T(8,128)(2,1)S(1)} %get-tuple-element.145.query_ref, bf16[1024,256]{1,0:T(8,128)(2,1)S(1)} %copy-done.49, bf16[1024,256]{1,0:T(8,128)(2,1)S(1)} %copy-done.45, bf16[1024,256]{1,0:T(8,128)(2,1)S(1)} %copy-done.47, ...), custom_call_target="tpu_custom_call" | custom-call | flops 3221225472 | bytes 2097152 | tf_op jit(solution)/shard_map/attend/pallas_call | solution.py:312
  125.5 3.5 collective-permute-start.20
  136.4 3.4 collective-permute-start.27
  140.8 3.3 collective-permute-start.21
  144.8 3.4 collective-permute-start.22
  149.8 4.2 collective-permute-start.28
  157.7 4.0 collective-permute-start.23
  165.1 8.4 %collective-permute-done.23.refs_5_.refs_6_ = bf16[512,384]{1,0:T(8,128)(2,1)S(1)} collective-permute-done((bf16[512,384]{1,0:T(8,128)(2,1)}, bf16[512,384]{1,0:T(8,128)(2,1)S(1)}, u32[]{:S(2)}, u32[]{:S(2)}) %collective-permute-start.23) | collective-permute-done | bytes 393248 | tf_op jit(solution)/shard_map/ppermute | solution.py:64
  173.5 7.5 %sum_dots.2 = bf16[512,1280]{1,0:T(8,128)(2,1)} custom-call(s32[4]{0:T(128)S(1)} %fusion.27.codes_ref, bf16[512,384]{1,0:T(8,128)(2,1)S(1)} %copy-done.23, bf16[512,384]{1,0:T(8,128)(2,1)S(1)} %copy-done.25, bf16[512,384]{1,0:T(8,128)(2,1)S(1)} %copy-done.27, bf16[512,384]{1,0:T(8,128)(2,1)S(1)} %copy-done.29, ...), custom_call_target="tpu_custom_call" | custom-call | bytes 4096 | tf_op jit(solution)/shard_map/sum_dots/pallas_call | solution.py:187
  185.3 8.4 %sum_dots.3 = bf16[512,1280]{1,0:T(8,128)(2,1)} custom-call(s32[4]{0:T(128)S(1)} %fusion.27.codes_ref, bf16[512,384]{1,0:T(8,128)(2,1)S(1)} %copy-done.31, bf16[512,384]{1,0:T(8,128)(2,1)S(1)} %copy-done.33, bf16[512,384]{1,0:T(8,128)(2,1)S(1)} %copy-done.35, bf16[512,384]{1,0:T(8,128)(2,1)S(1)} %copy-done.37, ...), custom_call_target="tpu_custom_call" | custom-call | bytes 4096 | tf_op jit(solution)/shard_map/sum_dots/pallas_call | solution.py:187
  196.4 13.8 %all-to-all-start = ((bf16[8,1,32,1280]{3,2,1,0:T(8,128)(2,1)}), bf16[8,1,32,1280]{3,2,1,0:T(8,128)(2,1)S(1)}, u32[]{:S(2)}, u32[]{:S(2)}) async-start(bf16[8,1,32,1280]{3,2,1,0:T(8,128)(2,1)} %bitcast.21), calls=%async_computation | async-start | bytes 1310720 | tf_op jit(solution)/shard_map/all_to_all | solution.py:689
  210.2 11.1 %all-to-all-done = bf16[8,1,32,1280]{3,2,1,0:T(8,128)(2,1)S(1)} async-done(((bf16[8,1,32,1280]{3,2,1,0:T(8,128)(2,1)}), bf16[8,1,32,1280]{3,2,1,0:T(8,128)(2,1)S(1)}, u32[]{:S(2)}, u32[]{:S(2)}) %all-to-all-start) | async-done | bytes 655392 | tf_op jit(solution)/shard_map/all_to_all | solution.py:689
  223.7 3.3 collective-permute-start.31
  227.1 5.3 %expert_share.6 = (f32[256,1024]{1,0:T(8,128)S(1)}, f32[256,1024]{1,0:T(8,128)S(1)}, f32[256,128]{1,0:T(8,128)S(1)}, f32[256,128]{1,0:T(8,128)S(1)}) custom-call(s32[3]{0:T(128)S(1)} %add_add_fusion.code_ref, bf16[256,1280]{1,0:T(8,128)(2,1)S(1)} %bitcast.83, bf16[1,5120]{1,0:T(2,128)(2,1)S(1)} %reshape.85.refs_1_.refs_2_.refs_4_.refs_6_, ...), custom_call_target="tpu_custom_call" | custom-call | bytes 4096 | tf_op jit(solution)/shard_map/expert_share/pallas_call | solution.py:369
  235.7 3.3 collective-permute-done.31.refs_1_
  240.3 3.3 collective-permute-start.33
  245.1 5.4 %expert_share.7 = (f32[256,1024]{1,0:T(8,128)S(1)}, f32[256,1024]{1,0:T(8,128)S(1)}, f32[256,128]{1,0:T(8,128)S(1)}, f32[256,128]{1,0:T(8,128)S(1)}) custom-call(s32[3]{0:T(128)S(1)} %get-tuple-element.252.code_ref, bf16[256,1280]{1,0:T(8,128)(2,1)S(1)} %collective-permute-done.30.refs_0_, bf16[256,1280]{1,0:T(8,128)(2,1)S(1)} %collective-permute-done.31.refs_1_, ...), custom_call_target="tpu_custom_call" | custom-call | bytes 4096 | tf_op jit(solution)/shard_map/expert_share/pallas_call | solution.py:369
  258.3 7.9 %all-to-all-start.1 = ((bf16[8,1,32,1280]{3,2,1,0:T(8,128)(2,1)}), bf16[8,1,32,1280]{3,2,1,0:T(8,128)(2,1)S(1)}, u32[]{:S(2)}, u32[]{:S(2)}) async-start(bf16[8,1,32,1280]{3,2,1,0:T(8,128)(2,1)} %bitcast.87), calls=%async_computation.1 | async-start | bytes 1310720 | tf_op jit(solution)/shard_map/all_to_all | solution.py:689
  267.9 5.7 %expert_share.8 = (f32[256,1024]{1,0:T(8,128)S(1)}, f32[256,1024]{1,0:T(8,128)S(1)}, f32[256,128]{1,0:T(8,128)S(1)}, f32[256,128]{1,0:T(8,128)S(1)}) custom-call(s32[3]{0:T(128)S(1)} %pad_add_fusion.4.code_ref, bf16[256,1280]{1,0:T(8,128)(2,1)S(1)} %collective-permute-done.30.refs_0_, bf16[256,1280]{1,0:T(8,128)(2,1)S(1)} %collective-permute-done.31.refs_1_, ...), custom_call_target="tpu_custom_call" | custom-call | bytes 4096 | tf_op jit(solution)/shard_map/expert_share/pallas_call | solution.py:369
  277.4 3.5 collective-permute-start.41
  285.2 13.9 %expert_finish.2 = bf16[4,256,1280]{2,1,0:T(8,128)(2,1)} custom-call(s32[3]{0:T(128)S(1)} %get-tuple-element.251.code_ref, bf16[256,1280]{1,0:T(8,128)(2,1)S(1)} %collective-permute-done.30.refs_0_, bf16[256,1280]{1,0:T(8,128)(2,1)S(1)} %collective-permute-done.31.refs_1_, bf16[256,1280]{1,0:T(8,128)(2,1)S(1)} %collective-permute-done.32.refs_2_, ...), custom_call_target="tpu_custom_call" | custom-call | bytes 4096 | tf_op jit(solution)/shard_map/expert_finish/pallas_call | solution.py:433
  302.2 5.3 %expert_share.9 = (f32[256,1024]{1,0:T(8,128)S(1)}, f32[256,1024]{1,0:T(8,128)S(1)}, f32[256,128]{1,0:T(8,128)S(1)}, f32[256,128]{1,0:T(8,128)S(1)}) custom-call(s32[3]{0:T(128)S(1)} %add_add_fusion.code_ref, bf16[256,1280]{1,0:T(8,128)(2,1)S(1)} %bitcast.80, bf16[1,5120]{1,0:T(2,128)(2,1)S(1)} %reshape.85.refs_1_.refs_2_.refs_4_.refs_6_, ...), custom_call_target="tpu_custom_call" | custom-call | bytes 4096 | tf_op jit(solution)/shard_map/expert_share/pallas_call | solution.py:369
  307.5 4.6 %collective-permute-start.42 = (bf16[256,1280]{1,0:T(8,128)(2,1)S(1)}, bf16[256,1280]{1,0:T(8,128)(2,1)S(1)}, u32[]{:S(2)}, u32[]{:S(2)}) collective-permute-start(bf16[256,1280]{1,0:T(8,128)(2,1)S(1)} %collective-permute-done.41.refs_1_), channel_id=1, source_target_pairs={{1,0},{2,3},{5,4},{6,7},{9,8},{10,11},{13,12},{14,15},{17,16},{18,... | collective-permute-start | bytes 1966088 | tf_op jit(solution)/shard_map/ppermute | solution.py:64
  314.5 4.7 %collective-permute-done.35 = bf16[256,1280]{1,0:T(8,128)(2,1)S(1)} collective-permute-done((bf16[256,1280]{1,0:T(8,128)(2,1)S(1)}, bf16[256,1280]{1,0:T(8,128)(2,1)S(1)}, u32[]{:S(2)}, u32[]{:S(2)}) %collective-permute-start.35) | collective-permute-done | bytes 655392 | tf_op jit(solution)/shard_map/ppermute | solution.py:64
  323.0 5.4 %expert_share.10 = (f32[256,1024]{1,0:T(8,128)S(1)}, f32[256,1024]{1,0:T(8,128)S(1)}, f32[256,128]{1,0:T(8,128)S(1)}, f32[256,128]{1,0:T(8,128)S(1)}) custom-call(s32[3]{0:T(128)S(1)} %get-tuple-element.252.code_ref, bf16[256,1280]{1,0:T(8,128)(2,1)S(1)} %collective-permute-done.40.refs_0_, bf16[256,1280]{1,0:T(8,128)(2,1)S(1)} %collective-permute-done.41.refs_1_, ...), custom_call_target="tpu_custom_call" | custom-call | bytes 4096 | tf_op jit(solution)/shard_map/expert_share/pallas_call | solution.py:369
  333.1 10.8 %collective-permute-done.36 = bf16[256,1280]{1,0:T(8,128)(2,1)S(1)} collective-permute-done((bf16[256,1280]{1,0:T(8,128)(2,1)S(1)}, bf16[256,1280]{1,0:T(8,128)(2,1)S(1)}, u32[]{:S(2)}, u32[]{:S(2)}) %collective-permute-start.36) | collective-permute-done | bytes 655392 | tf_op jit(solution)/shard_map/ppermute | solution.py:64
  346.8 5.8 %expert_share.11 = (f32[256,1024]{1,0:T(8,128)S(1)}, f32[256,1024]{1,0:T(8,128)S(1)}, f32[256,128]{1,0:T(8,128)S(1)}, f32[256,128]{1,0:T(8,128)S(1)}) custom-call(s32[3]{0:T(128)S(1)} %pad_add_fusion.4.code_ref, bf16[256,1280]{1,0:T(8,128)(2,1)S(1)} %collective-permute-done.40.refs_0_, bf16[256,1280]{1,0:T(8,128)(2,1)S(1)} %collective-permute-done.41.refs_1_, ...), custom_call_target="tpu_custom_call" | custom-call | bytes 4096 | tf_op jit(solution)/shard_map/expert_share/pallas_call | solution.py:369
  352.5 13.1 %expert_finish.3 = bf16[4,256,1280]{2,1,0:T(8,128)(2,1)} custom-call(s32[3]{0:T(128)S(1)} %get-tuple-element.251.code_ref, bf16[256,1280]{1,0:T(8,128)(2,1)S(1)} %collective-permute-done.40.refs_0_, bf16[256,1280]{1,0:T(8,128)(2,1)S(1)} %collective-permute-done.41.refs_1_, bf16[256,1280]{1,0:T(8,128)(2,1)S(1)} %collective-permute-done.42.refs_2_, ...), custom_call_target="tpu_custom_call" | custom-call | bytes 4096 | tf_op jit(solution)/shard_map/expert_finish/pallas_call | solution.py:433
  370.7 15.2 %collective-permute-done.45 = bf16[256,1280]{1,0:T(8,128)(2,1)S(1)} collective-permute-done((bf16[256,1280]{1,0:T(8,128)(2,1)S(1)}, bf16[256,1280]{1,0:T(8,128)(2,1)S(1)}, u32[]{:S(2)}, u32[]{:S(2)}) %collective-permute-start.45) | collective-permute-done | bytes 655392 | tf_op jit(solution)/shard_map/ppermute | solution.py:64
  386.9 3.5 collective-permute-start.46
  391.7 4.0 all-to-all-start.2
  395.6 7.2 %collective-permute-done.46 = bf16[256,1280]{1,0:T(8,128)(2,1)} collective-permute-done((bf16[256,1280]{1,0:T(8,128)(2,1)}, bf16[256,1280]{1,0:T(8,128)(2,1)}, u32[]{:S(2)}, u32[]{:S(2)}) %collective-permute-start.46) | collective-permute-done | bytes 655392 | tf_op jit(solution)/shard_map/ppermute | solution.py:64
  411.0 11.7 %collective-permute-done.49 = bf16[256,1280]{1,0:T(8,128)(2,1)S(1)} collective-permute-done((bf16[256,1280]{1,0:T(8,128)(2,1)}, bf16[256,1280]{1,0:T(8,128)(2,1)S(1)}, u32[]{:S(2)}, u32[]{:S(2)}) %collective-permute-start.49) | collective-permute-done | bytes 655392 | tf_op jit(solution)/shard_map/ppermute | solution.py:64
  424.4 4.7 %all-to-all-start.3 = ((bf16[8,1,32,1280]{3,2,1,0:T(8,128)(2,1)}), bf16[8,1,32,1280]{3,2,1,0:T(8,128)(2,1)S(1)}, u32[]{:S(2)}, u32[]{:S(2)}) async-start(bf16[8,1,32,1280]{3,2,1,0:T(8,128)(2,1)} %bitcast.85), calls=%async_computation.3 | async-start | bytes 1310720 | tf_op jit(solution)/shard_map/all_to_all | solution.py:681
  431.0 9.3 %all-to-all-done.3 = bf16[8,1,32,1280]{3,2,1,0:T(8,128)(2,1)S(1)} async-done(((bf16[8,1,32,1280]{3,2,1,0:T(8,128)(2,1)}), bf16[8,1,32,1280]{3,2,1,0:T(8,128)(2,1)S(1)}, u32[]{:S(2)}, u32[]{:S(2)}) %all-to-all-start.3) | async-done | bytes 655392 | tf_op jit(solution)/shard_map/all_to_all | solution.py:681
  (258 shorter events, 148.3 us)
Async XLA Ops:
  5.0 28.2 %collective-permute-start.2 = (bf16[512,5120]{1,0:T(8,128)(2,1)}, bf16[512,5120]{1,0:T(8,128)(2,1)}, u32[]{:S(2)}, u32[]{:S(2)}) collective-permute-start(bf16[512,5120]{1,0:T(8,128)(2,1)} %values_ref.1), channel_id=1, source_target_pairs={{0,4},{4,0},{8,12},{12,8},{16,20},{20,16},{24,28},{28,24},{1,5},{5... | collective-permute-start | bytes 15728648 | tf_op jit(solution)/shard_map/ppermute | solution.py:31
  9.0 24.2 %collective-permute-start.5 = (bf16[384,1280]{1,0:T(8,128)(2,1)}, bf16[384,1280]{1,0:T(8,128)(2,1)S(1)}, u32[]{:S(2)}, u32[]{:S(2)}) collective-permute-start(bf16[384,1280]{1,0:T(8,128)(2,1)} %get-tuple-element.236), channel_id=1, source_target_pairs={{0,1},{1,2},{2,3},{3,0},{4,5},{5,6},{6,7},{7,4},{8,9},{9,10},{10,1... | collective-permute-start | bytes 2949128 | tf_op jit(solution)/shard_map/ppermute | solution.py:49
  10.8 16.7 %collective-permute-start.3 = (bf16[1280,256]{1,0:T(8,128)(2,1)S(1)}, bf16[1280,256]{1,0:T(8,128)(2,1)S(1)}, u32[]{:S(2)}, u32[]{:S(2)}) collective-permute-start(bf16[1280,256]{1,0:T(8,128)(2,1)S(1)} %pad_maximum_fusion.1.refs_6_), channel_id=1, source_target_pairs={{0,8},{4,12},{8,0},{12,4},{16,24},{20,28},{24,16},{28,20},{1,9},{5... | collective-permute-start | bytes 1966088 | tf_op jit(solution)/shard_map/ppermute | solution.py:31
  12.4 16.5 %collective-permute-start.4 = (bf16[1280,256]{1,0:T(8,128)(2,1)S(1)}, bf16[1280,256]{1,0:T(8,128)(2,1)}, u32[]{:S(2)}, u32[]{:S(2)}) collective-permute-start(bf16[1280,256]{1,0:T(8,128)(2,1)S(1)} %pad_maximum_fusion.1.refs_6_), channel_id=1, source_target_pairs={{0,16},{4,20},{8,24},{12,28},{16,0},{20,4},{24,8},{28,12},{1,17},{... | collective-permute-start | bytes 1966088 | tf_op jit(solution)/shard_map/ppermute | solution.py:31
  33.2 31.5 %collective-permute-start.8 = (bf16[1280,384]{1,0:T(8,128)(2,1)S(1)}, bf16[1280,384]{1,0:T(8,128)(2,1)}, u32[]{:S(2)}, u32[]{:S(2)}) collective-permute-start(bf16[1280,384]{1,0:T(8,128)(2,1)S(1)} %pad_maximum_fusion.refs_6_), channel_id=1, source_target_pairs={{0,8},{4,12},{8,0},{12,4},{16,24},{20,28},{24,16},{28,20},{1,9},{5... | collective-permute-start | bytes 2949128 | tf_op jit(solution)/shard_map/ppermute | solution.py:31
  34.7 30.0 %collective-permute-start.9 = (bf16[1280,384]{1,0:T(8,128)(2,1)S(1)}, bf16[1280,384]{1,0:T(8,128)(2,1)}, u32[]{:S(2)}, u32[]{:S(2)}) collective-permute-start(bf16[1280,384]{1,0:T(8,128)(2,1)S(1)} %pad_maximum_fusion.refs_6_), channel_id=1, source_target_pairs={{0,16},{4,20},{8,24},{12,28},{16,0},{20,4},{24,8},{28,12},{1,17},{... | collective-permute-start | bytes 2949128 | tf_op jit(solution)/shard_map/ppermute | solution.py:31
  36.2 28.5 %collective-permute-start.10 = (bf16[384,1280]{1,0:T(8,128)(2,1)}, bf16[384,1280]{1,0:T(8,128)(2,1)}, u32[]{:S(2)}, u32[]{:S(2)}) collective-permute-start(bf16[384,1280]{1,0:T(8,128)(2,1)} %get-tuple-element.128), channel_id=1, source_target_pairs={{0,3},{1,0},{2,1},{3,2},{4,7},{5,4},{6,5},{7,6},{8,11},{9,8},{10,9... | collective-permute-start | bytes 2949128 | tf_op jit(solution)/shard_map/ppermute | solution.py:49
  39.4 24.1 %collective-permute-start.6 = (bf16[640,256]{1,0:T(8,128)(2,1)}, bf16[640,256]{1,0:T(8,128)(2,1)}, u32[]{:S(2)}, u32[]{:S(2)}) collective-permute-start(bf16[640,256]{1,0:T(8,128)(2,1)} %slice.54), channel_id=1, source_target_pairs={{0,8},{4,12},{8,0},{12,4},{16,24},{20,28},{24,16},{28,20},{1,9},{5... | collective-permute-start | bytes 983048 | tf_op jit(solution)/shard_map/ppermute | solution.py:31
  39.9 24.8 %collective-permute-start.7 = (bf16[640,256]{1,0:T(8,128)(2,1)}, bf16[640,256]{1,0:T(8,128)(2,1)}, u32[]{:S(2)}, u32[]{:S(2)}) collective-permute-start(bf16[640,256]{1,0:T(8,128)(2,1)} %slice.55), channel_id=1, source_target_pairs={{0,16},{4,20},{8,24},{12,28},{16,0},{20,4},{24,8},{28,12},{1,17},{... | collective-permute-start | bytes 983048 | tf_op jit(solution)/shard_map/ppermute | solution.py:31
  68.2 26.1 %collective-permute-start.11 = (bf16[1024,256]{1,0:T(8,128)(2,1)S(1)}, bf16[1024,256]{1,0:T(8,128)(2,1)S(1)}, u32[]{:S(2)}, u32[]{:S(2)}) collective-permute-start(bf16[1024,256]{1,0:T(8,128)(2,1)S(1)} %constant_dynamic-update-slice_fusion.refs_0_), channel_id=1, source_target_pairs={{0,8},{4,12},{8,0},{12,4},{16,24},{20,28},{24,16},{28,20},{1,9},{5... | collective-permute-start | bytes 1572872 | tf_op jit(solution)/shard_map/ppermute | solution.py:31
  68.8 25.5 %collective-permute-start.12 = (bf16[1024,256]{1,0:T(8,128)(2,1)S(1)}, bf16[1024,256]{1,0:T(8,128)(2,1)S(1)}, u32[]{:S(2)}, u32[]{:S(2)}) collective-permute-start(bf16[1024,256]{1,0:T(8,128)(2,1)S(1)} %constant_dynamic-update-slice_fusion.refs_0_), channel_id=1, source_target_pairs={{0,16},{4,20},{8,24},{12,28},{16,0},{20,4},{24,8},{28,12},{1,17},{... | collective-permute-start | bytes 1572872 | tf_op jit(solution)/shard_map/ppermute | solution.py:31
  72.5 18.4 %collective-permute-start.13 = (bf16[640,384]{1,0:T(8,128)(2,1)S(1)}, bf16[640,384]{1,0:T(8,128)(2,1)S(1)}, u32[]{:S(2)}, u32[]{:S(2)}) collective-permute-start(bf16[640,384]{1,0:T(8,128)(2,1)S(1)} %slice.56), channel_id=1, source_target_pairs={{0,8},{4,12},{8,0},{12,4},{16,24},{20,28},{24,16},{28,20},{1,9},{5... | collective-permute-start | bytes 1474568 | tf_op jit(solution)/shard_map/ppermute | solution.py:31
  74.1 17.2 %collective-permute-start.14 = (bf16[640,384]{1,0:T(8,128)(2,1)S(1)}, bf16[640,384]{1,0:T(8,128)(2,1)S(1)}, u32[]{:S(2)}, u32[]{:S(2)}) collective-permute-start(bf16[640,384]{1,0:T(8,128)(2,1)S(1)} %slice.57), channel_id=1, source_target_pairs={{0,16},{4,20},{8,24},{12,28},{16,0},{20,4},{24,8},{28,12},{1,17},{... | collective-permute-start | bytes 1474568 | tf_op jit(solution)/shard_map/ppermute | solution.py:31
  74.6 19.7 %collective-permute-start.15 = (bf16[192,1280]{1,0:T(8,128)(2,1)S(1)}, bf16[192,1280]{1,0:T(8,128)(2,1)S(1)}, u32[]{:S(2)}, u32[]{:S(2)}) collective-permute-start(bf16[192,1280]{1,0:T(8,128)(2,1)S(1)} %get-tuple-element.140), channel_id=1, source_target_pairs={{0,2},{1,3},{2,0},{3,1},{4,6},{5,7},{6,4},{7,5},{8,10},{9,11},{10,... | collective-permute-start | bytes 1474568 | tf_op jit(solution)/shard_map/ppermute | solution.py:49
  95.1 13.3 %collective-permute-start.16 = (bf16[512,256]{1,0:T(8,128)(2,1)}, bf16[512,256]{1,0:T(8,128)(2,1)}, u32[]{:S(2)}, u32[]{:S(2)}) collective-permute-start(bf16[512,256]{1,0:T(8,128)(2,1)} %slice.58), channel_id=1, source_target_pairs={{0,8},{4,12},{8,0},{12,4},{16,24},{20,28},{24,16},{28,20},{1,9},{5... | collective-permute-start | bytes 786440 | tf_op jit(solution)/shard_map/ppermute | solution.py:31
  98.9 24.3 %collective-permute-start.18 = (bf16[192,1280]{1,0:T(8,128)(2,1)}, bf16[192,1280]{1,0:T(8,128)(2,1)S(1)}, u32[]{:S(2)}, u32[]{:S(2)}) collective-permute-start(bf16[192,1280]{1,0:T(8,128)(2,1)} %get-tuple-element.148), channel_id=1, source_target_pairs={{0,2},{1,3},{2,0},{3,1},{4,6},{5,7},{6,4},{7,5},{8,10},{9,11},{10,... | collective-permute-start | bytes 1474568 | tf_op jit(solution)/shard_map/ppermute | solution.py:49
  111.7 19.6 %collective-permute-start.24 = (bf16[512,384]{1,0:T(8,128)(2,1)S(1)}, bf16[512,384]{1,0:T(8,128)(2,1)S(1)}, u32[]{:S(2)}, u32[]{:S(2)}) collective-permute-start(bf16[512,384]{1,0:T(8,128)(2,1)S(1)} %attend.3.refs_0_), channel_id=1, source_target_pairs={{0,1},{1,0},{2,3},{3,2},{4,5},{5,4},{6,7},{7,6},{8,9},{9,8},{10,11... | collective-permute-start | bytes 1179656 | tf_op jit(solution)/shard_map/ppermute | solution.py:64
  112.4 20.0 %collective-permute-start.25 = (bf16[512,384]{1,0:T(8,128)(2,1)S(1)}, bf16[512,384]{1,0:T(8,128)(2,1)S(1)}, u32[]{:S(2)}, u32[]{:S(2)}) collective-permute-start(bf16[512,384]{1,0:T(8,128)(2,1)S(1)} %attend.3.refs_0_), channel_id=1, source_target_pairs={{1,2},{2,1},{5,6},{6,5},{9,10},{10,9},{13,14},{14,13},{17,18},{18,... | collective-permute-start | bytes 1179656 | tf_op jit(solution)/shard_map/ppermute | solution.py:64
  123.2 17.5 %collective-permute-start.19 = (bf16[512,384]{1,0:T(8,128)(2,1)S(1)}, bf16[512,384]{1,0:T(8,128)(2,1)S(1)}, u32[]{:S(2)}, u32[]{:S(2)}) collective-permute-start(bf16[512,384]{1,0:T(8,128)(2,1)S(1)} %attend.2.refs_0_), channel_id=1, source_target_pairs={{0,1},{1,0},{2,3},{3,2},{4,5},{5,4},{6,7},{7,6},{8,9},{9,8},{10,11... | collective-permute-start | bytes 1179656 | tf_op jit(solution)/shard_map/ppermute | solution.py:64
  125.5 15.3 %collective-permute-start.20 = (bf16[512,384]{1,0:T(8,128)(2,1)S(1)}, bf16[512,384]{1,0:T(8,128)(2,1)S(1)}, u32[]{:S(2)}, u32[]{:S(2)}) collective-permute-start(bf16[512,384]{1,0:T(8,128)(2,1)S(1)} %attend.2.refs_0_), channel_id=1, source_target_pairs={{1,2},{2,1},{5,6},{6,5},{9,10},{10,9},{13,14},{14,13},{17,18},{18,... | collective-permute-start | bytes 1179656 | tf_op jit(solution)/shard_map/ppermute | solution.py:64
  132.4 16.6 %collective-permute-start.26 = (bf16[512,384]{1,0:T(8,128)(2,1)S(1)}, bf16[512,384]{1,0:T(8,128)(2,1)S(1)}, u32[]{:S(2)}, u32[]{:S(2)}) collective-permute-start(bf16[512,384]{1,0:T(8,128)(2,1)S(1)} %collective-permute-done.25.refs_2_), channel_id=1, source_target_pairs={{1,0},{2,3},{5,4},{6,7},{9,8},{10,11},{13,12},{14,15},{17,16},{18,... | collective-permute-start | bytes 1179656 | tf_op jit(solution)/shard_map/ppermute | solution.py:64
  136.4 13.4 %collective-permute-start.27 = (bf16[512,384]{1,0:T(8,128)(2,1)S(1)}, bf16[512,384]{1,0:T(8,128)(2,1)}, u32[]{:S(2)}, u32[]{:S(2)}) collective-permute-start(bf16[512,384]{1,0:T(8,128)(2,1)S(1)} %collective-permute-done.24.refs_1_), channel_id=1, source_target_pairs={{1,2},{2,1},{5,6},{6,5},{9,10},{10,9},{13,14},{14,13},{17,18},{18,... | collective-permute-start | bytes 1179656 | tf_op jit(solution)/shard_map/ppermute | solution.py:64
  140.8 15.8 %collective-permute-start.21 = (bf16[512,384]{1,0:T(8,128)(2,1)S(1)}, bf16[512,384]{1,0:T(8,128)(2,1)S(1)}, u32[]{:S(2)}, u32[]{:S(2)}) collective-permute-start(bf16[512,384]{1,0:T(8,128)(2,1)S(1)} %collective-permute-done.20.refs_2_), channel_id=1, source_target_pairs={{1,0},{2,3},{5,4},{6,7},{9,8},{10,11},{13,12},{14,15},{17,16},{18,... | collective-permute-start | bytes 1179656 | tf_op jit(solution)/shard_map/ppermute | solution.py:64
  149.8 15.3 %collective-permute-start.28 = (bf16[512,384]{1,0:T(8,128)(2,1)}, bf16[512,384]{1,0:T(8,128)(2,1)}, u32[]{:S(2)}, u32[]{:S(2)}) collective-permute-start(bf16[512,384]{1,0:T(8,128)(2,1)} %collective-permute-done.27.refs_4_), channel_id=1, source_target_pairs={{1,0},{2,3},{5,4},{6,7},{9,8},{10,11},{13,12},{14,15},{17,16},{18,... | collective-permute-start | bytes 1179656 | tf_op jit(solution)/shard_map/ppermute | solution.py:64
  157.7 15.8 %collective-permute-start.23 = (bf16[512,384]{1,0:T(8,128)(2,1)}, bf16[512,384]{1,0:T(8,128)(2,1)S(1)}, u32[]{:S(2)}, u32[]{:S(2)}) collective-permute-start(bf16[512,384]{1,0:T(8,128)(2,1)} %collective-permute-done.22.refs_4_), channel_id=1, source_target_pairs={{1,0},{2,3},{5,4},{6,7},{9,8},{10,11},{13,12},{14,15},{17,16},{18,... | collective-permute-start | bytes 1179656 | tf_op jit(solution)/shard_map/ppermute | solution.py:64
  196.4 24.9 %all-to-all-start = ((bf16[8,1,32,1280]{3,2,1,0:T(8,128)(2,1)}), bf16[8,1,32,1280]{3,2,1,0:T(8,128)(2,1)S(1)}, u32[]{:S(2)}, u32[]{:S(2)}) async-start(bf16[8,1,32,1280]{3,2,1,0:T(8,128)(2,1)} %bitcast.21), calls=%async_computation | async-start | bytes 1310720 | tf_op jit(solution)/shard_map/all_to_all | solution.py:689
  221.3 14.3 %collective-permute-start.30 = (bf16[256,1280]{1,0:T(8,128)(2,1)S(1)}, bf16[256,1280]{1,0:T(8,128)(2,1)S(1)}, u32[]{:S(2)}, u32[]{:S(2)}) collective-permute-start(bf16[256,1280]{1,0:T(8,128)(2,1)S(1)} %bitcast.81), channel_id=1, source_target_pairs={{0,1},{1,0},{2,3},{3,2},{4,5},{5,4},{6,7},{7,6},{8,9},{9,8},{10,11... | collective-permute-start | bytes 1966088 | tf_op jit(solution)/shard_map/ppermute | solution.py:64
  223.7 15.3 %collective-permute-start.31 = (bf16[256,1280]{1,0:T(8,128)(2,1)S(1)}, bf16[256,1280]{1,0:T(8,128)(2,1)S(1)}, u32[]{:S(2)}, u32[]{:S(2)}) collective-permute-start(bf16[256,1280]{1,0:T(8,128)(2,1)S(1)} %bitcast.82), channel_id=1, source_target_pairs={{1,2},{2,1},{5,6},{6,5},{9,10},{10,9},{13,14},{14,13},{17,18},{18,... | collective-permute-start | bytes 1966088 | tf_op jit(solution)/shard_map/ppermute | solution.py:64
  239.0 13.5 %collective-permute-start.32 = (bf16[256,1280]{1,0:T(8,128)(2,1)S(1)}, bf16[256,1280]{1,0:T(8,128)(2,1)S(1)}, u32[]{:S(2)}, u32[]{:S(2)}) collective-permute-start(bf16[256,1280]{1,0:T(8,128)(2,1)S(1)} %collective-permute-done.31.refs_1_), channel_id=1, source_target_pairs={{1,0},{2,3},{5,4},{6,7},{9,8},{10,11},{13,12},{14,15},{17,16},{18,... | collective-permute-start | bytes 1966088 | tf_op jit(solution)/shard_map/ppermute | solution.py:64
  240.3 14.4 %collective-permute-start.33 = (bf16[256,1280]{1,0:T(8,128)(2,1)S(1)}, bf16[256,1280]{1,0:T(8,128)(2,1)S(1)}, u32[]{:S(2)}, u32[]{:S(2)}) collective-permute-start(bf16[256,1280]{1,0:T(8,128)(2,1)S(1)} %collective-permute-done.30.refs_0_), channel_id=1, source_target_pairs={{1,2},{2,1},{5,6},{6,5},{9,10},{10,9},{13,14},{14,13},{17,18},{18,... | collective-permute-start | bytes 1966088 | tf_op jit(solution)/shard_map/ppermute | solution.py:64
  254.7 22.1 %collective-permute-start.34 = (bf16[256,1280]{1,0:T(8,128)(2,1)S(1)}, bf16[256,1280]{1,0:T(8,128)(2,1)}, u32[]{:S(2)}, u32[]{:S(2)}) collective-permute-start(bf16[256,1280]{1,0:T(8,128)(2,1)S(1)} %collective-permute-done.33.refs_3_), channel_id=1, source_target_pairs={{1,0},{2,3},{5,4},{6,7},{9,8},{10,11},{13,12},{14,15},{17,16},{18,... | collective-permute-start | bytes 1966088 | tf_op jit(solution)/shard_map/ppermute | solution.py:64
  258.3 19.1 %all-to-all-start.1 = ((bf16[8,1,32,1280]{3,2,1,0:T(8,128)(2,1)}), bf16[8,1,32,1280]{3,2,1,0:T(8,128)(2,1)S(1)}, u32[]{:S(2)}, u32[]{:S(2)}) async-start(bf16[8,1,32,1280]{3,2,1,0:T(8,128)(2,1)} %bitcast.87), calls=%async_computation.1 | async-start | bytes 1310720 | tf_op jit(solution)/shard_map/all_to_all | solution.py:689
  277.3 30.1 %collective-permute-start.40 = (bf16[256,1280]{1,0:T(8,128)(2,1)S(1)}, bf16[256,1280]{1,0:T(8,128)(2,1)S(1)}, u32[]{:S(2)}, u32[]{:S(2)}) collective-permute-start(bf16[256,1280]{1,0:T(8,128)(2,1)S(1)} %bitcast.78), channel_id=1, source_target_pairs={{0,1},{1,0},{2,3},{3,2},{4,5},{5,4},{6,7},{7,6},{8,9},{9,8},{10,11... | collective-permute-start | bytes 1966088 | tf_op jit(solution)/shard_map/ppermute | solution.py:64
  277.4 30.1 %collective-permute-start.41 = (bf16[256,1280]{1,0:T(8,128)(2,1)S(1)}, bf16[256,1280]{1,0:T(8,128)(2,1)S(1)}, u32[]{:S(2)}, u32[]{:S(2)}) collective-permute-start(bf16[256,1280]{1,0:T(8,128)(2,1)S(1)} %bitcast.79), channel_id=1, source_target_pairs={{1,2},{2,1},{5,6},{6,5},{9,10},{10,9},{13,14},{14,13},{17,18},{18,... | collective-permute-start | bytes 1966088 | tf_op jit(solution)/shard_map/ppermute | solution.py:64
  300.6 18.5 %collective-permute-start.35 = (bf16[256,1280]{1,0:T(8,128)(2,1)S(1)}, bf16[256,1280]{1,0:T(8,128)(2,1)S(1)}, u32[]{:S(2)}, u32[]{:S(2)}) collective-permute-start(bf16[256,1280]{1,0:T(8,128)(2,1)S(1)} %get-tuple-element.239), channel_id=1, source_target_pairs={{0,1},{3,2},{4,5},{7,6},{8,9},{11,10},{12,13},{15,14},{16,17},{19,... | collective-permute-start | bytes 1966088 | tf_op jit(solution)/shard_map/ppermute | solution.py:64
  307.5 20.9 %collective-permute-start.42 = (bf16[256,1280]{1,0:T(8,128)(2,1)S(1)}, bf16[256,1280]{1,0:T(8,128)(2,1)S(1)}, u32[]{:S(2)}, u32[]{:S(2)}) collective-permute-start(bf16[256,1280]{1,0:T(8,128)(2,1)S(1)} %collective-permute-done.41.refs_1_), channel_id=1, source_target_pairs={{1,0},{2,3},{5,4},{6,7},{9,8},{10,11},{13,12},{14,15},{17,16},{18,... | collective-permute-start | bytes 1966088 | tf_op jit(solution)/shard_map/ppermute | solution.py:64
  312.1 19.6 %collective-permute-start.43 = (bf16[256,1280]{1,0:T(8,128)(2,1)S(1)}, bf16[256,1280]{1,0:T(8,128)(2,1)S(1)}, u32[]{:S(2)}, u32[]{:S(2)}) collective-permute-start(bf16[256,1280]{1,0:T(8,128)(2,1)S(1)} %collective-permute-done.40.refs_0_), channel_id=1, source_target_pairs={{1,2},{2,1},{5,6},{6,5},{9,10},{10,9},{13,14},{14,13},{17,18},{18,... | collective-permute-start | bytes 1966088 | tf_op jit(solution)/shard_map/ppermute | solution.py:64
  319.3 24.6 %collective-permute-start.36 = (bf16[256,1280]{1,0:T(8,128)(2,1)S(1)}, bf16[256,1280]{1,0:T(8,128)(2,1)S(1)}, u32[]{:S(2)}, u32[]{:S(2)}) collective-permute-start(bf16[256,1280]{1,0:T(8,128)(2,1)S(1)} %add_convert_fusion.4), channel_id=1, source_target_pairs={{1,2},{2,1},{5,6},{6,5},{9,10},{10,9},{13,14},{14,13},{17,18},{18,... | collective-permute-start | bytes 1966088 | tf_op jit(solution)/shard_map/ppermute | solution.py:64
  321.7 22.5 %collective-permute-start.37 = (bf16[256,1280]{1,0:T(8,128)(2,1)S(1)}, bf16[256,1280]{1,0:T(8,128)(2,1)S(1)}, u32[]{:S(2)}, u32[]{:S(2)}) collective-permute-start(bf16[256,1280]{1,0:T(8,128)(2,1)S(1)} %get-tuple-element.200), channel_id=1, source_target_pairs={{0,1},{3,2},{4,5},{7,6},{8,9},{11,10},{12,13},{15,14},{16,17},{19,... | collective-permute-start | bytes 1966088 | tf_op jit(solution)/shard_map/ppermute | solution.py:64
  331.7 20.8 %collective-permute-start.44 = (bf16[256,1280]{1,0:T(8,128)(2,1)S(1)}, bf16[256,1280]{1,0:T(8,128)(2,1)S(1)}, u32[]{:S(2)}, u32[]{:S(2)}) collective-permute-start(bf16[256,1280]{1,0:T(8,128)(2,1)S(1)} %collective-permute-done.43.refs_3_), channel_id=1, source_target_pairs={{1,0},{2,3},{5,4},{6,7},{9,8},{10,11},{13,12},{14,15},{17,16},{18,... | collective-permute-start | bytes 1966088 | tf_op jit(solution)/shard_map/ppermute | solution.py:64
  344.3 21.3 %collective-permute-start.39 = (bf16[256,1280]{1,0:T(8,128)(2,1)S(1)}, bf16[256,1280]{1,0:T(8,128)(2,1)S(1)}, u32[]{:S(2)}, u32[]{:S(2)}) collective-permute-start(bf16[256,1280]{1,0:T(8,128)(2,1)S(1)} %add_convert_fusion.3), channel_id=1, source_target_pairs={{1,2},{2,1},{5,6},{6,5},{9,10},{10,9},{13,14},{14,13},{17,18},{18,... | collective-permute-start | bytes 1966088 | tf_op jit(solution)/shard_map/ppermute | solution.py:64
  346.7 18.9 %collective-permute-start.38 = (bf16[256,1280]{1,0:T(8,128)(2,1)S(1)}, bf16[256,1280]{1,0:T(8,128)(2,1)S(1)}, u32[]{:S(2)}, u32[]{:S(2)}) collective-permute-start(bf16[256,1280]{1,0:T(8,128)(2,1)S(1)} %fusion.3), channel_id=1, source_target_pairs={{0,1},{1,0},{2,3},{3,2},{4,5},{5,4},{6,7},{7,6},{8,9},{9,8},{10,11... | collective-permute-start | bytes 1966088 | tf_op jit(solution)/shard_map/ppermute | solution.py:64
  369.4 16.5 %collective-permute-start.45 = (bf16[256,1280]{1,0:T(8,128)(2,1)S(1)}, bf16[256,1280]{1,0:T(8,128)(2,1)S(1)}, u32[]{:S(2)}, u32[]{:S(2)}) collective-permute-start(bf16[256,1280]{1,0:T(8,128)(2,1)S(1)} %get-tuple-element.238), channel_id=1, source_target_pairs={{0,1},{3,2},{4,5},{7,6},{8,9},{11,10},{12,13},{15,14},{16,17},{19,... | collective-permute-start | bytes 1966088 | tf_op jit(solution)/shard_map/ppermute | solution.py:64
  386.9 15.9 %collective-permute-start.46 = (bf16[256,1280]{1,0:T(8,128)(2,1)}, bf16[256,1280]{1,0:T(8,128)(2,1)}, u32[]{:S(2)}, u32[]{:S(2)}) collective-permute-start(bf16[256,1280]{1,0:T(8,128)(2,1)} %add_convert_fusion.2), channel_id=1, source_target_pairs={{1,2},{2,1},{5,6},{6,5},{9,10},{10,9},{13,14},{14,13},{17,18},{18,... | collective-permute-start | bytes 1966088 | tf_op jit(solution)/shard_map/ppermute | solution.py:64
  390.4 15.6 %collective-permute-start.47 = (bf16[256,1280]{1,0:T(8,128)(2,1)}, bf16[256,1280]{1,0:T(8,128)(2,1)}, u32[]{:S(2)}, u32[]{:S(2)}) collective-permute-start(bf16[256,1280]{1,0:T(8,128)(2,1)} %get-tuple-element.230), channel_id=1, source_target_pairs={{0,1},{3,2},{4,5},{7,6},{8,9},{11,10},{12,13},{15,14},{16,17},{19,... | collective-permute-start | bytes 1966088 | tf_op jit(solution)/shard_map/ppermute | solution.py:64
  391.7 16.5 %all-to-all-start.2 = ((bf16[8,1,32,1280]{3,2,1,0:T(8,128)(2,1)}), bf16[8,1,32,1280]{3,2,1,0:T(8,128)(2,1)S(1)}, u32[]{:S(2)}, u32[]{:S(2)}) async-start(bf16[8,1,32,1280]{3,2,1,0:T(8,128)(2,1)} %bitcast.35), calls=%async_computation.2 | async-start | bytes 1310720 | tf_op jit(solution)/shard_map/all_to_all | solution.py:681
  408.1 14.6 %collective-permute-start.49 = (bf16[256,1280]{1,0:T(8,128)(2,1)}, bf16[256,1280]{1,0:T(8,128)(2,1)S(1)}, u32[]{:S(2)}, u32[]{:S(2)}) collective-permute-start(bf16[256,1280]{1,0:T(8,128)(2,1)} %add_convert_fusion.1), channel_id=1, source_target_pairs={{1,2},{2,1},{5,6},{6,5},{9,10},{10,9},{13,14},{14,13},{17,18},{18,... | collective-permute-start | bytes 1966088 | tf_op jit(solution)/shard_map/ppermute | solution.py:64
  424.4 15.8 %all-to-all-start.3 = ((bf16[8,1,32,1280]{3,2,1,0:T(8,128)(2,1)}), bf16[8,1,32,1280]{3,2,1,0:T(8,128)(2,1)S(1)}, u32[]{:S(2)}, u32[]{:S(2)}) async-start(bf16[8,1,32,1280]{3,2,1,0:T(8,128)(2,1)} %bitcast.85), calls=%async_computation.3 | async-start | bytes 1310720 | tf_op jit(solution)/shard_map/all_to_all | solution.py:681
  (68 other events, 581.6 us)

commit v3 on v2

--- a/solution.py
+++ b/solution.py
@@ -147,21 +147,22 @@
     )(values, gains.reshape(1, columns))
 
 
-def choose(code, refs):
-    value = refs[0][...]
-    for number in range(1, len(refs)):
+def choose(code, refs, numbers=None):
+    first, *others = numbers or range(len(refs))
+    value = refs[first][...]
+    for number in others:
         value = jnp.where(code == number, refs[number][...], value)
     return value
 
 
-def sum_dots_kernel(codes_ref, *refs, lefts, splits, added):
+def sum_dots_kernel(codes_ref, *refs, lefts, splits, added, numbers):
     left, right, chosen = refs[:lefts], refs[lefts : lefts + sum(splits)], refs[-1]
     out_ref = refs[-2]
 
     @pl.when(pl.program_id(0) == 0)
     def _():
         for k in range(len(splits)):
-            chosen[k] = choose(codes_ref[k], left)
+            chosen[k] = choose(codes_ref[k], left, numbers[k])
 
     total = None
     for more in refs[lefts + sum(splits) : lefts + sum(splits) + added]:
@@ -179,7 +180,7 @@
     out_ref[...] = total.astype(out_ref.dtype)
 
 
-def sum_dots(codes, lefts, rights, added):
+def sum_dots(codes, numbers, lefts, rights, added):
     rows, columns = lefts[0].shape[0], rights[0][0].shape[1]
     tile = 256 if columns % 256 == 0 else 128
     flat = [m for mats in rights for m in mats]
@@ -190,6 +191,7 @@
             lefts=len(lefts),
             splits=tuple(len(mats) for mats in rights),
             added=len(added),
+            numbers=numbers,
         ),
         out_shape=jax.ShapeDtypeStruct((rows, columns), BF16),
         grid_spec=pltpu.PrefetchScalarGridSpec(
@@ -255,7 +257,9 @@
     rows = query_ref.shape[0]
     own = places_ref[0]
     scale = HD ** (-0.5) * LOG2E
-    queries = [query_ref[:, g * HD : (g + 1) * HD] for g in range(group_size)]
+    queries = jnp.concatenate(
+        [query_ref[:, g * HD : (g + 1) * HD] for g in range(group_size)], axis=0
+    )
 
     number = 1
     for piece in pieces:
@@ -264,45 +268,41 @@
             held[pl.ds(to, rows), :] = piece[start : start + rows, :]
             number += 1
 
-    def block(start, states, masked):
-        keys = held[pl.ds(start, rows), :HD]
-        values = held[pl.ds(start, rows), HD:]
-        states_out = []
-        for query, (top, total, acc) in zip(queries, states):
-            scores = lax.dot_general(
-                keys, query, (((1,), (1,)), ((), ())), preferred_element_type=F32
-            )
-            if masked:
-                key_at = lax.broadcasted_iota(jnp.int32, scores.shape, 0)
-                query_at = lax.broadcasted_iota(jnp.int32, scores.shape, 1)
-                scores = jnp.where(key_at <= query_at, scores, -1e30)
-            new_top = jnp.maximum(top, jnp.max(scores, axis=0, keepdims=True))
-            weights = jnp.exp2((scores - new_top) * scale)
-            factor = jnp.exp2((top - new_top) * scale)
-            total = total * factor + jnp.sum(weights, axis=0, keepdims=True)
-            mixed = lax.dot_general(
-                values,
-                weights.astype(BF16),
-                (((0,), (0,)), ((), ())),
-                preferred_element_type=F32,
-            )
-            states_out.append((new_top, total, acc * factor + mixed))
-        return tuple(states_out)
-
-    start_state = tuple(
-        (
-            jnp.full((1, rows), -1e30, F32),
-            jnp.zeros((1, rows), F32),
-            jnp.zeros((HD, rows), F32),
+    def block(first, count, state, masked=False):
+        at = pl.ds(pl.multiple_of(first * rows, rows), count * rows)
+        top, total, acc = state
+        scores = lax.dot_general(
+            held[at, :HD], queries, (((1,), (1,)), ((), ())), preferred_element_type=F32
         )
-        for _ in range(group_size)
+        if masked:
+            key_at = lax.broadcasted_iota(jnp.int32, scores.shape, 0)
+            query_at = lax.broadcasted_iota(jnp.int32, scores.shape, 1) % rows
+            scores = jnp.where(key_at <= query_at, scores, -1e30)
+        new_top = jnp.maximum(top, jnp.max(scores, axis=0, keepdims=True))
+        weights = jnp.exp2((scores - new_top) * scale)
+        factor = jnp.exp2((top - new_top) * scale)
+        total = total * factor + jnp.sum(weights, axis=0, keepdims=True)
+        mixed = lax.dot_general(
+            held[at, HD:],
+            weights.astype(BF16),
+            (((0,), (0,)), ((), ())),
+            preferred_element_type=F32,
+        )
+        return new_top, total, acc * factor + mixed
+
+    state = (
+        jnp.full((1, group_size * rows), -1e30, F32),
+        jnp.zeros((1, group_size * rows), F32),
+        jnp.zeros((HD, group_size * rows), F32),
     )
-    states = block(pl.multiple_of(own * rows, rows), start_state, True)
-    states = lax.fori_loop(
-        0, own, lambda j, held: block(pl.multiple_of(j * rows, rows), held, False), states
-    )
-    for g, (_, total, acc) in enumerate(states):
-        out_ref[:, g * HD : (g + 1) * HD] = (acc / total).T.astype(BF16)
+    state = block(own, 1, state, masked=True)
+    pairs = own // 2
+    state = lax.fori_loop(0, pairs, lambda j, held_state: block(2 * j, 2, held_state), state)
+    state = lax.fori_loop(2 * pairs, own, lambda j, held_state: block(j, 1, held_state), state)
+    _, total, acc = state
+    acc = acc / total
+    for g in range(group_size):
+        out_ref[:, g * HD : (g + 1) * HD] = acc[:, g * rows : (g + 1) * rows].T.astype(BF16)
 
 
 def attend(own, queries, pieces, places):
@@ -564,7 +564,7 @@
     sent = next_block(take)
     following = next_block(take_query)
     kv_near = together(
-        near_blocks(kv_mats), *move(sent), *ready(following), other_tokens, normed[0]
+        near_blocks(kv_mats), *move(sent), *ready(following), other_tokens, normed[0], own_tokens
     )
     first = kv_near[2]
     sent, following = following, next_block(first)
@@ -618,10 +618,14 @@
     for own, entries in enumerate(arrival_order(hx_count)):
         for source, number in entries:
             table[own, (own - source) % hx_count] = 1 + number
+    used = sorted(set(table.reshape(-1).tolist()))
+    table = np.searchsorted(used, table).astype(np.int32)
+    lefts = {j: [lefts[j][number] for number in used] for j in lefts}
+    numbers = tuple(tuple(sorted(set(table[:, k].tolist()))) for k in range(hx_count))
     codes = jnp.asarray(table)[hx_index]
     rights = [out_parts[k] for k in range(hx_count)]
-    given = swap(sum_dots(codes, lefts[1], rights, ()), "ctx", 1)
-    return sum_dots(codes, lefts[0], rights, (given, own_tokens))
+    given = swap(sum_dots(codes, numbers, lefts[1], rights, ()), "ctx", 1)
+    return sum_dots(codes, numbers, lefts[0], rights, (given, own_tokens))
 
 
 def body(
@@ -672,52 +676,94 @@
     router_rows = w_router.T
     order = arrival_order(hx_count)
     codes = [jnp.stack([hx_index, jnp.int32(0), hx_index]).astype(jnp.int32)]
+    arrays = [None]
     for t in range(hx_count - 1):
-        found = jnp.asarray(np.array([entries[t] for entries in order], np.int32))[hx_index]
-        codes.append(jnp.concatenate([found, codes[0][2:]]))
+        found = np.array([entries[t] for entries in order], np.int32)
+        arrays.append(sorted(set(found[:, 1].tolist())))
+        found[:, 1] = np.searchsorted(arrays[-1], found[:, 1])
+        codes.append(jnp.concatenate([jnp.asarray(found)[hx_index], codes[0][2:]]))
 
     def give_back(c, reduced):
         reduced = jnp.stack([r.reshape(ctx_count, part, width) for r in reduced], axis=1)
         returned = lax.all_to_all(reduced, "ctx", split_axis=0, concat_axis=0, tiled=True)
         return returned.reshape(expert_count * part, width)
 
-    returned = []
-    scatter, arrived, reached = None, (), ()
-    for c in range(CHUNKS):
+    rows = [slice(e * ctx_count * part, (e + 1) * ctx_count * part) for e in range(exp_local)]
+    router = [
+        lax.dynamic_slice_in_dim(router_rows, ctx_index * exp_local + e, 1, 0)
+        for e in range(exp_local)
+    ]
+
+    def take_rows(c, *earlier):
         sent = dot32(pickers[c], stream).astype(BF16)
         sent = sent.reshape(ctx_count, exp_local, part, width)
+        sent = after(sent, *earlier) if earlier else sent
         taken = lax.all_to_all(sent, "ctx", split_axis=0, concat_axis=0, tiled=True)
-        if reached:
-            taken = after(taken, *reached)
         taken = taken.reshape(ctx_count, exp_local, part, width)
-        taken = taken.swapaxes(0, 1).reshape(exp_local * ctx_count * part, width)
-        gather = line_gather(taken)
-        rows = [slice(e * ctx_count * part, (e + 1) * ctx_count * part) for e in range(exp_local)]
-        router = [
-            lax.dynamic_slice_in_dim(router_rows, ctx_index * exp_local + e, 1, 0)
+        return taken.swapaxes(0, 1).reshape(exp_local * ctx_count * part, width)
+
+    def add_shares(t, shares, totals):
+        return [
+            expert_share(
+                codes[t], [x[rows[e]] for x in shares], gains, router[e], w_gate, w_up, totals[e], e
+            )
             for e in range(exp_local)
         ]
-        shares = [taken]
-        totals = [None] * exp_local
+
+    def held_back(values, totals):
+        marks = tuple(x for sums in totals for x in sums[2:])
+        return lax.optimization_barrier(tuple(values) + marks)[: len(values)]
+
+    def after_all(values, earlier):
+        return lax.optimization_barrier(tuple(values) + tuple(earlier))[: len(values)]
+
+    none = [None] * exp_local
+    returned = []
+    scatter, arrived = None, ()
+    taken = take_rows(0)
+    totals = None
+    for c in range(CHUNKS):
+        gather = line_gather(taken)
+        following = None
+        shares = []
         for t in range(hx_count - 1):
-            earlier = [x for sums in totals if sums for x in sums[2:]] + shares[-1:] * (t == 0)
-            if t == hx_count - 2:
-                earlier += arrived
+            inner = 0 < t < hx_count - 2
+            if inner and scatter:
+                totals = add_shares(t, [shares[n] for n in arrays[t]], totals)
+            earlier = list(arrived) if t == hx_count - 2 else []
+            if inner:
+                earlier = [x for sums in totals for x in sums[2:]]
+            elif t > 0 and following is not None:
+                earlier.append(following)
             pair = next(gather) if t == 0 else gather.send(earlier)
-            totals = [
-                expert_share(
-                    codes[t], [x[rows[e]] for x in shares[t > 0 :]], gains, router[e], w_gate, w_up, totals[e], e
-                )
-                for e in range(exp_local)
-            ]
-            reached = pair
+            if t == 0:
+                totals = totals or add_shares(0, [taken], none)
+            elif not (inner and scatter):
+                if inner:
+                    shares = list(after_all(shares, pair))
+                totals = add_shares(t, [shares[n] for n in arrays[t]], totals)
+            if t == 0 and c + 1 < CHUNKS:
+                following = take_rows(c + 1, *pair)
             if scatter and t == hx_count - 2:
                 arrived = [x for sums in scatter for x in next(sums)]
                 pair = lax.optimization_barrier(tuple(pair) + tuple(arrived))[:2]
             shares = shares + list(pair)
+        following_totals = None
+        if c + 1 < CHUNKS:
+            following_totals = add_shares(0, [following], none)
+            taken = after(following, *shares[-2:])
+            shares = held_back(shares, following_totals)
         outs = [
             expert_finish(
-                codes[-1], [x[rows[e]] for x in shares[1:]], gains, router[e], w_gate, w_up, totals[e], w_down, e
+                codes[-1],
+                [shares[n][rows[e]] for n in arrays[-1]],
+                gains,
+                router[e],
+                w_gate,
+                w_up,
+                totals[e],
+                w_down,
+                e,
             )
             for e in range(exp_local)
         ]
@@ -725,8 +771,10 @@
         if scatter:
             for _ in range(hx_count - 4):
                 [next(sums) for sums in scatter]
-            reduced = [next(sums) for sums in scatter]
+            marks = [x for sums in totals for x in sums[2:]]
+            reduced = [sums.send(marks) for sums in scatter]
             outs = [after(o, *reduced) for o in outs]
+        totals = following_totals
         scatter = [line_scatter(o) for o in outs]
         arrived = [x for sums in scatter for x in next(sums)]
         if reduced:

time: 452 us -> 444 us (0.982)
  local copies, waits for them, and re-layouts: 50 us -> 45.1 us
    all_to_all x2, starting transfers between devices: 21.7 us -> 10.3 us  [take_rows(): taken = lax.all_to_all(sent, 'ctx', split_axis=0, concat_axis=0, tiled=True)]
    ppermute x30, waiting for transfers between devices: 78.4 us -> 71 us  [pass_on(): lax.ppermute(values, 'hx', pairs)]
    all_to_all x2, waiting for transfers between devices: 11.6 us -> 17.3 us  [take_rows(): taken = lax.all_to_all(sent, 'ctx', split_axis=0, concat_axis=0, tiled=True)]
    all_to_all x2, waiting for transfers between devices: 9.33 us -> 14.4 us  [give_back(): lax.all_to_all(reduced, 'ctx', split_axis=0, concat_axis=0, tiled=True)]
    unnamed x125 -> x101, local copies, waits for them, and re-layouts: 28.4 us -> 23.7 us
  transfers between devices with their start and end apart: 54 -> 54, of which waited for: 32 -> 35; matrix products, arithmetic and copies ran while one was open for 7% -> 7% of each run, Pallas kernels for 22% -> 22%
where the time goes in v3:
time: 444 us; the launch traced here: 435 us
  waiting for transfers between devices  132 us (30%)
  starting transfers between devices  120 us (27%)
  Pallas kernels  114 us (26%)
  local copies, waits for them, and re-layouts  45.1 us (10%)
  other arithmetic  13.7 us (3%)
  matrix products  9.1 us (2%)
    ppermute x30, starting transfers between devices, pass_on(): lax.ppermute(values, 'hx', pairs)  75.7 us
    ppermute x30, waiting for transfers between devices, pass_on(): lax.ppermute(values, 'hx', pairs)  71 us
    pallas_call x6, Pallas kernels, expert_share(): pl.pallas_call(functools.partial(share_kernel, shares=len(shares), added=...  33 us
    pallas_call x2, Pallas kernels, expert_finish(): pl.pallas_call(functools.partial(finish_kernel, shares=len(shares), tiles...  26.3 us
    unnamed x101, local copies, waits for them, and re-layouts  23.7 us
    pallas_call x4, Pallas kernels, project(): pl.pallas_call(functools.partial(project_kernel, count=len(values), mats=...  22 us
    ppermute x16, waiting for transfers between devices, swap(): return lax.ppermute(value, axis, [(i, i ^ offset) for i in range(count)])  18.8 us
    all_to_all x2, waiting for transfers between devices, take_rows(): taken = lax.all_to_all(sent, 'ctx', split_axis=0, concat_axis=0, tiled=True)  17.3 us
  transfers between devices with their start and end apart: 54, of which 35 were waited for; matrix products, arithmetic and copies ran while one was open for 7% of the time, Pallas kernels for 22%

profile of v3, /device:TPU:16, one launch (start us, length us, event | category | flops | bytes accessed | tf_op | source)
XLA Modules:
  0.0 435.4 jit_solution(17501120053170788791)
XLA Ops:
  6.0 3.8 fusion.32
  17.1 5.1 %norm_rows.2.refs_0_.refs_1_.refs_2_ = bf16[512,5120]{1,0:T(8,128)(2,1)S(1)} custom-call(bf16[512,5120]{1,0:T(8,128)(2,1)} %values_ref.1, bf16[1,5120]{1,0:T(2,128)(2,1)S(1)} %reshape.82.gains_ref), custom_call_target="tpu_custom_call" | custom-call | bytes 4096 | tf_op jit(solution)/shard_map/norm_rows/pallas_call | solution.py:135
  29.3 4.5 %collective-permute-done.5.refs_7_ = bf16[384,1280]{1,0:T(8,128)(2,1)S(1)} collective-permute-done((bf16[384,1280]{1,0:T(8,128)(2,1)}, bf16[384,1280]{1,0:T(8,128)(2,1)S(1)}, u32[]{:S(2)}, u32[]{:S(2)}) %collective-permute-start.5) | collective-permute-done | bytes 983072 | tf_op jit(solution)/shard_map/ppermute | solution.py:49
  41.1 5.0 %norm_rows.3.refs_3_.refs_4_.refs_5_.refs_2_ = bf16[512,5120]{1,0:T(8,128)(2,1)S(1)} custom-call(bf16[512,5120]{1,0:T(8,128)(2,1)} %collective-permute-done.2.values_ref, bf16[1,5120]{1,0:T(2,128)(2,1)S(1)} %reshape.82.gains_ref), custom_call_target="tpu_custom_call" | custom-call | bytes 4096 | tf_op jit(solution)/shard_map/norm_rows/pallas_call | solution.py:135
  48.4 6.2 %project.4 = (f32[512,256]{1,0:T(8,128)S(1)}, f32[512,256]{1,0:T(8,128)S(1)}) custom-call(s32[3]{0:T(128)S(1)} %pad_add_fusion.1.places_ref, bf16[512,5120]{1,0:T(8,128)(2,1)} %copy-done.2, bf16[512,5120]{1,0:T(8,128)(2,1)} %copy-done.2, bf16[512,5120]{1,0:T(8,128)(2,1)} %copy-done.2, bf16[512,5120]{1,0:T(8,128)(2,1)} %copy-done.3, ...), custom_call_target="tpu_custom_call" | custom-call | bytes 4096 | tf_op jit(solution)/shard_map/project/pallas_call | solution.py:231
  58.7 5.2 %collective-permute-done.6.refs_4_ = bf16[640,256]{1,0:T(8,128)(2,1)} collective-permute-done((bf16[640,256]{1,0:T(8,128)(2,1)}, bf16[640,256]{1,0:T(8,128)(2,1)}, u32[]{:S(2)}, u32[]{:S(2)}) %collective-permute-start.6) | collective-permute-done | bytes 327712 | tf_op jit(solution)/shard_map/ppermute | solution.py:31
  65.1 3.4 project.5
  77.2 8.6 %project.6 = (f32[512,384]{1,0:T(8,128)S(1)}, f32[512,384]{1,0:T(8,128)S(1)}) custom-call(s32[3]{0:T(128)S(1)} %pad_add_fusion.1.places_ref, bf16[512,5120]{1,0:T(8,128)(2,1)} %copy-done.2, bf16[512,5120]{1,0:T(8,128)(2,1)} %copy-done.2, bf16[512,5120]{1,0:T(8,128)(2,1)} %copy-done.2, bf16[512,5120]{1,0:T(8,128)(2,1)} %copy-done.3, ...), custom_call_target="tpu_custom_call" | custom-call | bytes 4096 | tf_op jit(solution)/shard_map/project/pallas_call | solution.py:231
  87.6 3.5 collective-permute-done.13.refs_4_
  99.0 3.4 collective-permute-start.18
  104.6 3.9 project.7
  108.5 3.5 attend.3.refs_0_
  115.6 4.6 %attend.2.refs_0_ = bf16[512,384]{1,0:T(8,128)(2,1)S(1)} custom-call(s32[9]{0:T(128)S(1)} %stack.83.places_ref, bf16[512,384]{1,0:T(8,128)(2,1)S(1)} %get-tuple-element.141.query_ref, bf16[1024,256]{1,0:T(8,128)(2,1)S(1)} %copy-done.37, bf16[1024,256]{1,0:T(8,128)(2,1)S(1)} %copy-done.33, bf16[1024,256]{1,0:T(8,128)(2,1)S(1)} %copy-done.35, ...), custom_call_target="tpu_custom_call" | custom-call | flops 3221225472 | bytes 2097152 | tf_op jit(solution)/shard_map/attend/pallas_call | solution.py:312
  125.6 3.5 collective-permute-start.20
  136.6 3.4 collective-permute-start.27
  140.9 3.4 collective-permute-start.21
  145.0 3.4 collective-permute-start.22
  150.0 4.2 collective-permute-start.28
  157.8 4.8 %collective-permute-start.23 = (bf16[512,384]{1,0:T(8,128)(2,1)}, bf16[512,384]{1,0:T(8,128)(2,1)}, u32[]{:S(2)}, u32[]{:S(2)}) collective-permute-start(bf16[512,384]{1,0:T(8,128)(2,1)} %collective-permute-done.22.refs_4_), channel_id=1, source_target_pairs={{1,0},{2,3},{5,4},{6,7},{9,8},{10,11},{13,12},{14,15},{17,16},{18,... | collective-permute-start | bytes 1179656 | tf_op jit(solution)/shard_map/ppermute | solution.py:64
  165.2 8.4 %collective-permute-done.23.refs_5_ = bf16[512,384]{1,0:T(8,128)(2,1)} collective-permute-done((bf16[512,384]{1,0:T(8,128)(2,1)}, bf16[512,384]{1,0:T(8,128)(2,1)}, u32[]{:S(2)}, u32[]{:S(2)}) %collective-permute-start.23) | collective-permute-done | bytes 393248 | tf_op jit(solution)/shard_map/ppermute | solution.py:64
  173.6 7.0 %sum_dots.2 = bf16[512,1280]{1,0:T(8,128)(2,1)} custom-call(s32[4]{0:T(128)S(1)} %fusion.27.codes_ref, bf16[512,384]{1,0:T(8,128)(2,1)S(1)} %copy-done.25, bf16[512,384]{1,0:T(8,128)(2,1)S(1)} %copy-done.27, bf16[512,384]{1,0:T(8,128)(2,1)S(1)} %copy-done.29, bf16[512,384]{1,0:T(8,128)(2,1)S(1)} %copy-done.31, ...), custom_call_target="tpu_custom_call" | custom-call | bytes 4096 | tf_op jit(solution)/shard_map/sum_dots/pallas_call | solution.py:188
  187.0 7.5 %sum_dots.3 = bf16[512,1280]{1,0:T(8,128)(2,1)} custom-call(s32[4]{0:T(128)S(1)} %fusion.27.codes_ref, bf16[512,384]{1,0:T(8,128)(2,1)S(1)} %attend.3.refs_0_, bf16[512,384]{1,0:T(8,128)(2,1)S(1)} %copy-done.19, bf16[512,384]{1,0:T(8,128)(2,1)S(1)} %copy-done.21, bf16[512,384]{1,0:T(8,128)(2,1)S(1)} %copy-done.23, ...), custom_call_target="tpu_custom_call" | custom-call | bytes 4096 | tf_op jit(solution)/shard_map/sum_dots/pallas_call | solution.py:188
  197.2 5.4 %all-to-all-start = ((bf16[8,1,32,1280]{3,2,1,0:T(8,128)(2,1)}), bf16[8,1,32,1280]{3,2,1,0:T(8,128)(2,1)S(1)}, u32[]{:S(2)}, u32[]{:S(2)}) async-start(bf16[8,1,32,1280]{3,2,1,0:T(8,128)(2,1)} %bitcast.21), calls=%async_computation | async-start | bytes 1310720 | tf_op jit(solution)/shard_map/all_to_all | solution.py:701
  202.7 11.1 %all-to-all-done = bf16[8,1,32,1280]{3,2,1,0:T(8,128)(2,1)S(1)} async-done(((bf16[8,1,32,1280]{3,2,1,0:T(8,128)(2,1)}), bf16[8,1,32,1280]{3,2,1,0:T(8,128)(2,1)S(1)}, u32[]{:S(2)}, u32[]{:S(2)}) %all-to-all-start) | async-done | bytes 655392 | tf_op jit(solution)/shard_map/all_to_all | solution.py:701
  219.7 5.3 %expert_share.6 = (f32[256,1024]{1,0:T(8,128)S(1)}, f32[256,1024]{1,0:T(8,128)S(1)}, f32[256,128]{1,0:T(8,128)S(1)}, f32[256,128]{1,0:T(8,128)S(1)}) custom-call(s32[3]{0:T(128)S(1)} %add_add_fusion.code_ref, bf16[256,1280]{1,0:T(8,128)(2,1)S(1)} %bitcast.82, bf16[1,5120]{1,0:T(2,128)(2,1)S(1)} %reshape.85.refs_1_.refs_2_.refs_3_, ...), custom_call_target="tpu_custom_call" | custom-call | bytes 4096 | tf_op jit(solution)/shard_map/expert_share/pallas_call | solution.py:369
  228.3 3.3 collective-permute-done.31.refs_1_
  238.4 4.8 %all-to-all-start.1 = ((bf16[8,1,32,1280]{3,2,1,0:T(8,128)(2,1)}), bf16[8,1,32,1280]{3,2,1,0:T(8,128)(2,1)S(1)}, u32[]{:S(2)}, u32[]{:S(2)}) async-start(bf16[8,1,32,1280]{3,2,1,0:T(8,128)(2,1)} %bitcast.86), calls=%async_computation.1 | async-start | bytes 1310720 | tf_op jit(solution)/shard_map/all_to_all | solution.py:701
  243.3 4.9 %collective-permute-done.33.refs_0_ = bf16[256,1280]{1,0:T(8,128)(2,1)} collective-permute-done((bf16[256,1280]{1,0:T(8,128)(2,1)S(1)}, bf16[256,1280]{1,0:T(8,128)(2,1)}, u32[]{:S(2)}, u32[]{:S(2)}) %collective-permute-start.33) | collective-permute-done | bytes 655392 | tf_op jit(solution)/shard_map/ppermute | solution.py:64
  248.2 6.2 %all-to-all-done.1 = bf16[8,1,32,1280]{3,2,1,0:T(8,128)(2,1)S(1)} async-done(((bf16[8,1,32,1280]{3,2,1,0:T(8,128)(2,1)}), bf16[8,1,32,1280]{3,2,1,0:T(8,128)(2,1)S(1)}, u32[]{:S(2)}, u32[]{:S(2)}) %all-to-all-start.1) | async-done | bytes 655392 | tf_op jit(solution)/shard_map/all_to_all | solution.py:701
  259.0 5.3 %expert_share.7 = (f32[256,1024]{1,0:T(8,128)S(1)}, f32[256,1024]{1,0:T(8,128)S(1)}, f32[256,128]{1,0:T(8,128)S(1)}, f32[256,128]{1,0:T(8,128)S(1)}) custom-call(s32[3]{0:T(128)S(1)} %add_add_fusion.code_ref, bf16[256,1280]{1,0:T(8,128)(2,1)S(1)} %bitcast.77, bf16[1,5120]{1,0:T(2,128)(2,1)S(1)} %reshape.85.refs_1_.refs_2_.refs_3_, ...), custom_call_target="tpu_custom_call" | custom-call | bytes 4096 | tf_op jit(solution)/shard_map/expert_share/pallas_call | solution.py:369
  264.3 5.4 %expert_share.8 = (f32[256,1024]{1,0:T(8,128)S(1)}, f32[256,1024]{1,0:T(8,128)S(1)}, f32[256,128]{1,0:T(8,128)S(1)}, f32[256,128]{1,0:T(8,128)S(1)}) custom-call(s32[3]{0:T(128)S(1)} %pad_add_fusion.4.code_ref, bf16[256,1280]{1,0:T(8,128)(2,1)S(1)} %collective-permute-done.30.refs_0_, bf16[256,1280]{1,0:T(8,128)(2,1)S(1)} %collective-permute-done.31.refs_1_, ...), custom_call_target="tpu_custom_call" | custom-call | bytes 4096 | tf_op jit(solution)/shard_map/expert_share/pallas_call | solution.py:369
  270.7 5.8 %expert_share.9 = (f32[256,1024]{1,0:T(8,128)S(1)}, f32[256,1024]{1,0:T(8,128)S(1)}, f32[256,128]{1,0:T(8,128)S(1)}, f32[256,128]{1,0:T(8,128)S(1)}) custom-call(s32[3]{0:T(128)S(1)} %get-tuple-element.244.code_ref, bf16[256,1280]{1,0:T(8,128)(2,1)S(1)} %collective-permute-done.30.refs_0_, bf16[256,1280]{1,0:T(8,128)(2,1)S(1)} %collective-permute-done.31.refs_1_, ...), custom_call_target="tpu_custom_call" | custom-call | bytes 4096 | tf_op jit(solution)/shard_map/expert_share/pallas_call | solution.py:369
  279.1 13.3 %expert_finish.2 = bf16[4,256,1280]{2,1,0:T(8,128)(2,1)} custom-call(s32[3]{0:T(128)S(1)} %get-tuple-element.243.code_ref, bf16[256,1280]{1,0:T(8,128)(2,1)} %collective-permute-done.33.refs_0_, bf16[256,1280]{1,0:T(8,128)(2,1)} %collective-permute-done.34.refs_1_, bf16[1,5120]{1,0:T(2,128)(2,1)S(1)} %reshape.85.refs_1_.refs_2_.refs_3_, ...), custom_call_target="tpu_custom_call" | custom-call | bytes 4096 | tf_op jit(solution)/shard_map/expert_finish/pallas_call | solution.py:433
  295.4 5.6 %expert_share.10 = (f32[256,1024]{1,0:T(8,128)S(1)}, f32[256,1024]{1,0:T(8,128)S(1)}, f32[256,128]{1,0:T(8,128)S(1)}, f32[256,128]{1,0:T(8,128)S(1)}) custom-call(s32[3]{0:T(128)S(1)} %pad_add_fusion.4.code_ref, bf16[256,1280]{1,0:T(8,128)(2,1)S(1)} %collective-permute-done.38.refs_0_, bf16[256,1280]{1,0:T(8,128)(2,1)S(1)} %collective-permute-done.39.refs_1_, ...), custom_call_target="tpu_custom_call" | custom-call | bytes 4096 | tf_op jit(solution)/shard_map/expert_share/pallas_call | solution.py:369
  301.0 4.6 %collective-permute-start.40 = (bf16[256,1280]{1,0:T(8,128)(2,1)S(1)}, bf16[256,1280]{1,0:T(8,128)(2,1)S(1)}, u32[]{:S(2)}, u32[]{:S(2)}) collective-permute-start(bf16[256,1280]{1,0:T(8,128)(2,1)S(1)} %collective-permute-done.39.refs_1_), channel_id=1, source_target_pairs={{1,0},{2,3},{5,4},{6,7},{9,8},{10,11},{13,12},{14,15},{17,16},{18,... | collective-permute-start | bytes 1966088 | tf_op jit(solution)/shard_map/ppermute | solution.py:64
  305.7 3.3 collective-permute-start.41
  309.5 3.3 collective-permute-start.36
  316.3 9.0 %collective-permute-done.41.refs_0_ = bf16[256,1280]{1,0:T(8,128)(2,1)S(1)} collective-permute-done((bf16[256,1280]{1,0:T(8,128)(2,1)S(1)}, bf16[256,1280]{1,0:T(8,128)(2,1)S(1)}, u32[]{:S(2)}, u32[]{:S(2)}) %collective-permute-start.41) | collective-permute-done | bytes 655392 | tf_op jit(solution)/shard_map/ppermute | solution.py:64
  326.6 7.9 %collective-permute-done.36 = bf16[256,1280]{1,0:T(8,128)(2,1)S(1)} collective-permute-done((bf16[256,1280]{1,0:T(8,128)(2,1)S(1)}, bf16[256,1280]{1,0:T(8,128)(2,1)S(1)}, u32[]{:S(2)}, u32[]{:S(2)}) %collective-permute-start.36) | collective-permute-done | bytes 655392 | tf_op jit(solution)/shard_map/ppermute | solution.py:64
  334.9 5.6 %expert_share.11 = (f32[256,1024]{1,0:T(8,128)S(1)}, f32[256,1024]{1,0:T(8,128)S(1)}, f32[256,128]{1,0:T(8,128)S(1)}, f32[256,128]{1,0:T(8,128)S(1)}) custom-call(s32[3]{0:T(128)S(1)} %get-tuple-element.244.code_ref, bf16[256,1280]{1,0:T(8,128)(2,1)S(1)} %collective-permute-done.38.refs_0_, bf16[256,1280]{1,0:T(8,128)(2,1)S(1)} %collective-permute-done.39.refs_1_, ...), custom_call_target="tpu_custom_call" | custom-call | bytes 4096 | tf_op jit(solution)/shard_map/expert_share/pallas_call | solution.py:369
  343.9 13.0 %expert_finish.3 = bf16[4,256,1280]{2,1,0:T(8,128)(2,1)} custom-call(s32[3]{0:T(128)S(1)} %get-tuple-element.243.code_ref, bf16[256,1280]{1,0:T(8,128)(2,1)S(1)} %collective-permute-done.41.refs_0_, bf16[256,1280]{1,0:T(8,128)(2,1)S(1)} %collective-permute-done.44.refs_1_, bf16[1,5120]{1,0:T(2,128)(2,1)S(1)} %reshape.85.refs_1_.refs_2_.refs_3_, ...), custom_call_target="tpu_custom_call" | custom-call | bytes 4096 | tf_op jit(solution)/shard_map/expert_finish/pallas_call | solution.py:433
  361.9 12.2 %collective-permute-done.45 = bf16[256,1280]{1,0:T(8,128)(2,1)S(1)} collective-permute-done((bf16[256,1280]{1,0:T(8,128)(2,1)S(1)}, bf16[256,1280]{1,0:T(8,128)(2,1)S(1)}, u32[]{:S(2)}, u32[]{:S(2)}) %collective-permute-start.45) | collective-permute-done | bytes 655392 | tf_op jit(solution)/shard_map/ppermute | solution.py:64
  379.0 7.6 %all-to-all-start.2 = ((bf16[8,1,32,1280]{3,2,1,0:T(8,128)(2,1)}), bf16[8,1,32,1280]{3,2,1,0:T(8,128)(2,1)S(1)}, u32[]{:S(2)}, u32[]{:S(2)}) async-start(bf16[8,1,32,1280]{3,2,1,0:T(8,128)(2,1)} %bitcast.35), calls=%async_computation.2 | async-start | bytes 1310720 | tf_op jit(solution)/shard_map/all_to_all | solution.py:688
  392.6 5.1 %all-to-all-done.2 = bf16[8,1,32,1280]{3,2,1,0:T(8,128)(2,1)S(1)} async-done(((bf16[8,1,32,1280]{3,2,1,0:T(8,128)(2,1)}), bf16[8,1,32,1280]{3,2,1,0:T(8,128)(2,1)S(1)}, u32[]{:S(2)}, u32[]{:S(2)}) %all-to-all-start.2) | async-done | bytes 655392 | tf_op jit(solution)/shard_map/all_to_all | solution.py:688
  397.7 3.4 collective-permute-start.49
  401.9 11.6 %collective-permute-done.49 = bf16[256,1280]{1,0:T(8,128)(2,1)S(1)} collective-permute-done((bf16[256,1280]{1,0:T(8,128)(2,1)}, bf16[256,1280]{1,0:T(8,128)(2,1)S(1)}, u32[]{:S(2)}, u32[]{:S(2)}) %collective-permute-start.49) | collective-permute-done | bytes 655392 | tf_op jit(solution)/shard_map/ppermute | solution.py:64
  415.9 5.0 %all-to-all-start.3 = ((bf16[8,1,32,1280]{3,2,1,0:T(8,128)(2,1)}), bf16[8,1,32,1280]{3,2,1,0:T(8,128)(2,1)S(1)}, u32[]{:S(2)}, u32[]{:S(2)}) async-start(bf16[8,1,32,1280]{3,2,1,0:T(8,128)(2,1)} %bitcast.84), calls=%async_computation.3 | async-start | bytes 1310720 | tf_op jit(solution)/shard_map/all_to_all | solution.py:688
  422.7 9.3 %all-to-all-done.3 = bf16[8,1,32,1280]{3,2,1,0:T(8,128)(2,1)S(1)} async-done(((bf16[8,1,32,1280]{3,2,1,0:T(8,128)(2,1)}), bf16[8,1,32,1280]{3,2,1,0:T(8,128)(2,1)S(1)}, u32[]{:S(2)}, u32[]{:S(2)}) %all-to-all-start.3) | async-done | bytes 655392 | tf_op jit(solution)/shard_map/all_to_all | solution.py:688
  (234 shorter events, 150.8 us)
Async XLA Ops:
  5.0 28.8 %collective-permute-start.2 = (bf16[512,5120]{1,0:T(8,128)(2,1)}, bf16[512,5120]{1,0:T(8,128)(2,1)}, u32[]{:S(2)}, u32[]{:S(2)}) collective-permute-start(bf16[512,5120]{1,0:T(8,128)(2,1)} %values_ref.1), channel_id=1, source_target_pairs={{0,4},{4,0},{8,12},{12,8},{16,20},{20,16},{24,28},{28,24},{1,5},{5... | collective-permute-start | bytes 15728648 | tf_op jit(solution)/shard_map/ppermute | solution.py:31
  9.8 24.0 %collective-permute-start.5 = (bf16[384,1280]{1,0:T(8,128)(2,1)}, bf16[384,1280]{1,0:T(8,128)(2,1)S(1)}, u32[]{:S(2)}, u32[]{:S(2)}) collective-permute-start(bf16[384,1280]{1,0:T(8,128)(2,1)} %get-tuple-element.228), channel_id=1, source_target_pairs={{0,1},{1,2},{2,3},{3,0},{4,5},{5,6},{6,7},{7,4},{8,9},{9,10},{10,1... | collective-permute-start | bytes 2949128 | tf_op jit(solution)/shard_map/ppermute | solution.py:49
  11.4 16.5 %collective-permute-start.3 = (bf16[1280,256]{1,0:T(8,128)(2,1)S(1)}, bf16[1280,256]{1,0:T(8,128)(2,1)S(1)}, u32[]{:S(2)}, u32[]{:S(2)}) collective-permute-start(bf16[1280,256]{1,0:T(8,128)(2,1)S(1)} %pad_maximum_fusion.1.refs_6_), channel_id=1, source_target_pairs={{0,8},{4,12},{8,0},{12,4},{16,24},{20,28},{24,16},{28,20},{1,9},{5... | collective-permute-start | bytes 1966088 | tf_op jit(solution)/shard_map/ppermute | solution.py:31
  13.0 16.3 %collective-permute-start.4 = (bf16[1280,256]{1,0:T(8,128)(2,1)S(1)}, bf16[1280,256]{1,0:T(8,128)(2,1)}, u32[]{:S(2)}, u32[]{:S(2)}) collective-permute-start(bf16[1280,256]{1,0:T(8,128)(2,1)S(1)} %pad_maximum_fusion.1.refs_6_), channel_id=1, source_target_pairs={{0,16},{4,20},{8,24},{12,28},{16,0},{20,4},{24,8},{28,12},{1,17},{... | collective-permute-start | bytes 1966088 | tf_op jit(solution)/shard_map/ppermute | solution.py:31
  33.8 31.3 %collective-permute-start.8 = (bf16[1280,384]{1,0:T(8,128)(2,1)S(1)}, bf16[1280,384]{1,0:T(8,128)(2,1)}, u32[]{:S(2)}, u32[]{:S(2)}) collective-permute-start(bf16[1280,384]{1,0:T(8,128)(2,1)S(1)} %pad_maximum_fusion.refs_6_), channel_id=1, source_target_pairs={{0,8},{4,12},{8,0},{12,4},{16,24},{20,28},{24,16},{28,20},{1,9},{5... | collective-permute-start | bytes 2949128 | tf_op jit(solution)/shard_map/ppermute | solution.py:31
  35.3 29.8 %collective-permute-start.9 = (bf16[1280,384]{1,0:T(8,128)(2,1)S(1)}, bf16[1280,384]{1,0:T(8,128)(2,1)}, u32[]{:S(2)}, u32[]{:S(2)}) collective-permute-start(bf16[1280,384]{1,0:T(8,128)(2,1)S(1)} %pad_maximum_fusion.refs_6_), channel_id=1, source_target_pairs={{0,16},{4,20},{8,24},{12,28},{16,0},{20,4},{24,8},{28,12},{1,17},{... | collective-permute-start | bytes 2949128 | tf_op jit(solution)/shard_map/ppermute | solution.py:31
  36.8 28.3 %collective-permute-start.10 = (bf16[384,1280]{1,0:T(8,128)(2,1)}, bf16[384,1280]{1,0:T(8,128)(2,1)}, u32[]{:S(2)}, u32[]{:S(2)}) collective-permute-start(bf16[384,1280]{1,0:T(8,128)(2,1)} %get-tuple-element.124), channel_id=1, source_target_pairs={{0,3},{1,0},{2,1},{3,2},{4,7},{5,4},{6,5},{7,6},{8,11},{9,8},{10,9... | collective-permute-start | bytes 2949128 | tf_op jit(solution)/shard_map/ppermute | solution.py:49
  40.0 23.9 %collective-permute-start.6 = (bf16[640,256]{1,0:T(8,128)(2,1)}, bf16[640,256]{1,0:T(8,128)(2,1)}, u32[]{:S(2)}, u32[]{:S(2)}) collective-permute-start(bf16[640,256]{1,0:T(8,128)(2,1)} %slice.54), channel_id=1, source_target_pairs={{0,8},{4,12},{8,0},{12,4},{16,24},{20,28},{24,16},{28,20},{1,9},{5... | collective-permute-start | bytes 983048 | tf_op jit(solution)/shard_map/ppermute | solution.py:31
  40.5 24.6 %collective-permute-start.7 = (bf16[640,256]{1,0:T(8,128)(2,1)}, bf16[640,256]{1,0:T(8,128)(2,1)}, u32[]{:S(2)}, u32[]{:S(2)}) collective-permute-start(bf16[640,256]{1,0:T(8,128)(2,1)} %slice.55), channel_id=1, source_target_pairs={{0,16},{4,20},{8,24},{12,28},{16,0},{20,4},{24,8},{28,12},{1,17},{... | collective-permute-start | bytes 983048 | tf_op jit(solution)/shard_map/ppermute | solution.py:31
  68.6 25.8 %collective-permute-start.11 = (bf16[1024,256]{1,0:T(8,128)(2,1)S(1)}, bf16[1024,256]{1,0:T(8,128)(2,1)S(1)}, u32[]{:S(2)}, u32[]{:S(2)}) collective-permute-start(bf16[1024,256]{1,0:T(8,128)(2,1)S(1)} %constant_dynamic-update-slice_fusion.refs_0_), channel_id=1, source_target_pairs={{0,8},{4,12},{8,0},{12,4},{16,24},{20,28},{24,16},{28,20},{1,9},{5... | collective-permute-start | bytes 1572872 | tf_op jit(solution)/shard_map/ppermute | solution.py:31
  69.2 25.2 %collective-permute-start.12 = (bf16[1024,256]{1,0:T(8,128)(2,1)S(1)}, bf16[1024,256]{1,0:T(8,128)(2,1)S(1)}, u32[]{:S(2)}, u32[]{:S(2)}) collective-permute-start(bf16[1024,256]{1,0:T(8,128)(2,1)S(1)} %constant_dynamic-update-slice_fusion.refs_0_), channel_id=1, source_target_pairs={{0,16},{4,20},{8,24},{12,28},{16,0},{20,4},{24,8},{28,12},{1,17},{... | collective-permute-start | bytes 1572872 | tf_op jit(solution)/shard_map/ppermute | solution.py:31
  72.9 18.2 %collective-permute-start.13 = (bf16[640,384]{1,0:T(8,128)(2,1)S(1)}, bf16[640,384]{1,0:T(8,128)(2,1)S(1)}, u32[]{:S(2)}, u32[]{:S(2)}) collective-permute-start(bf16[640,384]{1,0:T(8,128)(2,1)S(1)} %slice.56), channel_id=1, source_target_pairs={{0,8},{4,12},{8,0},{12,4},{16,24},{20,28},{24,16},{28,20},{1,9},{5... | collective-permute-start | bytes 1474568 | tf_op jit(solution)/shard_map/ppermute | solution.py:31
  74.4 17.0 %collective-permute-start.14 = (bf16[640,384]{1,0:T(8,128)(2,1)S(1)}, bf16[640,384]{1,0:T(8,128)(2,1)S(1)}, u32[]{:S(2)}, u32[]{:S(2)}) collective-permute-start(bf16[640,384]{1,0:T(8,128)(2,1)S(1)} %slice.57), channel_id=1, source_target_pairs={{0,16},{4,20},{8,24},{12,28},{16,0},{20,4},{24,8},{28,12},{1,17},{... | collective-permute-start | bytes 1474568 | tf_op jit(solution)/shard_map/ppermute | solution.py:31
  74.9 19.5 %collective-permute-start.15 = (bf16[192,1280]{1,0:T(8,128)(2,1)S(1)}, bf16[192,1280]{1,0:T(8,128)(2,1)S(1)}, u32[]{:S(2)}, u32[]{:S(2)}) collective-permute-start(bf16[192,1280]{1,0:T(8,128)(2,1)S(1)} %get-tuple-element.136), channel_id=1, source_target_pairs={{0,2},{1,3},{2,0},{3,1},{4,6},{5,7},{6,4},{7,5},{8,10},{9,11},{10,... | collective-permute-start | bytes 1474568 | tf_op jit(solution)/shard_map/ppermute | solution.py:49
  95.2 13.3 %collective-permute-start.16 = (bf16[512,256]{1,0:T(8,128)(2,1)}, bf16[512,256]{1,0:T(8,128)(2,1)}, u32[]{:S(2)}, u32[]{:S(2)}) collective-permute-start(bf16[512,256]{1,0:T(8,128)(2,1)} %slice.58), channel_id=1, source_target_pairs={{0,8},{4,12},{8,0},{12,4},{16,24},{20,28},{24,16},{28,20},{1,9},{5... | collective-permute-start | bytes 786440 | tf_op jit(solution)/shard_map/ppermute | solution.py:31
  99.0 24.3 %collective-permute-start.18 = (bf16[192,1280]{1,0:T(8,128)(2,1)}, bf16[192,1280]{1,0:T(8,128)(2,1)S(1)}, u32[]{:S(2)}, u32[]{:S(2)}) collective-permute-start(bf16[192,1280]{1,0:T(8,128)(2,1)} %get-tuple-element.144), channel_id=1, source_target_pairs={{0,2},{1,3},{2,0},{3,1},{4,6},{5,7},{6,4},{7,5},{8,10},{9,11},{10,... | collective-permute-start | bytes 1474568 | tf_op jit(solution)/shard_map/ppermute | solution.py:49
  112.0 19.4 %collective-permute-start.24 = (bf16[512,384]{1,0:T(8,128)(2,1)S(1)}, bf16[512,384]{1,0:T(8,128)(2,1)S(1)}, u32[]{:S(2)}, u32[]{:S(2)}) collective-permute-start(bf16[512,384]{1,0:T(8,128)(2,1)S(1)} %attend.3.refs_0_), channel_id=1, source_target_pairs={{0,1},{1,0},{2,3},{3,2},{4,5},{5,4},{6,7},{7,6},{8,9},{9,8},{10,11... | collective-permute-start | bytes 1179656 | tf_op jit(solution)/shard_map/ppermute | solution.py:64
  112.7 19.8 %collective-permute-start.25 = (bf16[512,384]{1,0:T(8,128)(2,1)S(1)}, bf16[512,384]{1,0:T(8,128)(2,1)S(1)}, u32[]{:S(2)}, u32[]{:S(2)}) collective-permute-start(bf16[512,384]{1,0:T(8,128)(2,1)S(1)} %attend.3.refs_0_), channel_id=1, source_target_pairs={{1,2},{2,1},{5,6},{6,5},{9,10},{10,9},{13,14},{14,13},{17,18},{18,... | collective-permute-start | bytes 1179656 | tf_op jit(solution)/shard_map/ppermute | solution.py:64
  123.3 17.5 %collective-permute-start.19 = (bf16[512,384]{1,0:T(8,128)(2,1)S(1)}, bf16[512,384]{1,0:T(8,128)(2,1)S(1)}, u32[]{:S(2)}, u32[]{:S(2)}) collective-permute-start(bf16[512,384]{1,0:T(8,128)(2,1)S(1)} %attend.2.refs_0_), channel_id=1, source_target_pairs={{0,1},{1,0},{2,3},{3,2},{4,5},{5,4},{6,7},{7,6},{8,9},{9,8},{10,11... | collective-permute-start | bytes 1179656 | tf_op jit(solution)/shard_map/ppermute | solution.py:64
  125.6 15.3 %collective-permute-start.20 = (bf16[512,384]{1,0:T(8,128)(2,1)S(1)}, bf16[512,384]{1,0:T(8,128)(2,1)S(1)}, u32[]{:S(2)}, u32[]{:S(2)}) collective-permute-start(bf16[512,384]{1,0:T(8,128)(2,1)S(1)} %attend.2.refs_0_), channel_id=1, source_target_pairs={{1,2},{2,1},{5,6},{6,5},{9,10},{10,9},{13,14},{14,13},{17,18},{18,... | collective-permute-start | bytes 1179656 | tf_op jit(solution)/shard_map/ppermute | solution.py:64
  132.5 16.7 %collective-permute-start.26 = (bf16[512,384]{1,0:T(8,128)(2,1)S(1)}, bf16[512,384]{1,0:T(8,128)(2,1)S(1)}, u32[]{:S(2)}, u32[]{:S(2)}) collective-permute-start(bf16[512,384]{1,0:T(8,128)(2,1)S(1)} %collective-permute-done.25.refs_2_), channel_id=1, source_target_pairs={{1,0},{2,3},{5,4},{6,7},{9,8},{10,11},{13,12},{14,15},{17,16},{18,... | collective-permute-start | bytes 1179656 | tf_op jit(solution)/shard_map/ppermute | solution.py:64
  136.6 13.4 %collective-permute-start.27 = (bf16[512,384]{1,0:T(8,128)(2,1)S(1)}, bf16[512,384]{1,0:T(8,128)(2,1)}, u32[]{:S(2)}, u32[]{:S(2)}) collective-permute-start(bf16[512,384]{1,0:T(8,128)(2,1)S(1)} %collective-permute-done.24.refs_1_), channel_id=1, source_target_pairs={{1,2},{2,1},{5,6},{6,5},{9,10},{10,9},{13,14},{14,13},{17,18},{18,... | collective-permute-start | bytes 1179656 | tf_op jit(solution)/shard_map/ppermute | solution.py:64
  140.9 15.8 %collective-permute-start.21 = (bf16[512,384]{1,0:T(8,128)(2,1)S(1)}, bf16[512,384]{1,0:T(8,128)(2,1)S(1)}, u32[]{:S(2)}, u32[]{:S(2)}) collective-permute-start(bf16[512,384]{1,0:T(8,128)(2,1)S(1)} %collective-permute-done.20.refs_2_), channel_id=1, source_target_pairs={{1,0},{2,3},{5,4},{6,7},{9,8},{10,11},{13,12},{14,15},{17,16},{18,... | collective-permute-start | bytes 1179656 | tf_op jit(solution)/shard_map/ppermute | solution.py:64
  145.0 12.8 %collective-permute-start.22 = (bf16[512,384]{1,0:T(8,128)(2,1)S(1)}, bf16[512,384]{1,0:T(8,128)(2,1)}, u32[]{:S(2)}, u32[]{:S(2)}) collective-permute-start(bf16[512,384]{1,0:T(8,128)(2,1)S(1)} %collective-permute-done.19.refs_1_), channel_id=1, source_target_pairs={{1,2},{2,1},{5,6},{6,5},{9,10},{10,9},{13,14},{14,13},{17,18},{18,... | collective-permute-start | bytes 1179656 | tf_op jit(solution)/shard_map/ppermute | solution.py:64
  150.0 15.3 %collective-permute-start.28 = (bf16[512,384]{1,0:T(8,128)(2,1)}, bf16[512,384]{1,0:T(8,128)(2,1)}, u32[]{:S(2)}, u32[]{:S(2)}) collective-permute-start(bf16[512,384]{1,0:T(8,128)(2,1)} %collective-permute-done.27.refs_4_), channel_id=1, source_target_pairs={{1,0},{2,3},{5,4},{6,7},{9,8},{10,11},{13,12},{14,15},{17,16},{18,... | collective-permute-start | bytes 1179656 | tf_op jit(solution)/shard_map/ppermute | solution.py:64
  157.8 15.8 %collective-permute-start.23 = (bf16[512,384]{1,0:T(8,128)(2,1)}, bf16[512,384]{1,0:T(8,128)(2,1)}, u32[]{:S(2)}, u32[]{:S(2)}) collective-permute-start(bf16[512,384]{1,0:T(8,128)(2,1)} %collective-permute-done.22.refs_4_), channel_id=1, source_target_pairs={{1,0},{2,3},{5,4},{6,7},{9,8},{10,11},{13,12},{14,15},{17,16},{18,... | collective-permute-start | bytes 1179656 | tf_op jit(solution)/shard_map/ppermute | solution.py:64
  197.2 16.6 %all-to-all-start = ((bf16[8,1,32,1280]{3,2,1,0:T(8,128)(2,1)}), bf16[8,1,32,1280]{3,2,1,0:T(8,128)(2,1)S(1)}, u32[]{:S(2)}, u32[]{:S(2)}) async-start(bf16[8,1,32,1280]{3,2,1,0:T(8,128)(2,1)} %bitcast.21), calls=%async_computation | async-start | bytes 1310720 | tf_op jit(solution)/shard_map/all_to_all | solution.py:701
  213.8 14.4 %collective-permute-start.30 = (bf16[256,1280]{1,0:T(8,128)(2,1)S(1)}, bf16[256,1280]{1,0:T(8,128)(2,1)S(1)}, u32[]{:S(2)}, u32[]{:S(2)}) collective-permute-start(bf16[256,1280]{1,0:T(8,128)(2,1)S(1)} %bitcast.80), channel_id=1, source_target_pairs={{0,1},{1,0},{2,3},{3,2},{4,5},{5,4},{6,7},{7,6},{8,9},{9,8},{10,11... | collective-permute-start | bytes 1966088 | tf_op jit(solution)/shard_map/ppermute | solution.py:64
  216.3 15.3 %collective-permute-start.31 = (bf16[256,1280]{1,0:T(8,128)(2,1)S(1)}, bf16[256,1280]{1,0:T(8,128)(2,1)S(1)}, u32[]{:S(2)}, u32[]{:S(2)}) collective-permute-start(bf16[256,1280]{1,0:T(8,128)(2,1)S(1)} %bitcast.81), channel_id=1, source_target_pairs={{1,2},{2,1},{5,6},{6,5},{9,10},{10,9},{13,14},{14,13},{17,18},{18,... | collective-permute-start | bytes 1966088 | tf_op jit(solution)/shard_map/ppermute | solution.py:64
  233.7 14.5 %collective-permute-start.33 = (bf16[256,1280]{1,0:T(8,128)(2,1)S(1)}, bf16[256,1280]{1,0:T(8,128)(2,1)}, u32[]{:S(2)}, u32[]{:S(2)}) collective-permute-start(bf16[256,1280]{1,0:T(8,128)(2,1)S(1)} %collective-permute-done.30.refs_0_), channel_id=1, source_target_pairs={{1,2},{2,1},{5,6},{6,5},{9,10},{10,9},{13,14},{14,13},{17,18},{18,... | collective-permute-start | bytes 1966088 | tf_op jit(solution)/shard_map/ppermute | solution.py:64
  238.4 16.0 %all-to-all-start.1 = ((bf16[8,1,32,1280]{3,2,1,0:T(8,128)(2,1)}), bf16[8,1,32,1280]{3,2,1,0:T(8,128)(2,1)S(1)}, u32[]{:S(2)}, u32[]{:S(2)}) async-start(bf16[8,1,32,1280]{3,2,1,0:T(8,128)(2,1)} %bitcast.86), calls=%async_computation.1 | async-start | bytes 1310720 | tf_op jit(solution)/shard_map/all_to_all | solution.py:701
  254.4 22.1 %collective-permute-start.34 = (bf16[256,1280]{1,0:T(8,128)(2,1)}, bf16[256,1280]{1,0:T(8,128)(2,1)}, u32[]{:S(2)}, u32[]{:S(2)}) collective-permute-start(bf16[256,1280]{1,0:T(8,128)(2,1)} %collective-permute-done.33.refs_0_), channel_id=1, source_target_pairs={{1,0},{2,3},{5,4},{6,7},{9,8},{10,11},{13,12},{14,15},{17,16},{18,... | collective-permute-start | bytes 1966088 | tf_op jit(solution)/shard_map/ppermute | solution.py:64
  276.5 18.9 %collective-permute-start.38 = (bf16[256,1280]{1,0:T(8,128)(2,1)S(1)}, bf16[256,1280]{1,0:T(8,128)(2,1)S(1)}, u32[]{:S(2)}, u32[]{:S(2)}) collective-permute-start(bf16[256,1280]{1,0:T(8,128)(2,1)S(1)} %bitcast.78), channel_id=1, source_target_pairs={{0,1},{1,0},{2,3},{3,2},{4,5},{5,4},{6,7},{7,6},{8,9},{9,8},{10,11... | collective-permute-start | bytes 1966088 | tf_op jit(solution)/shard_map/ppermute | solution.py:64
  276.6 18.8 %collective-permute-start.39 = (bf16[256,1280]{1,0:T(8,128)(2,1)S(1)}, bf16[256,1280]{1,0:T(8,128)(2,1)S(1)}, u32[]{:S(2)}, u32[]{:S(2)}) collective-permute-start(bf16[256,1280]{1,0:T(8,128)(2,1)S(1)} %bitcast.79), channel_id=1, source_target_pairs={{1,2},{2,1},{5,6},{6,5},{9,10},{10,9},{13,14},{14,13},{17,18},{18,... | collective-permute-start | bytes 1966088 | tf_op jit(solution)/shard_map/ppermute | solution.py:64
  294.1 15.3 %collective-permute-start.35 = (bf16[256,1280]{1,0:T(8,128)(2,1)S(1)}, bf16[256,1280]{1,0:T(8,128)(2,1)S(1)}, u32[]{:S(2)}, u32[]{:S(2)}) collective-permute-start(bf16[256,1280]{1,0:T(8,128)(2,1)S(1)} %get-tuple-element.231), channel_id=1, source_target_pairs={{0,1},{3,2},{4,5},{7,6},{8,9},{11,10},{12,13},{15,14},{16,17},{19,... | collective-permute-start | bytes 1966088 | tf_op jit(solution)/shard_map/ppermute | solution.py:64
  301.0 15.2 %collective-permute-start.40 = (bf16[256,1280]{1,0:T(8,128)(2,1)S(1)}, bf16[256,1280]{1,0:T(8,128)(2,1)S(1)}, u32[]{:S(2)}, u32[]{:S(2)}) collective-permute-start(bf16[256,1280]{1,0:T(8,128)(2,1)S(1)} %collective-permute-done.39.refs_1_), channel_id=1, source_target_pairs={{1,0},{2,3},{5,4},{6,7},{9,8},{10,11},{13,12},{14,15},{17,16},{18,... | collective-permute-start | bytes 1966088 | tf_op jit(solution)/shard_map/ppermute | solution.py:64
  305.7 19.6 %collective-permute-start.41 = (bf16[256,1280]{1,0:T(8,128)(2,1)S(1)}, bf16[256,1280]{1,0:T(8,128)(2,1)S(1)}, u32[]{:S(2)}, u32[]{:S(2)}) collective-permute-start(bf16[256,1280]{1,0:T(8,128)(2,1)S(1)} %collective-permute-done.38.refs_0_), channel_id=1, source_target_pairs={{1,2},{2,1},{5,6},{6,5},{9,10},{10,9},{13,14},{14,13},{17,18},{18,... | collective-permute-start | bytes 1966088 | tf_op jit(solution)/shard_map/ppermute | solution.py:64
  309.5 24.9 %collective-permute-start.36 = (bf16[256,1280]{1,0:T(8,128)(2,1)S(1)}, bf16[256,1280]{1,0:T(8,128)(2,1)S(1)}, u32[]{:S(2)}, u32[]{:S(2)}) collective-permute-start(bf16[256,1280]{1,0:T(8,128)(2,1)S(1)} %add_convert_fusion.4), channel_id=1, source_target_pairs={{1,2},{2,1},{5,6},{6,5},{9,10},{10,9},{13,14},{14,13},{17,18},{18,... | collective-permute-start | bytes 1966088 | tf_op jit(solution)/shard_map/ppermute | solution.py:64
  312.8 21.9 %collective-permute-start.37 = (bf16[256,1280]{1,0:T(8,128)(2,1)S(1)}, bf16[256,1280]{1,0:T(8,128)(2,1)S(1)}, u32[]{:S(2)}, u32[]{:S(2)}) collective-permute-start(bf16[256,1280]{1,0:T(8,128)(2,1)S(1)} %get-tuple-element.197), channel_id=1, source_target_pairs={{0,1},{3,2},{4,5},{7,6},{8,9},{11,10},{12,13},{15,14},{16,17},{19,... | collective-permute-start | bytes 1966088 | tf_op jit(solution)/shard_map/ppermute | solution.py:64
  325.2 18.6 %collective-permute-start.44 = (bf16[256,1280]{1,0:T(8,128)(2,1)S(1)}, bf16[256,1280]{1,0:T(8,128)(2,1)S(1)}, u32[]{:S(2)}, u32[]{:S(2)}) collective-permute-start(bf16[256,1280]{1,0:T(8,128)(2,1)S(1)} %collective-permute-done.41.refs_0_), channel_id=1, source_target_pairs={{1,0},{2,3},{5,4},{6,7},{9,8},{10,11},{13,12},{14,15},{17,16},{18,... | collective-permute-start | bytes 1966088 | tf_op jit(solution)/shard_map/ppermute | solution.py:64
  340.5 16.3 %collective-permute-start.43 = (bf16[256,1280]{1,0:T(8,128)(2,1)S(1)}, bf16[256,1280]{1,0:T(8,128)(2,1)S(1)}, u32[]{:S(2)}, u32[]{:S(2)}) collective-permute-start(bf16[256,1280]{1,0:T(8,128)(2,1)S(1)} %add_convert_fusion.3), channel_id=1, source_target_pairs={{1,2},{2,1},{5,6},{6,5},{9,10},{10,9},{13,14},{14,13},{17,18},{18,... | collective-permute-start | bytes 1966088 | tf_op jit(solution)/shard_map/ppermute | solution.py:64
  343.8 13.0 %collective-permute-start.42 = (bf16[256,1280]{1,0:T(8,128)(2,1)S(1)}, bf16[256,1280]{1,0:T(8,128)(2,1)S(1)}, u32[]{:S(2)}, u32[]{:S(2)}) collective-permute-start(bf16[256,1280]{1,0:T(8,128)(2,1)S(1)} %fusion.3), channel_id=1, source_target_pairs={{0,1},{1,0},{2,3},{3,2},{4,5},{5,4},{6,7},{7,6},{8,9},{9,8},{10,11... | collective-permute-start | bytes 1966088 | tf_op jit(solution)/shard_map/ppermute | solution.py:64
  360.6 13.5 %collective-permute-start.45 = (bf16[256,1280]{1,0:T(8,128)(2,1)S(1)}, bf16[256,1280]{1,0:T(8,128)(2,1)S(1)}, u32[]{:S(2)}, u32[]{:S(2)}) collective-permute-start(bf16[256,1280]{1,0:T(8,128)(2,1)S(1)} %get-tuple-element.230), channel_id=1, source_target_pairs={{0,1},{3,2},{4,5},{7,6},{8,9},{11,10},{12,13},{15,14},{16,17},{19,... | collective-permute-start | bytes 1966088 | tf_op jit(solution)/shard_map/ppermute | solution.py:64
  375.1 12.9 %collective-permute-start.46 = (bf16[256,1280]{1,0:T(8,128)(2,1)}, bf16[256,1280]{1,0:T(8,128)(2,1)}, u32[]{:S(2)}, u32[]{:S(2)}) collective-permute-start(bf16[256,1280]{1,0:T(8,128)(2,1)} %add_convert_fusion.2), channel_id=1, source_target_pairs={{1,2},{2,1},{5,6},{6,5},{9,10},{10,9},{13,14},{14,13},{17,18},{18,... | collective-permute-start | bytes 1966088 | tf_op jit(solution)/shard_map/ppermute | solution.py:64
  379.0 18.7 %all-to-all-start.2 = ((bf16[8,1,32,1280]{3,2,1,0:T(8,128)(2,1)}), bf16[8,1,32,1280]{3,2,1,0:T(8,128)(2,1)S(1)}, u32[]{:S(2)}, u32[]{:S(2)}) async-start(bf16[8,1,32,1280]{3,2,1,0:T(8,128)(2,1)} %bitcast.35), calls=%async_computation.2 | async-start | bytes 1310720 | tf_op jit(solution)/shard_map/all_to_all | solution.py:688
  397.7 15.8 %collective-permute-start.49 = (bf16[256,1280]{1,0:T(8,128)(2,1)}, bf16[256,1280]{1,0:T(8,128)(2,1)S(1)}, u32[]{:S(2)}, u32[]{:S(2)}) collective-permute-start(bf16[256,1280]{1,0:T(8,128)(2,1)} %add_convert_fusion.1), channel_id=1, source_target_pairs={{1,2},{2,1},{5,6},{6,5},{9,10},{10,9},{13,14},{14,13},{17,18},{18,... | collective-permute-start | bytes 1966088 | tf_op jit(solution)/shard_map/ppermute | solution.py:64
  401.1 13.7 %collective-permute-start.48 = (bf16[256,1280]{1,0:T(8,128)(2,1)}, bf16[256,1280]{1,0:T(8,128)(2,1)S(1)}, u32[]{:S(2)}, u32[]{:S(2)}) collective-permute-start(bf16[256,1280]{1,0:T(8,128)(2,1)} %fusion), channel_id=1, source_target_pairs={{0,1},{1,0},{2,3},{3,2},{4,5},{5,4},{6,7},{7,6},{8,9},{9,8},{10,11... | collective-permute-start | bytes 1966088 | tf_op jit(solution)/shard_map/ppermute | solution.py:64
  415.9 16.1 %all-to-all-start.3 = ((bf16[8,1,32,1280]{3,2,1,0:T(8,128)(2,1)}), bf16[8,1,32,1280]{3,2,1,0:T(8,128)(2,1)S(1)}, u32[]{:S(2)}, u32[]{:S(2)}) async-start(bf16[8,1,32,1280]{3,2,1,0:T(8,128)(2,1)} %bitcast.84), calls=%async_computation.3 | async-start | bytes 1310720 | tf_op jit(solution)/shard_map/all_to_all | solution.py:688
  (56 other events, 531.7 us)

commit v4 on v3

--- a/solution.py
+++ b/solution.py
@@ -563,28 +563,29 @@
     normed = [norm_rows(t, attn_gain) for t in (tokens, other_tokens)]
     sent = next_block(take)
     following = next_block(take_query)
+    moved = move(sent)
     kv_near = together(
-        near_blocks(kv_mats), *move(sent), *ready(following), other_tokens, normed[0], own_tokens
+        near_blocks(kv_mats), *ready(following), other_tokens, normed[0], own_tokens
     )
     first = kv_near[2]
     sent, following = following, next_block(first)
     kv_total = project_near(kv_mats, kv_near)
     kv_far, query_near, kv_total = together(
         (far_block(kv_near), near_blocks(after(query_mats, first)), kv_total),
-        *move(sent, first),
+        *move(sent, first, *moved),
         *ready(following),
     )
     before, first = first, query_near[2]
     sent, following = following, next_block(before)
     kv_pair = jnp.concatenate(project_far(kv_far, kv_total), axis=0)
     query_total = project_near(query_mats, query_near)
+    moved = move(sent, first)
     block_near, query_far, query_total = together(
         (near_blocks(kv_pair), far_block(query_near), query_total),
-        *move(sent, first),
         *ready(following),
     )
     first = block_near[2]
-    last_move = move(following, first)
+    last_move = move(following, first, *moved)
     out_parts[0] = [out_block(0, 0, query_width, after(parity * query_width, first))]
     block_far = far_block(block_near)
     queries = project_far(query_far, query_total)

time: 444 us -> 434 us (0.977)
  waiting for transfers between devices: 132 us -> 126 us
    ppermute x16, waiting for transfers between devices: 18.8 us -> 13.6 us  [swap(): return lax.ppermute(value, axis, [(i, i ^ offset) for i in range(count)])]
    ppermute x4, waiting for transfers between devices: 10.7 us -> 5.49 us  [ring_shift(): lax.ppermute(values, 'hx', [(j, (j + k) % count) for j in range(count)])]
    ppermute x30, waiting for transfers between devices: 71 us -> 76 us  [pass_on(): lax.ppermute(values, 'hx', pairs)]
    ppermute x30, starting transfers between devices: 75.7 us -> 71.2 us  [pass_on(): lax.ppermute(values, 'hx', pairs)]
  transfers between devices with their start and end apart: 54 -> 54, of which waited for: 35 -> 36; matrix products, arithmetic and copies ran while one was open for 7% -> 8% of each run, Pallas kernels for 22% -> 23%
where the time goes in v4:
time: 434 us; the launch traced here: 425 us
  waiting for transfers between devices  126 us (29%)
  starting transfers between devices  116 us (27%)
  Pallas kernels  114 us (26%)
  local copies, waits for them, and re-layouts  45.3 us (10%)
  other arithmetic  13.7 us (3%)
  matrix products  9.11 us (2%)
    ppermute x30, waiting for transfers between devices, pass_on(): lax.ppermute(values, 'hx', pairs)  76 us
    ppermute x30, starting transfers between devices, pass_on(): lax.ppermute(values, 'hx', pairs)  71.2 us
    pallas_call x6, Pallas kernels, expert_share(): pl.pallas_call(functools.partial(share_kernel, shares=len(shares), added=...  33 us
    pallas_call x2, Pallas kernels, expert_finish(): pl.pallas_call(functools.partial(finish_kernel, shares=len(shares), tiles...  26.3 us
    unnamed x101, local copies, waits for them, and re-layouts  23.7 us
    pallas_call x4, Pallas kernels, project(): pl.pallas_call(functools.partial(project_kernel, count=len(values), mats=...  22 us
    all_to_all x2, waiting for transfers between devices, take_rows(): taken = lax.all_to_all(sent, 'ctx', split_axis=0, concat_axis=0, tiled=True)  16.5 us
    ppermute x16, starting transfers between devices, swap(): return lax.ppermute(value, axis, [(i, i ^ offset) for i in range(count)])  15.2 us
  transfers between devices with their start and end apart: 54, of which 36 were waited for; matrix products, arithmetic and copies ran while one was open for 8% of the time, Pallas kernels for 23%

profile of v4, /device:TPU:16, one launch (start us, length us, event | category | flops | bytes accessed | tf_op | source)
XLA Modules:
  0.0 425.2 jit_solution(955617052112274760)
XLA Ops:
  5.9 3.8 fusion.32
  17.1 5.1 %norm_rows.2.refs_0_.refs_1_.refs_2_ = bf16[512,5120]{1,0:T(8,128)(2,1)S(1)} custom-call(bf16[512,5120]{1,0:T(8,128)(2,1)} %values_ref.1, bf16[1,5120]{1,0:T(2,128)(2,1)S(1)} %reshape.82.gains_ref), custom_call_target="tpu_custom_call" | custom-call | bytes 4096 | tf_op jit(solution)/shard_map/norm_rows/pallas_call | solution.py:135
  40.0 5.0 %norm_rows.3.refs_3_.refs_4_.refs_5_.refs_2_ = bf16[512,5120]{1,0:T(8,128)(2,1)S(1)} custom-call(bf16[512,5120]{1,0:T(8,128)(2,1)} %collective-permute-done.2.values_ref, bf16[1,5120]{1,0:T(2,128)(2,1)S(1)} %reshape.82.gains_ref), custom_call_target="tpu_custom_call" | custom-call | bytes 4096 | tf_op jit(solution)/shard_map/norm_rows/pallas_call | solution.py:135
  47.3 6.2 %project.4 = (f32[512,256]{1,0:T(8,128)S(1)}, f32[512,256]{1,0:T(8,128)S(1)}) custom-call(s32[3]{0:T(128)S(1)} %pad_add_fusion.1.places_ref, bf16[512,5120]{1,0:T(8,128)(2,1)} %copy-done.2, bf16[512,5120]{1,0:T(8,128)(2,1)} %copy-done.2, bf16[512,5120]{1,0:T(8,128)(2,1)} %copy-done.2, bf16[512,5120]{1,0:T(8,128)(2,1)} %copy-done.3, ...), custom_call_target="tpu_custom_call" | custom-call | bytes 4096 | tf_op jit(solution)/shard_map/project/pallas_call | solution.py:231
  59.1 3.4 project.5
  71.3 8.6 %project.6 = (f32[512,384]{1,0:T(8,128)S(1)}, f32[512,384]{1,0:T(8,128)S(1)}) custom-call(s32[3]{0:T(128)S(1)} %pad_add_fusion.1.places_ref, bf16[512,5120]{1,0:T(8,128)(2,1)} %copy-done.2, bf16[512,5120]{1,0:T(8,128)(2,1)} %copy-done.2, bf16[512,5120]{1,0:T(8,128)(2,1)} %copy-done.2, bf16[512,5120]{1,0:T(8,128)(2,1)} %copy-done.3, ...), custom_call_target="tpu_custom_call" | custom-call | bytes 4096 | tf_op jit(solution)/shard_map/project/pallas_call | solution.py:231
  81.6 2.9 collective-permute-done.13.refs_4_
  95.3 3.9 project.7
  99.3 3.5 attend.3.refs_0_
  102.8 3.1 collective-permute-start.25
  106.0 4.6 %attend.2.refs_0_ = bf16[512,384]{1,0:T(8,128)(2,1)S(1)} custom-call(s32[9]{0:T(128)S(1)} %stack.83.places_ref, bf16[512,384]{1,0:T(8,128)(2,1)S(1)} %get-tuple-element.140.query_ref, bf16[1024,256]{1,0:T(8,128)(2,1)S(1)} %copy-done.37, bf16[1024,256]{1,0:T(8,128)(2,1)S(1)} %copy-done.33, bf16[1024,256]{1,0:T(8,128)(2,1)S(1)} %copy-done.35, ...), custom_call_target="tpu_custom_call" | custom-call | flops 3221225472 | bytes 2097152 | tf_op jit(solution)/shard_map/attend/pallas_call | solution.py:312
  110.6 3.1 collective-permute-done.18.refs_9_
  113.6 3.2 collective-permute-start.19
  123.8 3.2 collective-permute-start.26
  132.2 3.3 collective-permute-start.21
  140.7 4.7 %collective-permute-start.28 = (bf16[512,384]{1,0:T(8,128)(2,1)}, bf16[512,384]{1,0:T(8,128)(2,1)}, u32[]{:S(2)}, u32[]{:S(2)}) collective-permute-start(bf16[512,384]{1,0:T(8,128)(2,1)} %collective-permute-done.27.refs_4_), channel_id=1, source_target_pairs={{1,0},{2,3},{5,4},{6,7},{9,8},{10,11},{13,12},{14,15},{17,16},{18,... | collective-permute-start | bytes 1179656 | tf_op jit(solution)/shard_map/ppermute | solution.py:64
  149.2 4.6 %collective-permute-start.23 = (bf16[512,384]{1,0:T(8,128)(2,1)}, bf16[512,384]{1,0:T(8,128)(2,1)}, u32[]{:S(2)}, u32[]{:S(2)}) collective-permute-start(bf16[512,384]{1,0:T(8,128)(2,1)} %collective-permute-done.22.refs_4_), channel_id=1, source_target_pairs={{1,0},{2,3},{5,4},{6,7},{9,8},{10,11},{13,12},{14,15},{17,16},{18,... | collective-permute-start | bytes 1179656 | tf_op jit(solution)/shard_map/ppermute | solution.py:64
  156.4 8.4 %collective-permute-done.23.refs_5_ = bf16[512,384]{1,0:T(8,128)(2,1)} collective-permute-done((bf16[512,384]{1,0:T(8,128)(2,1)}, bf16[512,384]{1,0:T(8,128)(2,1)}, u32[]{:S(2)}, u32[]{:S(2)}) %collective-permute-start.23) | collective-permute-done | bytes 393248 | tf_op jit(solution)/shard_map/ppermute | solution.py:64
  164.9 7.0 %sum_dots.2 = bf16[512,1280]{1,0:T(8,128)(2,1)} custom-call(s32[4]{0:T(128)S(1)} %fusion.27.codes_ref, bf16[512,384]{1,0:T(8,128)(2,1)S(1)} %copy-done.25, bf16[512,384]{1,0:T(8,128)(2,1)S(1)} %copy-done.27, bf16[512,384]{1,0:T(8,128)(2,1)S(1)} %copy-done.29, bf16[512,384]{1,0:T(8,128)(2,1)S(1)} %copy-done.31, ...), custom_call_target="tpu_custom_call" | custom-call | bytes 4096 | tf_op jit(solution)/shard_map/sum_dots/pallas_call | solution.py:188
  178.2 7.5 %sum_dots.3 = bf16[512,1280]{1,0:T(8,128)(2,1)} custom-call(s32[4]{0:T(128)S(1)} %fusion.27.codes_ref, bf16[512,384]{1,0:T(8,128)(2,1)S(1)} %attend.3.refs_0_, bf16[512,384]{1,0:T(8,128)(2,1)S(1)} %copy-done.19, bf16[512,384]{1,0:T(8,128)(2,1)S(1)} %copy-done.21, bf16[512,384]{1,0:T(8,128)(2,1)S(1)} %copy-done.23, ...), custom_call_target="tpu_custom_call" | custom-call | bytes 4096 | tf_op jit(solution)/shard_map/sum_dots/pallas_call | solution.py:188
  188.5 4.7 %all-to-all-start = ((bf16[8,1,32,1280]{3,2,1,0:T(8,128)(2,1)}), bf16[8,1,32,1280]{3,2,1,0:T(8,128)(2,1)S(1)}, u32[]{:S(2)}, u32[]{:S(2)}) async-start(bf16[8,1,32,1280]{3,2,1,0:T(8,128)(2,1)} %bitcast.21), calls=%async_computation | async-start | bytes 1310720 | tf_op jit(solution)/shard_map/all_to_all | solution.py:702
  193.3 11.1 %all-to-all-done = bf16[8,1,32,1280]{3,2,1,0:T(8,128)(2,1)S(1)} async-done(((bf16[8,1,32,1280]{3,2,1,0:T(8,128)(2,1)}), bf16[8,1,32,1280]{3,2,1,0:T(8,128)(2,1)S(1)}, u32[]{:S(2)}, u32[]{:S(2)}) %all-to-all-start) | async-done | bytes 655392 | tf_op jit(solution)/shard_map/all_to_all | solution.py:702
  209.4 5.3 %expert_share.6 = (f32[256,1024]{1,0:T(8,128)S(1)}, f32[256,1024]{1,0:T(8,128)S(1)}, f32[256,128]{1,0:T(8,128)S(1)}, f32[256,128]{1,0:T(8,128)S(1)}) custom-call(s32[3]{0:T(128)S(1)} %add_add_fusion.code_ref, bf16[256,1280]{1,0:T(8,128)(2,1)S(1)} %bitcast.82, bf16[1,5120]{1,0:T(2,128)(2,1)S(1)} %reshape.85.refs_1_.refs_2_.refs_3_, ...), custom_call_target="tpu_custom_call" | custom-call | bytes 4096 | tf_op jit(solution)/shard_map/expert_share/pallas_call | solution.py:369
  215.7 3.1 collective-permute-done.30.refs_0_
  218.8 3.3 collective-permute-done.31.refs_1_
  228.1 4.8 %all-to-all-start.1 = ((bf16[8,1,32,1280]{3,2,1,0:T(8,128)(2,1)}), bf16[8,1,32,1280]{3,2,1,0:T(8,128)(2,1)S(1)}, u32[]{:S(2)}, u32[]{:S(2)}) async-start(bf16[8,1,32,1280]{3,2,1,0:T(8,128)(2,1)} %bitcast.86), calls=%async_computation.1 | async-start | bytes 1310720 | tf_op jit(solution)/shard_map/all_to_all | solution.py:702
  233.7 5.0 %collective-permute-done.33.refs_0_ = bf16[256,1280]{1,0:T(8,128)(2,1)} collective-permute-done((bf16[256,1280]{1,0:T(8,128)(2,1)S(1)}, bf16[256,1280]{1,0:T(8,128)(2,1)}, u32[]{:S(2)}, u32[]{:S(2)}) %collective-permute-start.33) | collective-permute-done | bytes 655392 | tf_op jit(solution)/shard_map/ppermute | solution.py:64
  238.8 5.4 %all-to-all-done.1 = bf16[8,1,32,1280]{3,2,1,0:T(8,128)(2,1)S(1)} async-done(((bf16[8,1,32,1280]{3,2,1,0:T(8,128)(2,1)}), bf16[8,1,32,1280]{3,2,1,0:T(8,128)(2,1)S(1)}, u32[]{:S(2)}, u32[]{:S(2)}) %all-to-all-start.1) | async-done | bytes 655392 | tf_op jit(solution)/shard_map/all_to_all | solution.py:702
  248.7 5.3 %expert_share.7 = (f32[256,1024]{1,0:T(8,128)S(1)}, f32[256,1024]{1,0:T(8,128)S(1)}, f32[256,128]{1,0:T(8,128)S(1)}, f32[256,128]{1,0:T(8,128)S(1)}) custom-call(s32[3]{0:T(128)S(1)} %add_add_fusion.code_ref, bf16[256,1280]{1,0:T(8,128)(2,1)S(1)} %bitcast.77, bf16[1,5120]{1,0:T(2,128)(2,1)S(1)} %reshape.85.refs_1_.refs_2_.refs_3_, ...), custom_call_target="tpu_custom_call" | custom-call | bytes 4096 | tf_op jit(solution)/shard_map/expert_share/pallas_call | solution.py:369
  254.0 5.4 %expert_share.8 = (f32[256,1024]{1,0:T(8,128)S(1)}, f32[256,1024]{1,0:T(8,128)S(1)}, f32[256,128]{1,0:T(8,128)S(1)}, f32[256,128]{1,0:T(8,128)S(1)}) custom-call(s32[3]{0:T(128)S(1)} %pad_add_fusion.4.code_ref, bf16[256,1280]{1,0:T(8,128)(2,1)S(1)} %collective-permute-done.30.refs_0_, bf16[256,1280]{1,0:T(8,128)(2,1)S(1)} %collective-permute-done.31.refs_1_, ...), custom_call_target="tpu_custom_call" | custom-call | bytes 4096 | tf_op jit(solution)/shard_map/expert_share/pallas_call | solution.py:369
  260.4 5.8 %expert_share.9 = (f32[256,1024]{1,0:T(8,128)S(1)}, f32[256,1024]{1,0:T(8,128)S(1)}, f32[256,128]{1,0:T(8,128)S(1)}, f32[256,128]{1,0:T(8,128)S(1)}) custom-call(s32[3]{0:T(128)S(1)} %get-tuple-element.244.code_ref, bf16[256,1280]{1,0:T(8,128)(2,1)S(1)} %collective-permute-done.30.refs_0_, bf16[256,1280]{1,0:T(8,128)(2,1)S(1)} %collective-permute-done.31.refs_1_, ...), custom_call_target="tpu_custom_call" | custom-call | bytes 4096 | tf_op jit(solution)/shard_map/expert_share/pallas_call | solution.py:369
  266.3 3.4 collective-permute-start.39
  269.7 13.3 %expert_finish.2 = bf16[4,256,1280]{2,1,0:T(8,128)(2,1)} custom-call(s32[3]{0:T(128)S(1)} %get-tuple-element.243.code_ref, bf16[256,1280]{1,0:T(8,128)(2,1)} %collective-permute-done.33.refs_0_, bf16[256,1280]{1,0:T(8,128)(2,1)} %collective-permute-done.34.refs_1_, bf16[1,5120]{1,0:T(2,128)(2,1)S(1)} %reshape.85.refs_1_.refs_2_.refs_3_, ...), custom_call_target="tpu_custom_call" | custom-call | bytes 4096 | tf_op jit(solution)/shard_map/expert_finish/pallas_call | solution.py:433
  286.0 5.6 %expert_share.10 = (f32[256,1024]{1,0:T(8,128)S(1)}, f32[256,1024]{1,0:T(8,128)S(1)}, f32[256,128]{1,0:T(8,128)S(1)}, f32[256,128]{1,0:T(8,128)S(1)}) custom-call(s32[3]{0:T(128)S(1)} %pad_add_fusion.4.code_ref, bf16[256,1280]{1,0:T(8,128)(2,1)S(1)} %collective-permute-done.38.refs_0_, bf16[256,1280]{1,0:T(8,128)(2,1)S(1)} %collective-permute-done.39.refs_1_, ...), custom_call_target="tpu_custom_call" | custom-call | bytes 4096 | tf_op jit(solution)/shard_map/expert_share/pallas_call | solution.py:369
  291.6 4.6 %collective-permute-start.40 = (bf16[256,1280]{1,0:T(8,128)(2,1)S(1)}, bf16[256,1280]{1,0:T(8,128)(2,1)S(1)}, u32[]{:S(2)}, u32[]{:S(2)}) collective-permute-start(bf16[256,1280]{1,0:T(8,128)(2,1)S(1)} %collective-permute-done.39.refs_1_), channel_id=1, source_target_pairs={{1,0},{2,3},{5,4},{6,7},{9,8},{10,11},{13,12},{14,15},{17,16},{18,... | collective-permute-start | bytes 1966088 | tf_op jit(solution)/shard_map/ppermute | solution.py:64
  303.8 3.0 collective-permute-done.40.refs_2_
  306.8 9.0 %collective-permute-done.41.refs_0_ = bf16[256,1280]{1,0:T(8,128)(2,1)S(1)} collective-permute-done((bf16[256,1280]{1,0:T(8,128)(2,1)S(1)}, bf16[256,1280]{1,0:T(8,128)(2,1)S(1)}, u32[]{:S(2)}, u32[]{:S(2)}) %collective-permute-start.41) | collective-permute-done | bytes 655392 | tf_op jit(solution)/shard_map/ppermute | solution.py:64
  317.1 7.9 %collective-permute-done.36 = bf16[256,1280]{1,0:T(8,128)(2,1)S(1)} collective-permute-done((bf16[256,1280]{1,0:T(8,128)(2,1)S(1)}, bf16[256,1280]{1,0:T(8,128)(2,1)S(1)}, u32[]{:S(2)}, u32[]{:S(2)}) %collective-permute-start.36) | collective-permute-done | bytes 655392 | tf_op jit(solution)/shard_map/ppermute | solution.py:64
  325.4 5.6 %expert_share.11 = (f32[256,1024]{1,0:T(8,128)S(1)}, f32[256,1024]{1,0:T(8,128)S(1)}, f32[256,128]{1,0:T(8,128)S(1)}, f32[256,128]{1,0:T(8,128)S(1)}) custom-call(s32[3]{0:T(128)S(1)} %get-tuple-element.244.code_ref, bf16[256,1280]{1,0:T(8,128)(2,1)S(1)} %collective-permute-done.38.refs_0_, bf16[256,1280]{1,0:T(8,128)(2,1)S(1)} %collective-permute-done.39.refs_1_, ...), custom_call_target="tpu_custom_call" | custom-call | bytes 4096 | tf_op jit(solution)/shard_map/expert_share/pallas_call | solution.py:369
  333.6 13.0 %expert_finish.3 = bf16[4,256,1280]{2,1,0:T(8,128)(2,1)} custom-call(s32[3]{0:T(128)S(1)} %get-tuple-element.243.code_ref, bf16[256,1280]{1,0:T(8,128)(2,1)S(1)} %collective-permute-done.41.refs_0_, bf16[256,1280]{1,0:T(8,128)(2,1)S(1)} %collective-permute-done.44.refs_1_, bf16[1,5120]{1,0:T(2,128)(2,1)S(1)} %reshape.85.refs_1_.refs_2_.refs_3_, ...), custom_call_target="tpu_custom_call" | custom-call | bytes 4096 | tf_op jit(solution)/shard_map/expert_finish/pallas_call | solution.py:433
  351.6 12.2 %collective-permute-done.45 = bf16[256,1280]{1,0:T(8,128)(2,1)S(1)} collective-permute-done((bf16[256,1280]{1,0:T(8,128)(2,1)S(1)}, bf16[256,1280]{1,0:T(8,128)(2,1)S(1)}, u32[]{:S(2)}, u32[]{:S(2)}) %collective-permute-start.45) | collective-permute-done | bytes 655392 | tf_op jit(solution)/shard_map/ppermute | solution.py:64
  364.8 3.4 collective-permute-start.46
  369.5 7.7 %all-to-all-start.2 = ((bf16[8,1,32,1280]{3,2,1,0:T(8,128)(2,1)}), bf16[8,1,32,1280]{3,2,1,0:T(8,128)(2,1)S(1)}, u32[]{:S(2)}, u32[]{:S(2)}) async-start(bf16[8,1,32,1280]{3,2,1,0:T(8,128)(2,1)} %bitcast.35), calls=%async_computation.2 | async-start | bytes 1310720 | tf_op jit(solution)/shard_map/all_to_all | solution.py:689
  383.1 5.3 %all-to-all-done.2 = bf16[8,1,32,1280]{3,2,1,0:T(8,128)(2,1)S(1)} async-done(((bf16[8,1,32,1280]{3,2,1,0:T(8,128)(2,1)}), bf16[8,1,32,1280]{3,2,1,0:T(8,128)(2,1)S(1)}, u32[]{:S(2)}, u32[]{:S(2)}) %all-to-all-start.2) | async-done | bytes 655392 | tf_op jit(solution)/shard_map/all_to_all | solution.py:689
  392.6 11.6 %collective-permute-done.49 = bf16[256,1280]{1,0:T(8,128)(2,1)S(1)} collective-permute-done((bf16[256,1280]{1,0:T(8,128)(2,1)}, bf16[256,1280]{1,0:T(8,128)(2,1)S(1)}, u32[]{:S(2)}, u32[]{:S(2)}) %collective-permute-start.49) | collective-permute-done | bytes 655392 | tf_op jit(solution)/shard_map/ppermute | solution.py:64
  405.9 4.8 %all-to-all-start.3 = ((bf16[8,1,32,1280]{3,2,1,0:T(8,128)(2,1)}), bf16[8,1,32,1280]{3,2,1,0:T(8,128)(2,1)S(1)}, u32[]{:S(2)}, u32[]{:S(2)}) async-start(bf16[8,1,32,1280]{3,2,1,0:T(8,128)(2,1)} %bitcast.84), calls=%async_computation.3 | async-start | bytes 1310720 | tf_op jit(solution)/shard_map/all_to_all | solution.py:689
  412.6 9.3 %all-to-all-done.3 = bf16[8,1,32,1280]{3,2,1,0:T(8,128)(2,1)S(1)} async-done(((bf16[8,1,32,1280]{3,2,1,0:T(8,128)(2,1)}), bf16[8,1,32,1280]{3,2,1,0:T(8,128)(2,1)S(1)}, u32[]{:S(2)}, u32[]{:S(2)}) %all-to-all-start.3) | async-done | bytes 655392 | tf_op jit(solution)/shard_map/all_to_all | solution.py:689
  421.9 3.1 add_convert_fusion
  (234 shorter events, 147.0 us)
Async XLA Ops:
  5.0 24.3 %collective-permute-start.2 = (bf16[512,5120]{1,0:T(8,128)(2,1)}, bf16[512,5120]{1,0:T(8,128)(2,1)}, u32[]{:S(2)}, u32[]{:S(2)}) collective-permute-start(bf16[512,5120]{1,0:T(8,128)(2,1)} %values_ref.1), channel_id=1, source_target_pairs={{0,4},{4,0},{8,12},{12,8},{16,20},{20,16},{24,28},{28,24},{1,5},{5... | collective-permute-start | bytes 15728648 | tf_op jit(solution)/shard_map/ppermute | solution.py:31
  9.8 24.0 %collective-permute-start.9 = (bf16[384,1280]{1,0:T(8,128)(2,1)}, bf16[384,1280]{1,0:T(8,128)(2,1)S(1)}, u32[]{:S(2)}, u32[]{:S(2)}) collective-permute-start(bf16[384,1280]{1,0:T(8,128)(2,1)} %get-tuple-element.227), channel_id=1, source_target_pairs={{0,1},{1,2},{2,3},{3,0},{4,5},{5,6},{6,7},{7,4},{8,9},{9,10},{10,1... | collective-permute-start | bytes 2949128 | tf_op jit(solution)/shard_map/ppermute | solution.py:49
  11.4 16.5 %collective-permute-start.3 = (bf16[1280,256]{1,0:T(8,128)(2,1)S(1)}, bf16[1280,256]{1,0:T(8,128)(2,1)S(1)}, u32[]{:S(2)}, u32[]{:S(2)}) collective-permute-start(bf16[1280,256]{1,0:T(8,128)(2,1)S(1)} %pad_maximum_fusion.1.refs_6_), channel_id=1, source_target_pairs={{0,8},{4,12},{8,0},{12,4},{16,24},{20,28},{24,16},{28,20},{1,9},{5... | collective-permute-start | bytes 1966088 | tf_op jit(solution)/shard_map/ppermute | solution.py:31
  13.0 16.3 %collective-permute-start.4 = (bf16[1280,256]{1,0:T(8,128)(2,1)S(1)}, bf16[1280,256]{1,0:T(8,128)(2,1)}, u32[]{:S(2)}, u32[]{:S(2)}) collective-permute-start(bf16[1280,256]{1,0:T(8,128)(2,1)S(1)} %pad_maximum_fusion.1.refs_6_), channel_id=1, source_target_pairs={{0,16},{4,20},{8,24},{12,28},{16,0},{20,4},{24,8},{28,12},{1,17},{... | collective-permute-start | bytes 1966088 | tf_op jit(solution)/shard_map/ppermute | solution.py:31
  29.3 29.8 %collective-permute-start.7 = (bf16[1280,384]{1,0:T(8,128)(2,1)S(1)}, bf16[1280,384]{1,0:T(8,128)(2,1)}, u32[]{:S(2)}, u32[]{:S(2)}) collective-permute-start(bf16[1280,384]{1,0:T(8,128)(2,1)S(1)} %pad_maximum_fusion.refs_6_), channel_id=1, source_target_pairs={{0,8},{4,12},{8,0},{12,4},{16,24},{20,28},{24,16},{28,20},{1,9},{5... | collective-permute-start | bytes 2949128 | tf_op jit(solution)/shard_map/ppermute | solution.py:31
  29.8 29.2 %collective-permute-start.8 = (bf16[1280,384]{1,0:T(8,128)(2,1)S(1)}, bf16[1280,384]{1,0:T(8,128)(2,1)}, u32[]{:S(2)}, u32[]{:S(2)}) collective-permute-start(bf16[1280,384]{1,0:T(8,128)(2,1)S(1)} %pad_maximum_fusion.refs_6_), channel_id=1, source_target_pairs={{0,16},{4,20},{8,24},{12,28},{16,0},{20,4},{24,8},{28,12},{1,17},{... | collective-permute-start | bytes 2949128 | tf_op jit(solution)/shard_map/ppermute | solution.py:31
  33.8 25.3 %collective-permute-start.10 = (bf16[384,1280]{1,0:T(8,128)(2,1)}, bf16[384,1280]{1,0:T(8,128)(2,1)}, u32[]{:S(2)}, u32[]{:S(2)}) collective-permute-start(bf16[384,1280]{1,0:T(8,128)(2,1)} %get-tuple-element.124), channel_id=1, source_target_pairs={{0,3},{1,0},{2,1},{3,2},{4,7},{5,4},{6,5},{7,6},{8,11},{9,8},{10,9... | collective-permute-start | bytes 2949128 | tf_op jit(solution)/shard_map/ppermute | solution.py:49
  36.9 21.8 %collective-permute-start.5 = (bf16[640,256]{1,0:T(8,128)(2,1)}, bf16[640,256]{1,0:T(8,128)(2,1)}, u32[]{:S(2)}, u32[]{:S(2)}) collective-permute-start(bf16[640,256]{1,0:T(8,128)(2,1)} %slice.54), channel_id=1, source_target_pairs={{0,8},{4,12},{8,0},{12,4},{16,24},{20,28},{24,16},{28,20},{1,9},{5... | collective-permute-start | bytes 983048 | tf_op jit(solution)/shard_map/ppermute | solution.py:31
  38.4 20.6 %collective-permute-start.6 = (bf16[640,256]{1,0:T(8,128)(2,1)}, bf16[640,256]{1,0:T(8,128)(2,1)}, u32[]{:S(2)}, u32[]{:S(2)}) collective-permute-start(bf16[640,256]{1,0:T(8,128)(2,1)} %slice.55), channel_id=1, source_target_pairs={{0,16},{4,20},{8,24},{12,28},{16,0},{20,4},{24,8},{28,12},{1,17},{... | collective-permute-start | bytes 983048 | tf_op jit(solution)/shard_map/ppermute | solution.py:31
  62.5 23.0 %collective-permute-start.11 = (bf16[1024,256]{1,0:T(8,128)(2,1)S(1)}, bf16[1024,256]{1,0:T(8,128)(2,1)S(1)}, u32[]{:S(2)}, u32[]{:S(2)}) collective-permute-start(bf16[1024,256]{1,0:T(8,128)(2,1)S(1)} %constant_dynamic-update-slice_fusion.refs_0_), channel_id=1, source_target_pairs={{0,8},{4,12},{8,0},{12,4},{16,24},{20,28},{24,16},{28,20},{1,9},{5... | collective-permute-start | bytes 1572872 | tf_op jit(solution)/shard_map/ppermute | solution.py:31
  64.0 21.5 %collective-permute-start.12 = (bf16[1024,256]{1,0:T(8,128)(2,1)S(1)}, bf16[1024,256]{1,0:T(8,128)(2,1)S(1)}, u32[]{:S(2)}, u32[]{:S(2)}) collective-permute-start(bf16[1024,256]{1,0:T(8,128)(2,1)S(1)} %constant_dynamic-update-slice_fusion.refs_0_), channel_id=1, source_target_pairs={{0,16},{4,20},{8,24},{12,28},{16,0},{20,4},{24,8},{28,12},{1,17},{... | collective-permute-start | bytes 1572872 | tf_op jit(solution)/shard_map/ppermute | solution.py:31
  66.6 17.9 %collective-permute-start.13 = (bf16[640,384]{1,0:T(8,128)(2,1)S(1)}, bf16[640,384]{1,0:T(8,128)(2,1)S(1)}, u32[]{:S(2)}, u32[]{:S(2)}) collective-permute-start(bf16[640,384]{1,0:T(8,128)(2,1)S(1)} %slice.56), channel_id=1, source_target_pairs={{0,8},{4,12},{8,0},{12,4},{16,24},{20,28},{24,16},{28,20},{1,9},{5... | collective-permute-start | bytes 1474568 | tf_op jit(solution)/shard_map/ppermute | solution.py:31
  68.4 17.2 %collective-permute-start.14 = (bf16[640,384]{1,0:T(8,128)(2,1)S(1)}, bf16[640,384]{1,0:T(8,128)(2,1)S(1)}, u32[]{:S(2)}, u32[]{:S(2)}) collective-permute-start(bf16[640,384]{1,0:T(8,128)(2,1)S(1)} %slice.57), channel_id=1, source_target_pairs={{0,16},{4,20},{8,24},{12,28},{16,0},{20,4},{24,8},{28,12},{1,17},{... | collective-permute-start | bytes 1474568 | tf_op jit(solution)/shard_map/ppermute | solution.py:31
  69.0 21.3 %collective-permute-start.17 = (bf16[192,1280]{1,0:T(8,128)(2,1)}, bf16[192,1280]{1,0:T(8,128)(2,1)S(1)}, u32[]{:S(2)}, u32[]{:S(2)}) collective-permute-start(bf16[192,1280]{1,0:T(8,128)(2,1)} %get-tuple-element.143), channel_id=1, source_target_pairs={{0,2},{1,3},{2,0},{3,1},{4,6},{5,7},{6,4},{7,5},{8,10},{9,11},{10,... | collective-permute-start | bytes 1474568 | tf_op jit(solution)/shard_map/ppermute | solution.py:49
  86.4 12.9 %collective-permute-start.15 = (bf16[512,256]{1,0:T(8,128)(2,1)}, bf16[512,256]{1,0:T(8,128)(2,1)}, u32[]{:S(2)}, u32[]{:S(2)}) collective-permute-start(bf16[512,256]{1,0:T(8,128)(2,1)} %slice.58), channel_id=1, source_target_pairs={{0,8},{4,12},{8,0},{12,4},{16,24},{20,28},{24,16},{28,20},{1,9},{5... | collective-permute-start | bytes 786440 | tf_op jit(solution)/shard_map/ppermute | solution.py:31
  90.3 23.3 %collective-permute-start.18 = (bf16[192,1280]{1,0:T(8,128)(2,1)}, bf16[192,1280]{1,0:T(8,128)(2,1)S(1)}, u32[]{:S(2)}, u32[]{:S(2)}) collective-permute-start(bf16[192,1280]{1,0:T(8,128)(2,1)} %get-tuple-element.144), channel_id=1, source_target_pairs={{0,2},{1,3},{2,0},{3,1},{4,6},{5,7},{6,4},{7,5},{8,10},{9,11},{10,... | collective-permute-start | bytes 1474568 | tf_op jit(solution)/shard_map/ppermute | solution.py:49
  102.8 19.9 %collective-permute-start.24 = (bf16[512,384]{1,0:T(8,128)(2,1)S(1)}, bf16[512,384]{1,0:T(8,128)(2,1)S(1)}, u32[]{:S(2)}, u32[]{:S(2)}) collective-permute-start(bf16[512,384]{1,0:T(8,128)(2,1)S(1)} %attend.3.refs_0_), channel_id=1, source_target_pairs={{0,1},{1,0},{2,3},{3,2},{4,5},{5,4},{6,7},{7,6},{8,9},{9,8},{10,11... | collective-permute-start | bytes 1179656 | tf_op jit(solution)/shard_map/ppermute | solution.py:64
  102.8 21.0 %collective-permute-start.25 = (bf16[512,384]{1,0:T(8,128)(2,1)S(1)}, bf16[512,384]{1,0:T(8,128)(2,1)S(1)}, u32[]{:S(2)}, u32[]{:S(2)}) collective-permute-start(bf16[512,384]{1,0:T(8,128)(2,1)S(1)} %attend.3.refs_0_), channel_id=1, source_target_pairs={{1,2},{2,1},{5,6},{6,5},{9,10},{10,9},{13,14},{14,13},{17,18},{18,... | collective-permute-start | bytes 1179656 | tf_op jit(solution)/shard_map/ppermute | solution.py:64
  113.6 17.5 %collective-permute-start.19 = (bf16[512,384]{1,0:T(8,128)(2,1)S(1)}, bf16[512,384]{1,0:T(8,128)(2,1)S(1)}, u32[]{:S(2)}, u32[]{:S(2)}) collective-permute-start(bf16[512,384]{1,0:T(8,128)(2,1)S(1)} %attend.2.refs_0_), channel_id=1, source_target_pairs={{0,1},{1,0},{2,3},{3,2},{4,5},{5,4},{6,7},{7,6},{8,9},{9,8},{10,11... | collective-permute-start | bytes 1179656 | tf_op jit(solution)/shard_map/ppermute | solution.py:64
  116.9 15.3 %collective-permute-start.20 = (bf16[512,384]{1,0:T(8,128)(2,1)S(1)}, bf16[512,384]{1,0:T(8,128)(2,1)S(1)}, u32[]{:S(2)}, u32[]{:S(2)}) collective-permute-start(bf16[512,384]{1,0:T(8,128)(2,1)S(1)} %attend.2.refs_0_), channel_id=1, source_target_pairs={{1,2},{2,1},{5,6},{6,5},{9,10},{10,9},{13,14},{14,13},{17,18},{18,... | collective-permute-start | bytes 1179656 | tf_op jit(solution)/shard_map/ppermute | solution.py:64
  123.8 15.7 %collective-permute-start.26 = (bf16[512,384]{1,0:T(8,128)(2,1)S(1)}, bf16[512,384]{1,0:T(8,128)(2,1)S(1)}, u32[]{:S(2)}, u32[]{:S(2)}) collective-permute-start(bf16[512,384]{1,0:T(8,128)(2,1)S(1)} %collective-permute-done.25.refs_2_), channel_id=1, source_target_pairs={{1,0},{2,3},{5,4},{6,7},{9,8},{10,11},{13,12},{14,15},{17,16},{18,... | collective-permute-start | bytes 1179656 | tf_op jit(solution)/shard_map/ppermute | solution.py:64
  127.8 12.9 %collective-permute-start.27 = (bf16[512,384]{1,0:T(8,128)(2,1)S(1)}, bf16[512,384]{1,0:T(8,128)(2,1)}, u32[]{:S(2)}, u32[]{:S(2)}) collective-permute-start(bf16[512,384]{1,0:T(8,128)(2,1)S(1)} %collective-permute-done.24.refs_1_), channel_id=1, source_target_pairs={{1,2},{2,1},{5,6},{6,5},{9,10},{10,9},{13,14},{14,13},{17,18},{18,... | collective-permute-start | bytes 1179656 | tf_op jit(solution)/shard_map/ppermute | solution.py:64
  132.2 15.7 %collective-permute-start.21 = (bf16[512,384]{1,0:T(8,128)(2,1)S(1)}, bf16[512,384]{1,0:T(8,128)(2,1)S(1)}, u32[]{:S(2)}, u32[]{:S(2)}) collective-permute-start(bf16[512,384]{1,0:T(8,128)(2,1)S(1)} %collective-permute-done.20.refs_2_), channel_id=1, source_target_pairs={{1,0},{2,3},{5,4},{6,7},{9,8},{10,11},{13,12},{14,15},{17,16},{18,... | collective-permute-start | bytes 1179656 | tf_op jit(solution)/shard_map/ppermute | solution.py:64
  136.2 12.9 %collective-permute-start.22 = (bf16[512,384]{1,0:T(8,128)(2,1)S(1)}, bf16[512,384]{1,0:T(8,128)(2,1)}, u32[]{:S(2)}, u32[]{:S(2)}) collective-permute-start(bf16[512,384]{1,0:T(8,128)(2,1)S(1)} %collective-permute-done.19.refs_1_), channel_id=1, source_target_pairs={{1,2},{2,1},{5,6},{6,5},{9,10},{10,9},{13,14},{14,13},{17,18},{18,... | collective-permute-start | bytes 1179656 | tf_op jit(solution)/shard_map/ppermute | solution.py:64
  140.7 15.7 %collective-permute-start.28 = (bf16[512,384]{1,0:T(8,128)(2,1)}, bf16[512,384]{1,0:T(8,128)(2,1)}, u32[]{:S(2)}, u32[]{:S(2)}) collective-permute-start(bf16[512,384]{1,0:T(8,128)(2,1)} %collective-permute-done.27.refs_4_), channel_id=1, source_target_pairs={{1,0},{2,3},{5,4},{6,7},{9,8},{10,11},{13,12},{14,15},{17,16},{18,... | collective-permute-start | bytes 1179656 | tf_op jit(solution)/shard_map/ppermute | solution.py:64
  149.2 15.7 %collective-permute-start.23 = (bf16[512,384]{1,0:T(8,128)(2,1)}, bf16[512,384]{1,0:T(8,128)(2,1)}, u32[]{:S(2)}, u32[]{:S(2)}) collective-permute-start(bf16[512,384]{1,0:T(8,128)(2,1)} %collective-permute-done.22.refs_4_), channel_id=1, source_target_pairs={{1,0},{2,3},{5,4},{6,7},{9,8},{10,11},{13,12},{14,15},{17,16},{18,... | collective-permute-start | bytes 1179656 | tf_op jit(solution)/shard_map/ppermute | solution.py:64
  188.5 15.9 %all-to-all-start = ((bf16[8,1,32,1280]{3,2,1,0:T(8,128)(2,1)}), bf16[8,1,32,1280]{3,2,1,0:T(8,128)(2,1)S(1)}, u32[]{:S(2)}, u32[]{:S(2)}) async-start(bf16[8,1,32,1280]{3,2,1,0:T(8,128)(2,1)} %bitcast.21), calls=%async_computation | async-start | bytes 1310720 | tf_op jit(solution)/shard_map/all_to_all | solution.py:702
  204.4 14.4 %collective-permute-start.30 = (bf16[256,1280]{1,0:T(8,128)(2,1)S(1)}, bf16[256,1280]{1,0:T(8,128)(2,1)S(1)}, u32[]{:S(2)}, u32[]{:S(2)}) collective-permute-start(bf16[256,1280]{1,0:T(8,128)(2,1)S(1)} %bitcast.80), channel_id=1, source_target_pairs={{0,1},{1,0},{2,3},{3,2},{4,5},{5,4},{6,7},{7,6},{8,9},{9,8},{10,11... | collective-permute-start | bytes 1966088 | tf_op jit(solution)/shard_map/ppermute | solution.py:64
  206.9 15.3 %collective-permute-start.31 = (bf16[256,1280]{1,0:T(8,128)(2,1)S(1)}, bf16[256,1280]{1,0:T(8,128)(2,1)S(1)}, u32[]{:S(2)}, u32[]{:S(2)}) collective-permute-start(bf16[256,1280]{1,0:T(8,128)(2,1)S(1)} %bitcast.81), channel_id=1, source_target_pairs={{1,2},{2,1},{5,6},{6,5},{9,10},{10,9},{13,14},{14,13},{17,18},{18,... | collective-permute-start | bytes 1966088 | tf_op jit(solution)/shard_map/ppermute | solution.py:64
  224.3 14.5 %collective-permute-start.33 = (bf16[256,1280]{1,0:T(8,128)(2,1)S(1)}, bf16[256,1280]{1,0:T(8,128)(2,1)}, u32[]{:S(2)}, u32[]{:S(2)}) collective-permute-start(bf16[256,1280]{1,0:T(8,128)(2,1)S(1)} %collective-permute-done.30.refs_0_), channel_id=1, source_target_pairs={{1,2},{2,1},{5,6},{6,5},{9,10},{10,9},{13,14},{14,13},{17,18},{18,... | collective-permute-start | bytes 1966088 | tf_op jit(solution)/shard_map/ppermute | solution.py:64
  228.1 16.0 %all-to-all-start.1 = ((bf16[8,1,32,1280]{3,2,1,0:T(8,128)(2,1)}), bf16[8,1,32,1280]{3,2,1,0:T(8,128)(2,1)S(1)}, u32[]{:S(2)}, u32[]{:S(2)}) async-start(bf16[8,1,32,1280]{3,2,1,0:T(8,128)(2,1)} %bitcast.86), calls=%async_computation.1 | async-start | bytes 1310720 | tf_op jit(solution)/shard_map/all_to_all | solution.py:702
  244.1 22.1 %collective-permute-start.34 = (bf16[256,1280]{1,0:T(8,128)(2,1)}, bf16[256,1280]{1,0:T(8,128)(2,1)}, u32[]{:S(2)}, u32[]{:S(2)}) collective-permute-start(bf16[256,1280]{1,0:T(8,128)(2,1)} %collective-permute-done.33.refs_0_), channel_id=1, source_target_pairs={{1,0},{2,3},{5,4},{6,7},{9,8},{10,11},{13,12},{14,15},{17,16},{18,... | collective-permute-start | bytes 1966088 | tf_op jit(solution)/shard_map/ppermute | solution.py:64
  266.2 19.7 %collective-permute-start.38 = (bf16[256,1280]{1,0:T(8,128)(2,1)S(1)}, bf16[256,1280]{1,0:T(8,128)(2,1)S(1)}, u32[]{:S(2)}, u32[]{:S(2)}) collective-permute-start(bf16[256,1280]{1,0:T(8,128)(2,1)S(1)} %bitcast.78), channel_id=1, source_target_pairs={{0,1},{1,0},{2,3},{3,2},{4,5},{5,4},{6,7},{7,6},{8,9},{9,8},{10,11... | collective-permute-start | bytes 1966088 | tf_op jit(solution)/shard_map/ppermute | solution.py:64
  266.3 19.6 %collective-permute-start.39 = (bf16[256,1280]{1,0:T(8,128)(2,1)S(1)}, bf16[256,1280]{1,0:T(8,128)(2,1)S(1)}, u32[]{:S(2)}, u32[]{:S(2)}) collective-permute-start(bf16[256,1280]{1,0:T(8,128)(2,1)S(1)} %bitcast.79), channel_id=1, source_target_pairs={{1,2},{2,1},{5,6},{6,5},{9,10},{10,9},{13,14},{14,13},{17,18},{18,... | collective-permute-start | bytes 1966088 | tf_op jit(solution)/shard_map/ppermute | solution.py:64
  284.6 15.3 %collective-permute-start.35 = (bf16[256,1280]{1,0:T(8,128)(2,1)S(1)}, bf16[256,1280]{1,0:T(8,128)(2,1)S(1)}, u32[]{:S(2)}, u32[]{:S(2)}) collective-permute-start(bf16[256,1280]{1,0:T(8,128)(2,1)S(1)} %get-tuple-element.231), channel_id=1, source_target_pairs={{0,1},{3,2},{4,5},{7,6},{8,9},{11,10},{12,13},{15,14},{16,17},{19,... | collective-permute-start | bytes 1966088 | tf_op jit(solution)/shard_map/ppermute | solution.py:64
  291.6 15.2 %collective-permute-start.40 = (bf16[256,1280]{1,0:T(8,128)(2,1)S(1)}, bf16[256,1280]{1,0:T(8,128)(2,1)S(1)}, u32[]{:S(2)}, u32[]{:S(2)}) collective-permute-start(bf16[256,1280]{1,0:T(8,128)(2,1)S(1)} %collective-permute-done.39.refs_1_), channel_id=1, source_target_pairs={{1,0},{2,3},{5,4},{6,7},{9,8},{10,11},{13,12},{14,15},{17,16},{18,... | collective-permute-start | bytes 1966088 | tf_op jit(solution)/shard_map/ppermute | solution.py:64
  296.2 19.6 %collective-permute-start.41 = (bf16[256,1280]{1,0:T(8,128)(2,1)S(1)}, bf16[256,1280]{1,0:T(8,128)(2,1)S(1)}, u32[]{:S(2)}, u32[]{:S(2)}) collective-permute-start(bf16[256,1280]{1,0:T(8,128)(2,1)S(1)} %collective-permute-done.38.refs_0_), channel_id=1, source_target_pairs={{1,2},{2,1},{5,6},{6,5},{9,10},{10,9},{13,14},{14,13},{17,18},{18,... | collective-permute-start | bytes 1966088 | tf_op jit(solution)/shard_map/ppermute | solution.py:64
  300.1 24.9 %collective-permute-start.36 = (bf16[256,1280]{1,0:T(8,128)(2,1)S(1)}, bf16[256,1280]{1,0:T(8,128)(2,1)S(1)}, u32[]{:S(2)}, u32[]{:S(2)}) collective-permute-start(bf16[256,1280]{1,0:T(8,128)(2,1)S(1)} %add_convert_fusion.4), channel_id=1, source_target_pairs={{1,2},{2,1},{5,6},{6,5},{9,10},{10,9},{13,14},{14,13},{17,18},{18,... | collective-permute-start | bytes 1966088 | tf_op jit(solution)/shard_map/ppermute | solution.py:64
  302.5 22.7 %collective-permute-start.37 = (bf16[256,1280]{1,0:T(8,128)(2,1)S(1)}, bf16[256,1280]{1,0:T(8,128)(2,1)S(1)}, u32[]{:S(2)}, u32[]{:S(2)}) collective-permute-start(bf16[256,1280]{1,0:T(8,128)(2,1)S(1)} %get-tuple-element.197), channel_id=1, source_target_pairs={{0,1},{3,2},{4,5},{7,6},{8,9},{11,10},{12,13},{15,14},{16,17},{19,... | collective-permute-start | bytes 1966088 | tf_op jit(solution)/shard_map/ppermute | solution.py:64
  315.8 17.8 %collective-permute-start.44 = (bf16[256,1280]{1,0:T(8,128)(2,1)S(1)}, bf16[256,1280]{1,0:T(8,128)(2,1)S(1)}, u32[]{:S(2)}, u32[]{:S(2)}) collective-permute-start(bf16[256,1280]{1,0:T(8,128)(2,1)S(1)} %collective-permute-done.41.refs_0_), channel_id=1, source_target_pairs={{1,0},{2,3},{5,4},{6,7},{9,8},{10,11},{13,12},{14,15},{17,16},{18,... | collective-permute-start | bytes 1966088 | tf_op jit(solution)/shard_map/ppermute | solution.py:64
  331.0 15.5 %collective-permute-start.43 = (bf16[256,1280]{1,0:T(8,128)(2,1)S(1)}, bf16[256,1280]{1,0:T(8,128)(2,1)S(1)}, u32[]{:S(2)}, u32[]{:S(2)}) collective-permute-start(bf16[256,1280]{1,0:T(8,128)(2,1)S(1)} %add_convert_fusion.3), channel_id=1, source_target_pairs={{1,2},{2,1},{5,6},{6,5},{9,10},{10,9},{13,14},{14,13},{17,18},{18,... | collective-permute-start | bytes 1966088 | tf_op jit(solution)/shard_map/ppermute | solution.py:64
  333.5 13.0 %collective-permute-start.42 = (bf16[256,1280]{1,0:T(8,128)(2,1)S(1)}, bf16[256,1280]{1,0:T(8,128)(2,1)S(1)}, u32[]{:S(2)}, u32[]{:S(2)}) collective-permute-start(bf16[256,1280]{1,0:T(8,128)(2,1)S(1)} %fusion.3), channel_id=1, source_target_pairs={{0,1},{1,0},{2,3},{3,2},{4,5},{5,4},{6,7},{7,6},{8,9},{9,8},{10,11... | collective-permute-start | bytes 1966088 | tf_op jit(solution)/shard_map/ppermute | solution.py:64
  350.3 13.5 %collective-permute-start.45 = (bf16[256,1280]{1,0:T(8,128)(2,1)S(1)}, bf16[256,1280]{1,0:T(8,128)(2,1)S(1)}, u32[]{:S(2)}, u32[]{:S(2)}) collective-permute-start(bf16[256,1280]{1,0:T(8,128)(2,1)S(1)} %get-tuple-element.230), channel_id=1, source_target_pairs={{0,1},{3,2},{4,5},{7,6},{8,9},{11,10},{12,13},{15,14},{16,17},{19,... | collective-permute-start | bytes 1966088 | tf_op jit(solution)/shard_map/ppermute | solution.py:64
  364.8 12.9 %collective-permute-start.46 = (bf16[256,1280]{1,0:T(8,128)(2,1)}, bf16[256,1280]{1,0:T(8,128)(2,1)}, u32[]{:S(2)}, u32[]{:S(2)}) collective-permute-start(bf16[256,1280]{1,0:T(8,128)(2,1)} %add_convert_fusion.2), channel_id=1, source_target_pairs={{1,2},{2,1},{5,6},{6,5},{9,10},{10,9},{13,14},{14,13},{17,18},{18,... | collective-permute-start | bytes 1966088 | tf_op jit(solution)/shard_map/ppermute | solution.py:64
  369.5 18.9 %all-to-all-start.2 = ((bf16[8,1,32,1280]{3,2,1,0:T(8,128)(2,1)}), bf16[8,1,32,1280]{3,2,1,0:T(8,128)(2,1)S(1)}, u32[]{:S(2)}, u32[]{:S(2)}) async-start(bf16[8,1,32,1280]{3,2,1,0:T(8,128)(2,1)} %bitcast.35), calls=%async_computation.2 | async-start | bytes 1310720 | tf_op jit(solution)/shard_map/all_to_all | solution.py:689
  388.4 15.8 %collective-permute-start.49 = (bf16[256,1280]{1,0:T(8,128)(2,1)}, bf16[256,1280]{1,0:T(8,128)(2,1)S(1)}, u32[]{:S(2)}, u32[]{:S(2)}) collective-permute-start(bf16[256,1280]{1,0:T(8,128)(2,1)} %add_convert_fusion.1), channel_id=1, source_target_pairs={{1,2},{2,1},{5,6},{6,5},{9,10},{10,9},{13,14},{14,13},{17,18},{18,... | collective-permute-start | bytes 1966088 | tf_op jit(solution)/shard_map/ppermute | solution.py:64
  390.8 14.0 %collective-permute-start.48 = (bf16[256,1280]{1,0:T(8,128)(2,1)}, bf16[256,1280]{1,0:T(8,128)(2,1)S(1)}, u32[]{:S(2)}, u32[]{:S(2)}) collective-permute-start(bf16[256,1280]{1,0:T(8,128)(2,1)} %fusion), channel_id=1, source_target_pairs={{0,1},{1,0},{2,3},{3,2},{4,5},{5,4},{6,7},{7,6},{8,9},{9,8},{10,11... | collective-permute-start | bytes 1966088 | tf_op jit(solution)/shard_map/ppermute | solution.py:64
  405.9 16.0 %all-to-all-start.3 = ((bf16[8,1,32,1280]{3,2,1,0:T(8,128)(2,1)}), bf16[8,1,32,1280]{3,2,1,0:T(8,128)(2,1)S(1)}, u32[]{:S(2)}, u32[]{:S(2)}) async-start(bf16[8,1,32,1280]{3,2,1,0:T(8,128)(2,1)} %bitcast.84), calls=%async_computation.3 | async-start | bytes 1310720 | tf_op jit(solution)/shard_map/all_to_all | solution.py:689
  (56 other events, 504.3 us)
